TPU v7x, 32 devices: a whole 2x2x4 slice. The times are simulated.
32 devices in a mesh: context: 8 (over z, x), mp: 4 (over y, core).
Axes of the slice: x: 2, y: 2, z: 4, core: 2. Of those that a mesh axis runs over, the one named last changes fastest.
Arguments:
- queries: bfloat16 [8192, 2048], P('context', 'mp'), may hold values from -32 to 32
- keys: bfloat16 [8192, 1024], P('context', 'mp'), may hold values from -32 to 32
- values: bfloat16 [8192, 1024], P('context', 'mp'), may hold values from -6 to 6
- out_grad: bfloat16 [8192, 5376], P(('context', 'mp')), may hold values from -6 to 6
- out_weight: bfloat16 [5376, 2048], P(None, 'mp'), may hold values from -0.125 to 0.125
Outputs:
- query_grad: bfloat16 [8192, 2048], P('context', 'mp')
- key_grad: bfloat16 [8192, 1024], P('context', 'mp')
- value_grad: bfloat16 [8192, 1024], P('context', 'mp')
- weight_grad: bfloat16 [5376, 2048], P('context', 'mp')
All inputs are finite; a program needn't handle non-finite values.
Results may differ from a plain program's by a relative error of at most 0.02.
Values may be sent and summed in bfloat16 or wider, within the bound.
No kernel may reach another device: no remote copies, remote signals or barrier semaphores. Data moves between devices by JAX's collectives and lax.ppermute only.
A program may use at most 128 MiB of HBM per device.

v0:
```python
import jax
import jax.numpy as jnp
from jax import lax
from jax.sharding import PartitionSpec as P

HEAD_SIZE = 128
WINDOW_KEYS = 512


SCALE = 168.0 ** (-0.5)
NEG = -1e30


def shifted(x, axis, by):
    devices = lax.axis_size(axis)
    pairs = [(i, i + by) for i in range(devices) if 0 <= i + by < devices]
    return lax.ppermute(x, axis, pairs)


def band_grads(query_rows_block, key_rows_block, value_rows_block, output_grad_rows, key_start):
    rows = query_rows_block.shape[0]
    span = key_rows_block.shape[0]
    scores = (
        jnp.einsum(
            "qhgd,khd->hgqk", query_rows_block, key_rows_block, preferred_element_type=jnp.float32
        )
        * SCALE
    )
    qpos = jnp.arange(rows, dtype=jnp.int32)[:, None]
    kpos = jnp.arange(span, dtype=jnp.int32)[None, :]
    allowed = (kpos > qpos) & (kpos <= qpos + (span - rows)) & (kpos + key_start >= 0)
    scores = jnp.where(allowed, scores, NEG)
    top = jnp.max(scores, axis=-1, keepdims=True)
    weights = jnp.exp(scores - top)
    prob = weights / jnp.sum(weights, axis=-1, keepdims=True)
    prob_b = prob.astype(jnp.bfloat16)
    attn = jnp.einsum(
        "hgqk,khd->qhgd", prob_b, value_rows_block, preferred_element_type=jnp.float32
    ).astype(jnp.bfloat16)
    delta = jnp.sum(output_grad_rows.astype(jnp.float32) * attn.astype(jnp.float32), axis=-1)
    delta = jnp.transpose(delta, (1, 2, 0))[..., None]
    dprob = jnp.einsum(
        "qhgd,khd->hgqk", output_grad_rows, value_rows_block, preferred_element_type=jnp.float32
    )
    dscore = (prob * (dprob - delta) * SCALE).astype(jnp.bfloat16)
    dq = jnp.einsum("hgqk,khd->qhgd", dscore, key_rows_block, preferred_element_type=jnp.float32)
    key_gradient = jnp.einsum(
        "hgqk,qhgd->khd", dscore, query_rows_block, preferred_element_type=jnp.float32
    )
    value_gradient = jnp.einsum(
        "hgqk,qhgd->khd", prob_b, output_grad_rows, preferred_element_type=jnp.float32
    )
    return (dq, attn, key_gradient, value_gradient)


def shards(queries, keys, values, out_grad, out_weight):
    shard = queries.shape[0]
    kv_local = keys.shape[1] // HEAD_SIZE
    q_local = queries.shape[1] // HEAD_SIZE
    query_group = q_local // kv_local
    block_index = WINDOW_KEYS // 2
    root = lax.axis_index("context") * shard - WINDOW_KEYS
    prev_keys, prev_values = shifted((keys, values), "context", 1)
    prev_keys = prev_keys[shard - WINDOW_KEYS :]
    prev_values = prev_values[shard - WINDOW_KEYS :]
    key_buf = jnp.concatenate([prev_keys, keys], 0)
    value_buf = jnp.concatenate([prev_values, values], 0)
    grad_full = lax.all_gather(out_grad, "mp", axis=0, tiled=True)
    output_gradient = jnp.dot(grad_full, out_weight, preferred_element_type=jnp.float32).astype(
        jnp.bfloat16
    )

    def step(index, carry):
        dq_all, attn_all, key_gradient_total, value_gradient_total = carry
        start_position = index * block_index
        query_rows_block = lax.dynamic_slice_in_dim(
            queries, start_position, block_index, 0
        ).reshape(block_index, kv_local, query_group, HEAD_SIZE)
        output_grad_rows = lax.dynamic_slice_in_dim(
            output_gradient, start_position, block_index, 0
        ).reshape(block_index, kv_local, query_group, HEAD_SIZE)
        key_rows_block = lax.dynamic_slice_in_dim(
            key_buf, start_position, WINDOW_KEYS + block_index, 0
        ).reshape(WINDOW_KEYS + block_index, kv_local, HEAD_SIZE)
        value_rows_block = lax.dynamic_slice_in_dim(
            value_buf, start_position, WINDOW_KEYS + block_index, 0
        ).reshape(WINDOW_KEYS + block_index, kv_local, HEAD_SIZE)
        dq, attn, key_gradient, value_gradient = band_grads(
            query_rows_block,
            key_rows_block,
            value_rows_block,
            output_grad_rows,
            root + start_position,
        )
        dq_all = lax.dynamic_update_slice_in_dim(
            dq_all, dq.reshape(block_index, q_local * HEAD_SIZE), start_position, 0
        )
        attn_all = lax.dynamic_update_slice_in_dim(
            attn_all, attn.reshape(block_index, q_local * HEAD_SIZE), start_position, 0
        )
        earlier_keys = lax.dynamic_slice_in_dim(
            key_gradient_total, start_position, WINDOW_KEYS + block_index, 0
        )
        earlier_values = lax.dynamic_slice_in_dim(
            value_gradient_total, start_position, WINDOW_KEYS + block_index, 0
        )
        key_gradient_total = lax.dynamic_update_slice_in_dim(
            key_gradient_total,
            earlier_keys + key_gradient.reshape(WINDOW_KEYS + block_index, kv_local * HEAD_SIZE),
            start_position,
            0,
        )
        value_gradient_total = lax.dynamic_update_slice_in_dim(
            value_gradient_total,
            earlier_values
            + value_gradient.reshape(WINDOW_KEYS + block_index, kv_local * HEAD_SIZE),
            start_position,
            0,
        )
        return (dq_all, attn_all, key_gradient_total, value_gradient_total)

    start_state = (
        jnp.zeros((shard, q_local * HEAD_SIZE), jnp.float32),
        jnp.zeros((shard, q_local * HEAD_SIZE), jnp.bfloat16),
        jnp.zeros((WINDOW_KEYS + shard, kv_local * HEAD_SIZE), jnp.float32),
        jnp.zeros((WINDOW_KEYS + shard, kv_local * HEAD_SIZE), jnp.float32),
    )
    dq_all, attn_all, key_gradient_total, value_gradient_total = lax.fori_loop(
        0, shard // block_index, step, start_state
    )
    back_keys, back_values = (
        shifted(key_gradient_total[:WINDOW_KEYS].astype(jnp.bfloat16), "context", -1).astype(
            jnp.float32
        ),
        shifted(value_gradient_total[:WINDOW_KEYS].astype(jnp.bfloat16), "context", -1).astype(
            jnp.float32
        ),
    )
    own_keys = key_gradient_total[WINDOW_KEYS:]
    own_values = value_gradient_total[WINDOW_KEYS:]
    key_grad = jnp.concatenate(
        [own_keys[: shard - WINDOW_KEYS], own_keys[shard - WINDOW_KEYS :] + back_keys], 0
    ).astype(jnp.bfloat16)
    value_grad = jnp.concatenate(
        [own_values[: shard - WINDOW_KEYS], own_values[shard - WINDOW_KEYS :] + back_values], 0
    ).astype(jnp.bfloat16)
    query_grad = dq_all.astype(jnp.bfloat16)
    weight_grad = lax.psum_scatter(
        lax.dot_general(
            grad_full, attn_all, (((0,), (0,)), ((), ())), preferred_element_type=jnp.float32
        ),
        "context",
        scatter_dimension=0,
        tiled=True,
    ).astype(jnp.bfloat16)
    return (query_grad, key_grad, value_grad, weight_grad)


def solution(mesh):
    return jax.shard_map(
        shards,
        mesh=mesh,
        in_specs=(
            P("context", "mp"),
            P("context", "mp"),
            P("context", "mp"),
            P(("context", "mp"), None),
            P(None, "mp"),
        ),
        out_specs=(P("context", "mp"), P("context", "mp"), P("context", "mp"), P("context", "mp")),
        check_vma=False,
    )
```

profile of v0, /device:TPU:0, one launch (start us, length us, event | category | flops | bytes accessed | tf_op | source)
XLA Modules:
  0.0 454.1 jit_solution(16094105019892783782)
XLA Ops:
  8.4 4.9 %collective-permute-start = (bf16[1024,256]{0,1:T(8,128)(2,1)S(1)}, bf16[1024,256]{0,1:T(8,128)(2,1)S(1)}, u32[]{:S(2)}, u32[]{:S(2)}) collective-permute-start(bf16[1024,256]{0,1:T(8,128)(2,1)S(1)} %copy.52), channel_id=1, source_target_pairs={{0,4},{4,8},{8,12},{12,16},{16,20},{20,24},{24,28},{1,5},{5,9},{9,... | collective-permute-start | bytes 1572872 | tf_op jit(solution)/shard_map/ppermute | solution.py:17
  13.5 3.5 collective-permute-start.1
  17.0 8.6 %collective-permute-done = bf16[1024,256]{0,1:T(8,128)(2,1)S(1)} collective-permute-done((bf16[1024,256]{0,1:T(8,128)(2,1)S(1)}, bf16[1024,256]{0,1:T(8,128)(2,1)S(1)}, u32[]{:S(2)}, u32[]{:S(2)}) %collective-permute-start) | collective-permute-done | bytes 524320 | tf_op jit(solution)/shard_map/ppermute | solution.py:17
  25.6 10.1 %collective-permute-done.1 = bf16[1024,256]{0,1:T(8,128)(2,1)S(1)} collective-permute-done((bf16[1024,256]{0,1:T(8,128)(2,1)S(1)}, bf16[1024,256]{0,1:T(8,128)(2,1)S(1)}, u32[]{:S(2)}, u32[]{:S(2)}) %collective-permute-start.1) | collective-permute-done | bytes 524320 | tf_op jit(solution)/shard_map/ppermute | solution.py:17
  36.7 48.8 %all-gather.2.cloned.1.call-done = bf16[1024,5376]{1,0:T(8,128)(2,1)} async-done(((bf16[256,5376]{1,0:T(8,128)(2,1)}), bf16[1024,5376]{1,0:T(8,128)(2,1)}) %all-gather.2.cloned.1.call-update) | async-done | bytes 11010064 | tf_op jit(solution)/shard_map/all_gather | solution.py:68
  85.5 11.0 %convolution_convert_fusion.1 = bf16[1024,512]{1,0:T(8,128)(2,1)} fusion(bf16[1024,5376]{1,0:T(8,128)(2,1)} %all-gather.2.cloned.1.call-done, bf16[5376,512]{1,0:T(8,128)(2,1)} %param.11), kind=kOutput, calls=%fused_computation.37 | convolution fusion | flops 5637668864 | bytes 17563648 | tf_op jit(solution)/shard_map/dot_general | solution.py:69
  101.3 125.8 %while.19 = (s32[]{:T(128)}, bf16[1024,512]{1,0:T(8,128)(2,1)}, bf16[1024,512]{0,1:T(8,128)(2,1)}, f32[1536,256]{1,0:T(8,128)}, f32[1536,256]{1,0:T(8,128)}, /*i...) while((s32[]{:T(128)}, bf16[1024,512]{1,0:T(8,128)(2,1)}, ...), condition=%wide.region_4.5_spmd, body=%wide.region_0.4_spmd.sunk | while | flops 1218446848 | bytes 76701752 | solution.py:128
  104.1 3.0 fusion.71
  111.7 2.7 fusion.73
  117.0 2.4 copy.104
  119.3 2.4 bitcast_add_fusion.5
  128.2 2.4 constant_dynamic-update-slice_fusion.9
  135.5 3.0 fusion.71
  143.2 2.7 fusion.73
  148.4 2.4 copy.104
  150.8 2.4 bitcast_add_fusion.5
  159.7 2.5 constant_dynamic-update-slice_fusion.9
  167.0 3.0 fusion.71
  174.6 2.7 fusion.73
  179.9 2.4 copy.104
  182.2 2.4 bitcast_add_fusion.5
  191.1 2.5 constant_dynamic-update-slice_fusion.9
  198.5 3.0 fusion.71
  206.1 2.7 fusion.73
  211.3 2.4 copy.104
  213.7 2.4 bitcast_add_fusion.5
  222.6 2.5 constant_dynamic-update-slice_fusion.9
  227.1 12.7 %convolution_bitcast_fusion = f32[5376,512]{0,1:T(8,128)} fusion(bf16[1024,512]{0,1:T(8,128)(2,1)} %get-tuple-element.179, bf16[1024,5376]{1,0:T(8,128)(2,1)} %all-gather.2.cloned.1.call-done), kind=kOutput, calls=%fused_computation.36 | convolution fusion | flops 5637144576 | bytes 23068672 | tf_op jit(solution)/shard_map/dot_general | solution.py:149
  239.8 12.1 %copy.80 = f32[5376,512]{1,0:T(8,128)} copy(f32[5376,512]{0,1:T(8,128)} %convolution_bitcast_fusion) | data formatting | bytes 22020096
  256.3 11.5 %collective-permute-done.3 = bf16[512,256]{1,0:T(8,128)(2,1)S(1)} collective-permute-done((bf16[512,256]{1,0:T(8,128)(2,1)S(1)}, bf16[512,256]{1,0:T(8,128)(2,1)S(1)}, u32[]{:S(2)}, u32[]{:S(2)}) %collective-permute-start.3) | collective-permute-done | bytes 262176 | tf_op jit(solution)/shard_map/ppermute | solution.py:17
  268.8 9.7 %collective-permute-done.2 = bf16[512,256]{1,0:T(8,128)(2,1)S(1)} collective-permute-done((bf16[512,256]{1,0:T(8,128)(2,1)S(1)}, bf16[512,256]{1,0:T(8,128)(2,1)S(1)}, u32[]{:S(2)}, u32[]{:S(2)}) %collective-permute-start.2) | collective-permute-done | bytes 262176 | tf_op jit(solution)/shard_map/ppermute | solution.py:17
  279.3 165.2 %reduce-scatter.4.cloned.1.call-done = f32[672,512]{1,0:T(8,128)} async-done(((f32[5376,512]{1,0:T(8,128)}), f32[672,512]{1,0:T(8,128)}) %reduce-scatter.4.cloned.1.call-update) | async-done | bytes 1376272
  (214 shorter events, 89.1 us)
Async XLA Ops:
  7.2 6.1 %copy-start.14 = (bf16[1024,256]{1,0:T(8,128)(2,1)S(1)}, bf16[1024,256]{1,0:T(8,128)(2,1)}, u32[]{:S(2)}) copy-start(bf16[1024,256]{1,0:T(8,128)(2,1)} %param.9) | copy-start | bytes 1572868
  7.2 78.3 %all-gather.2.cloned.1.call-start = ((), (), s32[]{:S(2)}) async-start(), calls=%async_computation.1 | async-start | bytes 13762560 | tf_op jit(solution)/shard_map/all_gather | solution.py:68
  7.9 436.6 %reduce-scatter.4.cloned.1.call-start = ((), (), s32[]{:S(2)}) async-start(), calls=%async_computation.2 | async-start | bytes 12386304
  8.4 17.2 %collective-permute-start = (bf16[1024,256]{0,1:T(8,128)(2,1)S(1)}, bf16[1024,256]{0,1:T(8,128)(2,1)S(1)}, u32[]{:S(2)}, u32[]{:S(2)}) collective-permute-start(bf16[1024,256]{0,1:T(8,128)(2,1)S(1)} %copy.52), channel_id=1, source_target_pairs={{0,4},{4,8},{8,12},{12,16},{16,20},{20,24},{24,28},{1,5},{5,9},{9,... | collective-permute-start | bytes 1572872 | tf_op jit(solution)/shard_map/ppermute | solution.py:17
  13.5 22.1 %collective-permute-start.1 = (bf16[1024,256]{0,1:T(8,128)(2,1)S(1)}, bf16[1024,256]{0,1:T(8,128)(2,1)S(1)}, u32[]{:S(2)}, u32[]{:S(2)}) collective-permute-start(bf16[1024,256]{0,1:T(8,128)(2,1)S(1)} %copy.54), channel_id=1, source_target_pairs={{0,4},{4,8},{8,12},{12,16},{16,20},{20,24},{24,28},{1,5},{5,9},{9,... | collective-permute-start | bytes 1572872 | tf_op jit(solution)/shard_map/ppermute | solution.py:17
  101.3 8.0 %copy-start.11 = (bf16[1536,256]{0,1:T(8,128)(2,1)}, bf16[1536,256]{0,1:T(8,128)(2,1)S(1)}, u32[]{:S(2)}) copy-start(bf16[1536,256]{0,1:T(8,128)(2,1)S(1)} %get-tuple-element.353) | copy-start | bytes 2359300 | tf_op jit(solution)/shard_map/while
  102.6 4.6 %copy-start.2 = (bf16[768,256]{0,1:T(8,128)(2,1)}, bf16[768,256]{0,1:T(8,128)(2,1)S(1)}, u32[]{:S(2)}) copy-start(bf16[768,256]{0,1:T(8,128)(2,1)S(1)} %constant_dynamic-slice_fusion.12) | copy-start | bytes 1179652 | tf_op jit(solution)/shard_map/while
  103.8 3.3 copy-start.9
  109.4 2.4 copy-start.1
  111.7 2.7 copy-start.10
  128.2 2.4 copy-start.3
  132.7 8.0 %copy-start.11 = (bf16[1536,256]{0,1:T(8,128)(2,1)}, bf16[1536,256]{0,1:T(8,128)(2,1)S(1)}, u32[]{:S(2)}) copy-start(bf16[1536,256]{0,1:T(8,128)(2,1)S(1)} %get-tuple-element.353) | copy-start | bytes 2359300 | tf_op jit(solution)/shard_map/while
  134.0 4.6 %copy-start.2 = (bf16[768,256]{0,1:T(8,128)(2,1)}, bf16[768,256]{0,1:T(8,128)(2,1)S(1)}, u32[]{:S(2)}) copy-start(bf16[768,256]{0,1:T(8,128)(2,1)S(1)} %constant_dynamic-slice_fusion.12) | copy-start | bytes 1179652 | tf_op jit(solution)/shard_map/while
  135.3 3.3 copy-start.9
  140.8 2.4 copy-start.1
  143.2 2.7 copy-start.10
  159.7 2.5 copy-start.3
  162.5 1.7 copy-start.12
  164.2 8.0 %copy-start.11 = (bf16[1536,256]{0,1:T(8,128)(2,1)}, bf16[1536,256]{0,1:T(8,128)(2,1)S(1)}, u32[]{:S(2)}) copy-start(bf16[1536,256]{0,1:T(8,128)(2,1)S(1)} %get-tuple-element.353) | copy-start | bytes 2359300 | tf_op jit(solution)/shard_map/while
  165.5 4.6 %copy-start.2 = (bf16[768,256]{0,1:T(8,128)(2,1)}, bf16[768,256]{0,1:T(8,128)(2,1)S(1)}, u32[]{:S(2)}) copy-start(bf16[768,256]{0,1:T(8,128)(2,1)S(1)} %constant_dynamic-slice_fusion.12) | copy-start | bytes 1179652 | tf_op jit(solution)/shard_map/while
  166.7 3.3 copy-start.9
  172.3 2.4 copy-start.1
  174.6 2.7 copy-start.10
  191.1 2.5 copy-start.3
  195.6 8.0 %copy-start.11 = (bf16[1536,256]{0,1:T(8,128)(2,1)}, bf16[1536,256]{0,1:T(8,128)(2,1)S(1)}, u32[]{:S(2)}) copy-start(bf16[1536,256]{0,1:T(8,128)(2,1)S(1)} %get-tuple-element.353) | copy-start | bytes 2359300 | tf_op jit(solution)/shard_map/while
  196.9 4.6 %copy-start.2 = (bf16[768,256]{0,1:T(8,128)(2,1)}, bf16[768,256]{0,1:T(8,128)(2,1)S(1)}, u32[]{:S(2)}) copy-start(bf16[768,256]{0,1:T(8,128)(2,1)S(1)} %constant_dynamic-slice_fusion.12) | copy-start | bytes 1179652 | tf_op jit(solution)/shard_map/while
  198.2 3.3 copy-start.9
  203.7 2.4 copy-start.1
  206.1 2.7 copy-start.10
  222.6 2.5 copy-start.3
  253.5 14.4 %collective-permute-start.3 = (bf16[512,256]{1,0:T(8,128)(2,1)S(1)}, bf16[512,256]{1,0:T(8,128)(2,1)S(1)}, u32[]{:S(2)}, u32[]{:S(2)}) collective-permute-start(bf16[512,256]{1,0:T(8,128)(2,1)S(1)} %get-tuple-element.239), channel_id=1, source_target_pairs={{4,0},{8,4},{12,8},{16,12},{20,16},{24,20},{28,24},{5,1},{9,5},{13... | collective-permute-start | bytes 786440 | tf_op jit(solution)/shard_map/ppermute | solution.py:17
  255.0 23.4 %collective-permute-start.2 = (bf16[512,256]{1,0:T(8,128)(2,1)S(1)}, bf16[512,256]{1,0:T(8,128)(2,1)S(1)}, u32[]{:S(2)}, u32[]{:S(2)}) collective-permute-start(bf16[512,256]{1,0:T(8,128)(2,1)S(1)} %get-tuple-element.241), channel_id=1, source_target_pairs={{4,0},{8,4},{12,8},{16,12},{20,16},{24,20},{28,24},{5,1},{9,5},{13... | collective-permute-start | bytes 786440 | tf_op jit(solution)/shard_map/ppermute | solution.py:17
  (22 other events, 30.8 us)
Sparse Core Ops, SparseCore 0:
  9.6 75.8 all-gather.1
  252.1 192.4 reduce-scatter.3
where the time goes:
time: 456 us; the launch traced here: 454 us
  waiting for transfers between devices  255 us (56%)
  local copies, waits for them, and re-layouts  81.7 us (18%)
  matrix products  64.8 us (14%)
  other arithmetic  26.9 us (6%)
  between operations  14.2 us (3%)
  starting transfers between devices  11.1 us (2%)
    unnamed x3, waiting for transfers between devices  166 us
    all_gather x1, waiting for transfers between devices, shards(): grad_full = lax.all_gather(out_grad, 'mp', axis=0, tiled=True)  48.8 us
    ppermute x4, waiting for transfers between devices, shifted(): return lax.ppermute(x, axis, pairs)  39.9 us
    unnamed x13, local copies, waits for them, and re-layouts  16.8 us
    dynamic_update_slice x8, local copies, waits for them, and re-layouts, step(): lax.dynamic_update_slice_in_dim(value_gradient_total, earlier_values + va...  14.4 us
    dynamic_slice x8, local copies, waits for them, and re-layouts, step(): lax.dynamic_slice_in_dim(key_gradient_total, start_position, WINDOW_KEYS...  13.2 us
    dot_general x1, matrix products, shards(): lax.dot_general(grad_full, attn_all, (((0,), (0,)), ((), ())), preferred_...  12.7 us
    sub x4, matrix products, band_grads(): weights = jnp.exp(scores - top)  12.2 us
  transfers between devices with their start and end apart: 6, of which 6 were waited for; matrix products, arithmetic and copies ran while one was open for 1% of the time, Pallas kernels for 0%

commit v1 on v0

v1 whole, which is shorter than its diff:
```python
import functools

import jax
import jax.numpy as jnp
from jax import lax
from jax.experimental import pallas as pl
from jax.experimental.pallas import tpu as pltpu
from jax.sharding import PartitionSpec as P

HEAD_SIZE = 128
WINDOW_KEYS = 512
SCALE = 168.0 ** (-0.5)
LOG2E = 1.4426950408889634
NEG = -1e30
TILE = WINDOW_KEYS // 2
F32 = jnp.float32
BF16 = jnp.bfloat16
VMEM_LIMIT = 28 * 1024 * 1024


def dot(a, b, contract_a, contract_b):
    return lax.dot_general(
        a, b, (((contract_a,), (contract_b,)), ((), ())), preferred_element_type=F32
    )


def vmem():
    return pl.BlockSpec(memory_space=pltpu.VMEM)


def smem():
    return pl.BlockSpec(memory_space=pltpu.SMEM)


def params():
    return pltpu.CompilerParams(vmem_limit_bytes=VMEM_LIMIT)


def cost(flops, nbytes, trans=0):
    return pl.CostEstimate(flops=flops, bytes_accessed=nbytes, transcendentals=trans)


def gather_columns_kernel(blocks, blk, lens, og_ref, *out_refs):
    off = 0
    for out, length in zip(out_refs, lens):
        out[...] = jnp.concatenate(
            [og_ref[:, t * blk + off : t * blk + off + length] for t in range(blocks)], axis=1
        )
        off += length


def gather_columns(og, blocks, lens):
    rows, width = og.shape
    return pl.pallas_call(
        functools.partial(gather_columns_kernel, blocks, width // blocks, lens),
        out_shape=[jax.ShapeDtypeStruct((rows, blocks * n), BF16) for n in lens],
        in_specs=[vmem()],
        out_specs=[vmem() for _ in lens],
        compiler_params=params(),
        cost_estimate=cost(0, 4 * rows * width),
        name="gather_columns",
    )(og)


def forward_kernel(kv_local, group, first, flag_ref, q_ref, k_ref, v_ref, attn_ref, prob_ref):
    row = lax.broadcasted_iota(jnp.int32, (TILE, TILE), 0)
    col = lax.broadcasted_iota(jnp.int32, (TILE, TILE), 1)
    upper = col > row
    if first:
        has_prev = flag_ref[0] > 0
    for g in range(kv_local):
        gcols = slice(g * HEAD_SIZE, (g + 1) * HEAD_SIZE)
        for i in range(2):
            k = k_ref[i * TILE : i * TILE + 3 * TILE, gcols]
            v = v_ref[i * TILE : i * TILE + 3 * TILE, gcols]
            for h in range(group):
                head = g * group + h
                hcols = slice(head * HEAD_SIZE, (head + 1) * HEAD_SIZE)
                q = q_ref[i * TILE : (i + 1) * TILE, hcols]
                s = dot(q, k, 1, 1)
                s0, s1, s2 = s[:, :TILE], s[:, TILE : 2 * TILE], s[:, 2 * TILE :]
                if first:
                    s0 = jnp.where(has_prev, s0, NEG)
                    if i == 0:
                        s1 = jnp.where(has_prev, s1, NEG)
                edge = jnp.where(upper, s0, s2)
                top = jnp.max(jnp.maximum(edge, s1), axis=1, keepdims=True)
                edge = jnp.exp2((edge - top) * (SCALE * LOG2E))
                mid = jnp.exp2((s1 - top) * (SCALE * LOG2E))
                inv = 1.0 / jnp.sum(edge + mid, axis=1, keepdims=True)
                edge = edge * inv
                p0 = jnp.where(upper, edge, 0.0).astype(BF16)
                p1 = (mid * inv).astype(BF16)
                p2 = jnp.where(upper, 0.0, edge).astype(BF16)
                prob_ref[g, i, h, :, :TILE] = p0
                prob_ref[g, i, h, :, TILE : 2 * TILE] = p1
                prob_ref[g, i, h, :, 2 * TILE :] = p2
                attn = dot(jnp.concatenate([p0, p1, p2], axis=1), v, 1, 0)
                attn_ref[i * TILE : (i + 1) * TILE, hcols] = attn.astype(BF16)


def forward(flag, q, k, v, first):
    rows, width = q.shape
    kv_local = k.shape[1] // HEAD_SIZE
    group = width // k.shape[1]
    return pl.pallas_call(
        functools.partial(forward_kernel, kv_local, group, first),
        out_shape=[
            jax.ShapeDtypeStruct((rows, width), BF16),
            jax.ShapeDtypeStruct((kv_local, 2, group, TILE, 3 * TILE), BF16),
        ],
        in_specs=[smem(), vmem(), vmem(), vmem()],
        out_specs=[vmem(), vmem()],
        compiler_params=params(),
        cost_estimate=cost(16 * rows * width * 3 * TILE, 8 * rows * width),
        name="attention_forward_first" if first else "attention_forward_second",
    )(flag, q, k, v)


def backward_kernel(kv_local, group, first, q_ref, k_ref, v_ref, do_ref, attn_ref, prob_ref, *rest):
    if first:
        dq_ref, halo_ref, own_ref, dk_acc, dv_acc = rest
    else:
        prev_ref, dq_ref, done_ref, own_ref, dk_acc, dv_acc = rest
    kv_width = kv_local * HEAD_SIZE
    for g in range(kv_local):
        gcols = slice(g * HEAD_SIZE, (g + 1) * HEAD_SIZE)
        for i in range(2):
            rows = slice(i * TILE, (i + 1) * TILE)
            span = slice(i * TILE, i * TILE + 3 * TILE)
            k = k_ref[span, gcols]
            v = v_ref[span, gcols]
            dk = jnp.zeros((HEAD_SIZE, 3 * TILE), F32)
            dv = jnp.zeros((HEAD_SIZE, 3 * TILE), F32)
            for h in range(group):
                head = g * group + h
                hcols = slice(head * HEAD_SIZE, (head + 1) * HEAD_SIZE)
                q = q_ref[rows, hcols]
                do = do_ref[rows, hcols]
                delta = jnp.sum(
                    do.astype(F32) * attn_ref[rows, hcols].astype(F32), axis=1, keepdims=True
                )
                p = prob_ref[g, i, h]
                ds = (p.astype(F32) * (dot(do, v, 1, 1) - delta)).astype(BF16)
                dq_ref[rows, hcols] = (dot(ds, k, 1, 0) * SCALE).astype(BF16)
                dk += dot(q, ds, 0, 0)
                dv += dot(do, p, 0, 0)
            if i == 0:
                dk_acc[:, : 3 * TILE] = dk
                dv_acc[:, : 3 * TILE] = dv
            else:
                dk_acc[:, TILE : 3 * TILE] += dk[:, : 2 * TILE]
                dv_acc[:, TILE : 3 * TILE] += dv[:, : 2 * TILE]
                dk_acc[:, 3 * TILE :] = dk[:, 2 * TILE :]
                dv_acc[:, 3 * TILE :] = dv[:, 2 * TILE :]
        for acc, base, factor in ((dk_acc, 0, SCALE), (dv_acc, kv_width, 1.0)):
            cols = slice(base + g * HEAD_SIZE, base + (g + 1) * HEAD_SIZE)
            low = acc[:, :WINDOW_KEYS].T
            high = acc[:, WINDOW_KEYS:].T
            if factor != 1.0:
                low, high = low * factor, high * factor
            if first:
                halo_ref[:, cols] = low.astype(BF16)
            else:
                done_ref[:, cols] = (low + prev_ref[:, cols]).astype(BF16)
            own_ref[:, cols] = high


def backward(q, k, v, do, attn, prob, prev=None):
    first = prev is None
    rows, width = q.shape
    kv_width = k.shape[1]
    kv_local = kv_width // HEAD_SIZE
    group = width // kv_width
    args = [q, k, v, do, attn, prob] + ([] if first else [prev])
    return pl.pallas_call(
        functools.partial(backward_kernel, kv_local, group, first),
        out_shape=[
            jax.ShapeDtypeStruct((rows, width), BF16),
            jax.ShapeDtypeStruct((WINDOW_KEYS, 2 * kv_width), BF16),
            jax.ShapeDtypeStruct((WINDOW_KEYS, 2 * kv_width), F32),
        ],
        in_specs=[vmem() for _ in args],
        out_specs=[vmem() for _ in range(3)],
        scratch_shapes=[
            pltpu.VMEM((HEAD_SIZE, 4 * TILE), F32),
            pltpu.VMEM((HEAD_SIZE, 4 * TILE), F32),
        ],
        compiler_params=params(),
        cost_estimate=cost(16 * rows * width * 3 * TILE, 8 * rows * width),
        name="attention_backward_first" if first else "attention_backward_second",
    )(*args)


def projection_kernel(peers, blocks, off, length, start, last, place_ref, *refs):
    og_refs = refs[:peers]
    refs = refs[peers:]
    w_ref, attn_ref = refs[:2]
    refs = refs[2:]
    if not start:
        acc_ref, refs = refs[0], refs[1:]
    out_ref, send_ref, keep_ref, w_vmem, part, sem = refs
    copy = pltpu.make_async_copy(w_ref.at[:, pl.ds(off, length), :], w_vmem, sem)
    copy.start()
    mine, context = place_ref[0], place_ref[1]
    width = attn_ref.shape[2]
    total = blocks * length
    attn = jnp.concatenate([attn_ref[mine ^ r] for r in range(peers)], axis=0)
    step = 256 if total % 256 == 0 else 128
    for s in range(0, total, step):
        og = jnp.concatenate([og_ref[:, s : s + step] for og_ref in og_refs], axis=0)
        part[s : s + step, :] = dot(og, attn, 0, 0)
    for i in range(blocks // 2):
        target = (2 * i) ^ context
        at = pl.multiple_of(target * length, 8)
        keep_ref[i] = part[pl.ds(at, length), :].astype(keep_ref.dtype)
        at = pl.multiple_of((target ^ 1) * length, 8)
        send_ref[i] = part[pl.ds(at, length), :].astype(BF16)
    copy.wait()
    w = w_vmem[...].reshape(total, width)
    for r in range(peers):
        out = dot(og_refs[r][...], w, 1, 0)
        if not start:
            out = out + acc_ref[r]
        if last:
            out_ref[mine ^ r] = out.astype(BF16)
        else:
            out_ref[r] = out


def projection(place, ogs, w, attn, acc, blocks, off, length, last):
    peers = len(ogs)
    rows, total = ogs[0].shape
    width = attn.shape[2]
    start = acc is None
    args = [place, *ogs, w, attn] + ([] if start else [acc])
    specs = [smem()] + [vmem()] * peers + [pl.BlockSpec(memory_space=pl.ANY), vmem()]
    specs += [] if start else [vmem()]
    half = jax.ShapeDtypeStruct((blocks // 2, length, width), BF16)
    return pl.pallas_call(
        functools.partial(projection_kernel, peers, blocks, off, length, start, last),
        out_shape=[
            jax.ShapeDtypeStruct((peers, rows, width), BF16 if last else F32),
            half,
            half,
        ],
        in_specs=specs,
        out_specs=[vmem()] * 3,
        scratch_shapes=[
            pltpu.VMEM((blocks, length, width), BF16),
            pltpu.VMEM((total, width), F32),
            pltpu.SemaphoreType.DMA,
        ],
        compiler_params=params(),
        cost_estimate=cost(4 * peers * rows * total * width, 4 * rows * peers * total),
        name="projection",
    )(*args)


def chunk_lengths(blk):
    if blk == 672:
        return (224, 192, 160, 96)
    return (blk,)


def exchange(x, axis, by):
    return lax.ppermute(x, axis, [(i, i ^ by) for i in range(lax.axis_size(axis))])


def shards(queries, keys, values, out_grad, out_weight):
    shard, width = queries.shape
    kv_width = keys.shape[1]
    contexts = lax.axis_size("context")
    peers = lax.axis_size("mp")
    context = lax.axis_index("context")
    mine = lax.axis_index("mp")
    blk = out_weight.shape[0] // contexts
    lens = chunk_lengths(blk)
    half = WINDOW_KEYS

    halo = jnp.concatenate([keys[shard - half :], values[shard - half :]], axis=1)
    halo = lax.ppermute(halo, "context", [(i, i + 1) for i in range(contexts - 1)])
    if len(lens) == 1:
        own = [out_grad]
    else:
        own = gather_columns(out_grad, contexts, lens)
    gathered = []
    for og in own:
        parts = [og, exchange(og, "mp", 1)]
        for by in range(2, peers, 2):
            far = exchange(og, "mp", by)
            parts += [far, exchange(far, "mp", 1)]
        gathered.append(parts)

    flag = context.reshape(1).astype(jnp.int32)
    place = jnp.stack([mine, context]).astype(jnp.int32)
    attn_high, prob_high = forward(flag, queries[half:], keys, values, False)
    key_window = jnp.concatenate([halo[:, :kv_width], keys[:half]], axis=0)
    value_window = jnp.concatenate([halo[:, kv_width:], values[:half]], axis=0)
    attn_low, prob_low = forward(flag, queries[:half], key_window, value_window, True)
    attn = jnp.concatenate([attn_low, attn_high], axis=0).reshape(peers, shard // peers, width)

    weight = out_weight.reshape(contexts, blk, width)
    acc, off, reduced = None, 0, []
    for j, length in enumerate(lens):
        acc, send, keep = projection(
            place, gathered[j], weight, attn, acc, contexts, off, length, j == len(lens) - 1
        )
        off += length
        by, count = 1, contexts // 2
        order = list(range(count))
        keep = keep.astype(F32)
        while True:
            keep = keep + exchange(send, "context", by).astype(F32)
            if count == 1:
                break
            by, count = by * 2, count // 2
            send, keep = keep[1::2].astype(BF16), keep[0::2]
        reduced.append(keep[0])
    weight_grad = jnp.concatenate(reduced, axis=0).astype(BF16)

    dout = acc.reshape(shard, width)
    dq_low, halo_grad, own_low = backward(
        queries[:half], key_window, value_window, dout[:half], attn_low, prob_low
    )
    halo_grad = lax.ppermute(halo_grad, "context", [(i + 1, i) for i in range(contexts - 1)])
    dq_high, done, own_high = backward(
        queries[half:], keys, values, dout[half:], attn_high, prob_high, own_low
    )
    own_high = (own_high + halo_grad.astype(F32)).astype(BF16)
    query_grad = jnp.concatenate([dq_low, dq_high], axis=0)
    kv_grad = jnp.concatenate([done, own_high], axis=0)
    return query_grad, kv_grad[:, :kv_width], kv_grad[:, kv_width:], weight_grad


def solution(mesh):
    return jax.shard_map(
        shards,
        mesh=mesh,
        in_specs=(
            P("context", "mp"),
            P("context", "mp"),
            P("context", "mp"),
            P(("context", "mp"), None),
            P(None, "mp"),
        ),
        out_specs=(P("context", "mp"), P("context", "mp"), P("context", "mp"), P("context", "mp")),
        check_vma=False,
    )
```

time: 456 us -> 199 us (0.44)
  waiting for transfers between devices: 255 us -> 124 us
  local copies, waits for them, and re-layouts: 81.7 us -> 5.59 us
  matrix products: 64.8 us -> 0 us
  Pallas kernels: 0 us -> 35 us
  other arithmetic: 26.9 us -> 6.7 us
  starting transfers between devices: 11.1 us -> 26.1 us
  between operations: 14.2 us -> 1.02 us
    unnamed x3 -> x0, waiting for transfers between devices: 166 us -> none
    ppermute x4 -> x26, waiting for transfers between devices: 39.9 us -> 124 us  [the longest x24 124 us: exchange(): lax.ppermute(x, axis, [(i, i ^ by) for i in range(lax.axis_size(axis))])]
    dot_general x22 -> x0, matrix products: 52.7 us -> none  [the longest x1 12.7 us: shards(): lax.dot_general(grad_full, attn_all, (((0,), (0,)), ((), ())), preferred_...]
    all_gather x1 -> x0, waiting for transfers between devices: 48.8 us -> none  [shards(): grad_full = lax.all_gather(out_grad, 'mp', axis=0, tiled=True)]
    pallas_call x0 -> x9, Pallas kernels: none -> 35 us  [the longest x4 19 us: projection(): pl.pallas_call(functools.partial(projection_kernel, peers, blocks, off, l...]
    dynamic_update_slice x24 -> x0, local copies, waits for them, and re-layouts: 30.1 us -> none  [the longest x8 14.4 us: step(): lax.dynamic_update_slice_in_dim(value_gradient_total, earlier_values + va...]
    dynamic_slice x40 -> x0, local copies, waits for them, and re-layouts: 29.7 us -> none  [the longest x8 13.2 us: step(): lax.dynamic_slice_in_dim(key_gradient_total, start_position, WINDOW_KEYS...]
    ppermute x4 -> x26, starting transfers between devices: 11 us -> 26.1 us  [the longest x24 20.4 us: exchange(): lax.ppermute(x, axis, [(i, i ^ by) for i in range(lax.axis_size(axis))])]
  transfers between devices with their start and end apart: 6 -> 26, of which waited for: 6 -> 12; matrix products, arithmetic and copies ran while one was open for 1% -> 4% of each run, Pallas kernels for 0% -> 17%
where the time goes in v1:
time: 199 us; the launch traced here: 198 us
  waiting for transfers between devices  124 us (62%)
  Pallas kernels  35 us (18%)
  starting transfers between devices  26.1 us (13%)
  other arithmetic  6.7 us (3%)
  local copies, waits for them, and re-layouts  5.59 us (3%)
    ppermute x24, waiting for transfers between devices, exchange(): lax.ppermute(x, axis, [(i, i ^ by) for i in range(lax.axis_size(axis))])  124 us
    ppermute x24, starting transfers between devices, exchange(): lax.ppermute(x, axis, [(i, i ^ by) for i in range(lax.axis_size(axis))])  20.4 us
    pallas_call x4, Pallas kernels, projection(): pl.pallas_call(functools.partial(projection_kernel, peers, blocks, off, l...  19 us
    pallas_call x2, Pallas kernels, forward(): pl.pallas_call(functools.partial(forward_kernel, kv_local, group, first),...  8.46 us
    pallas_call x2, Pallas kernels, backward(): pl.pallas_call(functools.partial(backward_kernel, kv_local, group, first)...  6.05 us
    ppermute x1, starting transfers between devices, shards(): lax.ppermute(halo, 'context', [(i, i + 1) for i in range(contexts - 1)])  4.43 us
  transfers between devices with their start and end apart: 26, of which 12 were waited for; matrix products, arithmetic and copies ran while one was open for 4% of the time, Pallas kernels for 17%

profile of v1, /device:TPU:0, one launch (start us, length us, event | category | flops | bytes accessed | tf_op | source)
XLA Modules:
  0.0 198.3 jit_solution(6510943017240897146)
XLA Ops:
  0.6 1.8 copy-done
  2.4 1.5 gather_columns.1
  3.9 3.0 %collective-permute-start.11 = (bf16[256,1792]{1,0:T(8,128)(2,1)}, bf16[256,1792]{1,0:T(8,128)(2,1)}, u32[]{:S(2)}, u32[]{:S(2)}) collective-permute-start(bf16[256,1792]{1,0:T(8,128)(2,1)} %get-tuple-element.35.refs_0_), channel_id=1, source_target_pairs={{0,2},{1,3},{2,0},{3,1},{4,6},{5,7},{6,4},{7,5},{8,10},{9,11},{10,... | collective-permute-start | bytes 2752520 | tf_op jit(solution)/shard_map/ppermute | solution.py:267
  9.0 4.4 %collective-permute-start = (bf16[512,512]{1,0:T(8,128)(2,1)}, bf16[512,512]{1,0:T(8,128)(2,1)}, u32[]{:S(2)}, u32[]{:S(2)}) collective-permute-start(bf16[512,512]{1,0:T(8,128)(2,1)} %pad_maximum_fusion.4), channel_id=1, source_target_pairs={{0,4},{4,8},{8,12},{12,16},{16,20},{20,24},{24,28},{1,5},{5,9},{9,... | collective-permute-start | bytes 1572872 | tf_op jit(solution)/shard_map/ppermute | solution.py:282
  13.5 14.8 %collective-permute-done.11.refs_2_ = bf16[256,1792]{1,0:T(8,128)(2,1)} collective-permute-done((bf16[256,1792]{1,0:T(8,128)(2,1)}, bf16[256,1792]{1,0:T(8,128)(2,1)}, u32[]{:S(2)}, u32[]{:S(2)}) %collective-permute-start.11) | collective-permute-done | bytes 917536 | tf_op jit(solution)/shard_map/ppermute | solution.py:267
  28.4 4.2 %attention_forward_second.1 = (bf16[512,512]{1,0:T(8,128)(2,1)S(1)}, bf16[2,2,2,256,768]{4,3,2,1,0:T(8,128)(2,1)S(1)}) custom-call(s32[1]{0:T(128)} %bitcast.1.flag_ref, bf16[512,512]{1,0:T(8,128)(2,1)S(1)} %get-tuple-element.67.q_ref, bf16[1024,256]{1,0:T(8,128)(2,1)S(1)} %copy-done.1, bf16[1024,256]{1,0:T(8,128)(2,1)S(1)} %copy-done.2), custom_call_target="tpu_custom_call" | custom-call | flops 3221225472 | bytes 2097152 | tf_op jit(solution)/shard_map/attention_forward_second/pallas_call | solution.py:106
  32.6 1.6 copy-done.5
  34.3 2.0 %collective-permute-start.5 = (bf16[256,1280]{1,0:T(8,128)(2,1)S(1)}, bf16[256,1280]{1,0:T(8,128)(2,1)S(1)}, u32[]{:S(2)}, u32[]{:S(2)}) collective-permute-start(bf16[256,1280]{1,0:T(8,128)(2,1)S(1)} %get-tuple-element.33.refs_0_), channel_id=1, source_target_pairs={{0,2},{1,3},{2,0},{3,1},{4,6},{5,7},{6,4},{7,5},{8,10},{9,11},{10,... | collective-permute-start | bytes 1966088 | tf_op jit(solution)/shard_map/ppermute | solution.py:267
  38.4 6.8 %collective-permute-done.8.refs_2_ = bf16[256,1536]{1,0:T(8,128)(2,1)} collective-permute-done((bf16[256,1536]{1,0:T(8,128)(2,1)}, bf16[256,1536]{1,0:T(8,128)(2,1)}, u32[]{:S(2)}, u32[]{:S(2)}) %collective-permute-start.8) | collective-permute-done | bytes 786464 | tf_op jit(solution)/shard_map/ppermute | solution.py:267
  45.2 4.2 %attention_forward_first.1 = (bf16[512,512]{1,0:T(8,128)(2,1)S(1)}, bf16[2,2,2,256,768]{4,3,2,1,0:T(8,128)(2,1)S(1)}) custom-call(s32[1]{0:T(128)} %bitcast.1.flag_ref, bf16[512,512]{1,0:T(8,128)(2,1)S(1)} %get-tuple-element.66.q_ref, bf16[1024,256]{1,0:T(8,128)(2,1)S(1)} %pad_maximum_fusion.5.k_ref, bf16[1024,256]{1,0:T(8,128)(2,1)S(1)} %pad_maximum_fusion.6.v_ref), custom_call_target="tpu_custom_call" | custom-call | flops 3221225472 | bytes 2097152 | tf_op jit(solution)/shard_map/attention_forward_first/pallas_call | solution.py:106
  49.5 8.9 %collective-permute-done.5.refs_2_ = bf16[256,1280]{1,0:T(8,128)(2,1)S(1)} collective-permute-done((bf16[256,1280]{1,0:T(8,128)(2,1)S(1)}, bf16[256,1280]{1,0:T(8,128)(2,1)S(1)}, u32[]{:S(2)}, u32[]{:S(2)}) %collective-permute-start.5) | collective-permute-done | bytes 655392 | tf_op jit(solution)/shard_map/ppermute | solution.py:267
  58.3 1.8 collective-permute-start.2
  60.4 6.7 %projection.4 = (f32[4,256,512]{2,1,0:T(8,128)S(1)}, bf16[4,224,512]{2,1,0:T(8,128)(2,1)S(1)}, bf16[4,224,512]{2,1,0:T(8,128)(2,1)S(1)}) custom-call(s32[2]{0:T(128)S(1)} %pad_add_fusion.place_ref, bf16[256,1792]{1,0:T(8,128)(2,1)} %get-tuple-element.35.refs_0_, bf16[256,1792]{1,0:T(8,128)(2,1)} %collective-permute-done.10.refs_1_, ...), custom_call_target="tpu_custom_call" | custom-call | flops 3758096384 | bytes 7340032 | tf_op jit(solution)/shard_map/projection/pallas_call | solution.py:240
  67.1 2.8 %collective-permute-done.2.refs_2_ = bf16[256,768]{1,0:T(8,128)(2,1)S(1)} collective-permute-done((bf16[256,768]{1,0:T(8,128)(2,1)S(1)}, bf16[256,768]{1,0:T(8,128)(2,1)S(1)}, u32[]{:S(2)}, u32[]{:S(2)}) %collective-permute-start.2) | collective-permute-done | bytes 393248 | tf_op jit(solution)/shard_map/ppermute | solution.py:267
  70.4 1.7 collective-permute-start.14
  72.1 5.6 %projection.5 = (f32[4,256,512]{2,1,0:T(8,128)S(1)}, bf16[4,192,512]{2,1,0:T(8,128)(2,1)S(1)}, bf16[4,192,512]{2,1,0:T(8,128)(2,1)S(1)}) custom-call(s32[2]{0:T(128)S(1)} %pad_add_fusion.place_ref, bf16[256,1536]{1,0:T(8,128)(2,1)} %get-tuple-element.34.refs_0_, bf16[256,1536]{1,0:T(8,128)(2,1)} %collective-permute-done.7.refs_1_, ...), custom_call_target="tpu_custom_call" | custom-call | flops 3221225472 | bytes 6291456 | tf_op jit(solution)/shard_map/projection/pallas_call | solution.py:240
  78.0 3.9 %projection.6 = (f32[4,256,512]{2,1,0:T(8,128)S(1)}, bf16[4,160,512]{2,1,0:T(8,128)(2,1)S(1)}, bf16[4,160,512]{2,1,0:T(8,128)(2,1)S(1)}) custom-call(s32[2]{0:T(128)S(1)} %pad_add_fusion.place_ref, bf16[256,1280]{1,0:T(8,128)(2,1)S(1)} %get-tuple-element.33.refs_0_, bf16[256,1280]{1,0:T(8,128)(2,1)S(1)} %collective-permute-done.4.refs_1_, ...), custom_call_target="tpu_custom_call" | custom-call | flops 2684354560 | bytes 5242880 | tf_op jit(solution)/shard_map/projection/pallas_call | solution.py:240
  81.9 1.8 collective-permute-start.20
  83.7 2.9 %projection.7 = (bf16[4,256,512]{2,1,0:T(8,128)(2,1)S(1)}, bf16[4,96,512]{2,1,0:T(8,128)(2,1)S(1)}, bf16[4,96,512]{2,1,0:T(8,128)(2,1)S(1)}) custom-call(s32[2]{0:T(128)S(1)} %pad_add_fusion.place_ref, bf16[256,768]{1,0:T(8,128)(2,1)S(1)} %copy-done.4, bf16[256,768]{1,0:T(8,128)(2,1)S(1)} %collective-permute-done.1.refs_1_, ...), custom_call_target="tpu_custom_call" | custom-call | flops 1610612736 | bytes 3145728 | tf_op jit(solution)/shard_map/projection/pallas_call | solution.py:240
  87.1 3.0 %attention_backward_first.1 = (bf16[512,512]{1,0:T(8,128)(2,1)S(1)}, bf16[512,512]{1,0:T(8,128)(2,1)S(1)}, f32[512,512]{1,0:T(8,128)S(1)}) custom-call(bf16[512,512]{1,0:T(8,128)(2,1)S(1)} %get-tuple-element.66.q_ref, bf16[1024,256]{1,0:T(8,128)(2,1)S(1)} %pad_maximum_fusion.5.k_ref, bf16[1024,256]{1,0:T(8,128)(2,1)S(1)} %pad_maximum_fusion.6.v_ref, ...), custom_call_target="tpu_custom_call" | custom-call | flops 3221225472 | bytes 2097152 | tf_op jit(solution)/shard_map/attention_backward_first/pallas_call | solution.py:176
  91.4 3.0 %attention_backward_second.1 = (bf16[512,512]{1,0:T(8,128)(2,1)S(1)}, bf16[512,512]{1,0:T(8,128)(2,1)S(1)}, f32[512,512]{1,0:T(8,128)S(1)}) custom-call(bf16[512,512]{1,0:T(8,128)(2,1)S(1)} %get-tuple-element.67.q_ref, bf16[1024,256]{1,0:T(8,128)(2,1)S(1)} %copy-done.1, bf16[1024,256]{1,0:T(8,128)(2,1)S(1)} %copy-done.2, bf16[512,512]{1,0:T(8,128)(2,1)S(1)} %bitcast.24, ...), custom_call_target="tpu_custom_call" | custom-call | flops 3221225472 | bytes 2097152 | tf_op jit(solution)/shard_map/attention_backward_second/pallas_call | solution.py:176
  95.5 47.0 %collective-permute-done.23 = bf16[4,96,512]{2,1,0:T(8,128)(2,1)S(1)} collective-permute-done((bf16[4,96,512]{2,1,0:T(8,128)(2,1)S(1)}, bf16[4,96,512]{2,1,0:T(8,128)(2,1)S(1)}, u32[]{:S(2)}, u32[]{:S(2)}) %collective-permute-start.23) | collective-permute-done | bytes 393248 | tf_op jit(solution)/shard_map/ppermute | solution.py:267
  142.6 1.6 collective-permute-start.24
  145.5 3.2 %collective-permute-done.24 = bf16[2,96,512]{2,1,0:T(8,128)(2,1)S(1)} collective-permute-done((bf16[2,96,512]{2,1,0:T(8,128)(2,1)S(1)}, bf16[2,96,512]{2,1,0:T(8,128)(2,1)S(1)}, u32[]{:S(2)}, u32[]{:S(2)}) %collective-permute-start.24) | collective-permute-done | bytes 196640 | tf_op jit(solution)/shard_map/ppermute | solution.py:267
  148.8 2.7 %collective-permute-start.25 = (bf16[1,96,512]{2,1,0:T(8,128)(2,1)S(1)}, bf16[1,96,512]{2,1,0:T(8,128)(2,1)S(1)}, u32[]{:S(2)}, u32[]{:S(2)}) collective-permute-start(bf16[1,96,512]{2,1,0:T(8,128)(2,1)S(1)} %slice.187), channel_id=1, source_target_pairs={{0,16},{4,20},{8,24},{12,28},{16,0},{20,4},{24,8},{28,12},{1,17},{... | collective-permute-start | bytes 294920 | tf_op jit(solution)/shard_map/ppermute | solution.py:267
  152.1 2.6 %collective-permute-done.25 = bf16[1,96,512]{2,1,0:T(8,128)(2,1)S(1)} collective-permute-done((bf16[1,96,512]{2,1,0:T(8,128)(2,1)S(1)}, bf16[1,96,512]{2,1,0:T(8,128)(2,1)S(1)}, u32[]{:S(2)}, u32[]{:S(2)}) %collective-permute-start.25) | collective-permute-done | bytes 98336 | tf_op jit(solution)/shard_map/ppermute | solution.py:267
  155.1 2.4 %collective-permute-start.18 = (bf16[2,192,512]{2,1,0:T(8,128)(2,1)S(1)}, bf16[2,192,512]{2,1,0:T(8,128)(2,1)S(1)}, u32[]{:S(2)}, u32[]{:S(2)}) collective-permute-start(bf16[2,192,512]{2,1,0:T(8,128)(2,1)S(1)} %slice.127), channel_id=1, source_target_pairs={{0,8},{4,12},{8,0},{12,4},{16,24},{20,28},{24,16},{28,20},{1,9},{5... | collective-permute-start | bytes 1179656 | tf_op jit(solution)/shard_map/ppermute | solution.py:267
  157.5 6.7 %collective-permute-done.21 = bf16[2,160,512]{2,1,0:T(8,128)(2,1)S(1)} collective-permute-done((bf16[2,160,512]{2,1,0:T(8,128)(2,1)S(1)}, bf16[2,160,512]{2,1,0:T(8,128)(2,1)S(1)}, u32[]{:S(2)}, u32[]{:S(2)}) %collective-permute-start.21) | collective-permute-done | bytes 327712 | tf_op jit(solution)/shard_map/ppermute | solution.py:267
  165.1 8.6 %collective-permute-done.22 = bf16[1,160,512]{2,1,0:T(8,128)(2,1)S(1)} collective-permute-done((bf16[1,160,512]{2,1,0:T(8,128)(2,1)S(1)}, bf16[1,160,512]{2,1,0:T(8,128)(2,1)S(1)}, u32[]{:S(2)}, u32[]{:S(2)}) %collective-permute-start.22) | collective-permute-done | bytes 163872 | tf_op jit(solution)/shard_map/ppermute | solution.py:267
  173.7 2.8 %collective-permute-done.18 = bf16[2,192,512]{2,1,0:T(8,128)(2,1)S(1)} collective-permute-done((bf16[2,192,512]{2,1,0:T(8,128)(2,1)S(1)}, bf16[2,192,512]{2,1,0:T(8,128)(2,1)S(1)}, u32[]{:S(2)}, u32[]{:S(2)}) %collective-permute-start.18) | collective-permute-done | bytes 393248 | tf_op jit(solution)/shard_map/ppermute | solution.py:267
  177.4 9.1 %collective-permute-done.15 = bf16[2,224,512]{2,1,0:T(8,128)(2,1)S(1)} collective-permute-done((bf16[2,224,512]{2,1,0:T(8,128)(2,1)S(1)}, bf16[2,224,512]{2,1,0:T(8,128)(2,1)S(1)}, u32[]{:S(2)}, u32[]{:S(2)}) %collective-permute-start.15) | collective-permute-done | bytes 458784 | tf_op jit(solution)/shard_map/ppermute | solution.py:267
  186.8 10.5 %collective-permute-done.16 = bf16[1,224,512]{2,1,0:T(8,128)(2,1)S(1)} collective-permute-done((bf16[1,224,512]{2,1,0:T(8,128)(2,1)S(1)}, bf16[1,224,512]{2,1,0:T(8,128)(2,1)S(1)}, u32[]{:S(2)}, u32[]{:S(2)}) %collective-permute-start.16) | collective-permute-done | bytes 229408 | tf_op jit(solution)/shard_map/ppermute | solution.py:267
  (83 shorter events, 13.6 us)
Async XLA Ops:
  2.4 5.0 %copy-start.2 = (bf16[1024,256]{1,0:T(8,128)(2,1)S(1)}, bf16[1024,256]{1,0:T(8,128)(2,1)}, u32[]{:S(2)}) copy-start(bf16[1024,256]{1,0:T(8,128)(2,1)} %v_ref.3) | copy-start | bytes 1572868
  3.9 9.6 %copy-start.3 = (bf16[256,768]{1,0:T(8,128)(2,1)}, bf16[256,768]{1,0:T(8,128)(2,1)S(1)}, u32[]{:S(2)}) copy-start(bf16[256,768]{1,0:T(8,128)(2,1)S(1)} %get-tuple-element.30.refs_0_) | copy-start | bytes 1179652
  3.9 9.5 %copy-start.7 = (bf16[1024,512]{1,0:T(8,128)(2,1)S(1)}, bf16[1024,512]{1,0:T(8,128)(2,1)}, u32[]{:S(2)}) copy-start(bf16[1024,512]{1,0:T(8,128)(2,1)} %param.5) | copy-start | bytes 3145732
  3.9 24.5 %collective-permute-start.11 = (bf16[256,1792]{1,0:T(8,128)(2,1)}, bf16[256,1792]{1,0:T(8,128)(2,1)}, u32[]{:S(2)}, u32[]{:S(2)}) collective-permute-start(bf16[256,1792]{1,0:T(8,128)(2,1)} %get-tuple-element.35.refs_0_), channel_id=1, source_target_pairs={{0,2},{1,3},{2,0},{3,1},{4,6},{5,7},{6,4},{7,5},{8,10},{9,11},{10,... | collective-permute-start | bytes 2752520 | tf_op jit(solution)/shard_map/ppermute | solution.py:267
  6.9 51.5 %collective-permute-start.10 = (bf16[256,1792]{1,0:T(8,128)(2,1)}, bf16[256,1792]{1,0:T(8,128)(2,1)}, u32[]{:S(2)}, u32[]{:S(2)}) collective-permute-start(bf16[256,1792]{1,0:T(8,128)(2,1)} %get-tuple-element.35.refs_0_), channel_id=1, source_target_pairs={{0,1},{1,0},{2,3},{3,2},{4,5},{5,4},{6,7},{7,6},{8,9},{9,8},{10,11... | collective-permute-start | bytes 2752520 | tf_op jit(solution)/shard_map/ppermute | solution.py:267
  6.9 38.3 %collective-permute-start.8 = (bf16[256,1536]{1,0:T(8,128)(2,1)}, bf16[256,1536]{1,0:T(8,128)(2,1)}, u32[]{:S(2)}, u32[]{:S(2)}) collective-permute-start(bf16[256,1536]{1,0:T(8,128)(2,1)} %get-tuple-element.34.refs_0_), channel_id=1, source_target_pairs={{0,2},{1,3},{2,0},{3,1},{4,6},{5,7},{6,4},{7,5},{8,10},{9,11},{10,... | collective-permute-start | bytes 2359304 | tf_op jit(solution)/shard_map/ppermute | solution.py:267
  7.0 62.9 %collective-permute-start.7 = (bf16[256,1536]{1,0:T(8,128)(2,1)}, bf16[256,1536]{1,0:T(8,128)(2,1)}, u32[]{:S(2)}, u32[]{:S(2)}) collective-permute-start(bf16[256,1536]{1,0:T(8,128)(2,1)} %get-tuple-element.34.refs_0_), channel_id=1, source_target_pairs={{0,1},{1,0},{2,3},{3,2},{4,5},{5,4},{6,7},{7,6},{8,9},{9,8},{10,11... | collective-permute-start | bytes 2359304 | tf_op jit(solution)/shard_map/ppermute | solution.py:267
  9.0 25.3 %collective-permute-start = (bf16[512,512]{1,0:T(8,128)(2,1)}, bf16[512,512]{1,0:T(8,128)(2,1)}, u32[]{:S(2)}, u32[]{:S(2)}) collective-permute-start(bf16[512,512]{1,0:T(8,128)(2,1)} %pad_maximum_fusion.4), channel_id=1, source_target_pairs={{0,4},{4,8},{8,12},{12,16},{16,20},{20,24},{24,28},{1,5},{5,9},{9,... | collective-permute-start | bytes 1572872 | tf_op jit(solution)/shard_map/ppermute | solution.py:282
  28.3 31.8 %collective-permute-start.12 = (bf16[256,1792]{1,0:T(8,128)(2,1)}, bf16[256,1792]{1,0:T(8,128)(2,1)}, u32[]{:S(2)}, u32[]{:S(2)}) collective-permute-start(bf16[256,1792]{1,0:T(8,128)(2,1)} %collective-permute-done.11.refs_2_), channel_id=1, source_target_pairs={{0,1},{1,0},{2,3},{3,2},{4,5},{5,4},{6,7},{7,6},{8,9},{9,8},{10,11... | collective-permute-start | bytes 2752520 | tf_op jit(solution)/shard_map/ppermute | solution.py:267
  34.3 24.0 %collective-permute-start.5 = (bf16[256,1280]{1,0:T(8,128)(2,1)S(1)}, bf16[256,1280]{1,0:T(8,128)(2,1)S(1)}, u32[]{:S(2)}, u32[]{:S(2)}) collective-permute-start(bf16[256,1280]{1,0:T(8,128)(2,1)S(1)} %get-tuple-element.33.refs_0_), channel_id=1, source_target_pairs={{0,2},{1,3},{2,0},{3,1},{4,6},{5,7},{6,4},{7,5},{8,10},{9,11},{10,... | collective-permute-start | bytes 1966088 | tf_op jit(solution)/shard_map/ppermute | solution.py:267
  45.2 25.2 %collective-permute-start.9 = (bf16[256,1536]{1,0:T(8,128)(2,1)}, bf16[256,1536]{1,0:T(8,128)(2,1)S(1)}, u32[]{:S(2)}, u32[]{:S(2)}) collective-permute-start(bf16[256,1536]{1,0:T(8,128)(2,1)} %collective-permute-done.8.refs_2_), channel_id=1, source_target_pairs={{0,1},{1,0},{2,3},{3,2},{4,5},{5,4},{6,7},{7,6},{8,9},{9,8},{10,11... | collective-permute-start | bytes 2359304 | tf_op jit(solution)/shard_map/ppermute | solution.py:267
  45.2 15.2 %slice-start = ((s8[5505024]{0:T(1024)(128)(4,1)}), s8[4194304]{0:T(1024)(128)(4,1)S(1)}, s32[]{:S(2)}) async-start(s8[5505024]{0:T(1024)(128)(4,1)} %bitcast.14), calls=%async_computation | async-start | bytes 8388608
  45.2 13.1 %copy-start.4 = (bf16[256,768]{1,0:T(8,128)(2,1)S(1)}, bf16[256,768]{1,0:T(8,128)(2,1)}, u32[]{:S(2)}) copy-start(bf16[256,768]{1,0:T(8,128)(2,1)} %copy-done.3) | copy-start | bytes 1179652
  45.2 15.2 %slice-start.1 = ((s8[5505024]{0:T(1024)(128)(4,1)}), s8[1310720]{0:T(1024)(128)(4,1)S(1)}, s32[]{:S(2)}) async-start(s8[5505024]{0:T(1024)(128)(4,1)} %bitcast.14), calls=%async_computation.1 | async-start | bytes 2621440
  58.3 19.3 %collective-permute-start.4 = (bf16[256,1280]{1,0:T(8,128)(2,1)S(1)}, bf16[256,1280]{1,0:T(8,128)(2,1)S(1)}, u32[]{:S(2)}, u32[]{:S(2)}) collective-permute-start(bf16[256,1280]{1,0:T(8,128)(2,1)S(1)} %get-tuple-element.33.refs_0_), channel_id=1, source_target_pairs={{0,1},{1,0},{2,3},{3,2},{4,5},{5,4},{6,7},{7,6},{8,9},{9,8},{10,11... | collective-permute-start | bytes 1966088 | tf_op jit(solution)/shard_map/ppermute | solution.py:267
  58.3 11.5 %collective-permute-start.2 = (bf16[256,768]{1,0:T(8,128)(2,1)S(1)}, bf16[256,768]{1,0:T(8,128)(2,1)S(1)}, u32[]{:S(2)}, u32[]{:S(2)}) collective-permute-start(bf16[256,768]{1,0:T(8,128)(2,1)S(1)} %copy-done.4), channel_id=1, source_target_pairs={{0,2},{1,3},{2,0},{3,1},{4,6},{5,7},{6,4},{7,5},{8,10},{9,11},{10,... | collective-permute-start | bytes 1179656 | tf_op jit(solution)/shard_map/ppermute | solution.py:267
  60.1 17.9 %collective-permute-start.6 = (bf16[256,1280]{1,0:T(8,128)(2,1)S(1)}, bf16[256,1280]{1,0:T(8,128)(2,1)S(1)}, u32[]{:S(2)}, u32[]{:S(2)}) collective-permute-start(bf16[256,1280]{1,0:T(8,128)(2,1)S(1)} %collective-permute-done.5.refs_2_), channel_id=1, source_target_pairs={{0,1},{1,0},{2,3},{3,2},{4,5},{5,4},{6,7},{7,6},{8,9},{9,8},{10,11... | collective-permute-start | bytes 1966088 | tf_op jit(solution)/shard_map/ppermute | solution.py:267
  69.8 13.8 %collective-permute-start.1 = (bf16[256,768]{1,0:T(8,128)(2,1)S(1)}, bf16[256,768]{1,0:T(8,128)(2,1)S(1)}, u32[]{:S(2)}, u32[]{:S(2)}) collective-permute-start(bf16[256,768]{1,0:T(8,128)(2,1)S(1)} %copy-done.4), channel_id=1, source_target_pairs={{0,1},{1,0},{2,3},{3,2},{4,5},{5,4},{6,7},{7,6},{8,9},{9,8},{10,11... | collective-permute-start | bytes 1179656 | tf_op jit(solution)/shard_map/ppermute | solution.py:267
  69.9 13.8 %collective-permute-start.3 = (bf16[256,768]{1,0:T(8,128)(2,1)S(1)}, bf16[256,768]{1,0:T(8,128)(2,1)S(1)}, u32[]{:S(2)}, u32[]{:S(2)}) collective-permute-start(bf16[256,768]{1,0:T(8,128)(2,1)S(1)} %collective-permute-done.2.refs_2_), channel_id=1, source_target_pairs={{0,1},{1,0},{2,3},{3,2},{4,5},{5,4},{6,7},{7,6},{8,9},{9,8},{10,11... | collective-permute-start | bytes 1179656 | tf_op jit(solution)/shard_map/ppermute | solution.py:267
  70.4 94.1 %collective-permute-start.14 = (bf16[4,224,512]{2,1,0:T(8,128)(2,1)S(1)}, bf16[4,224,512]{2,1,0:T(8,128)(2,1)S(1)}, u32[]{:S(2)}, u32[]{:S(2)}) collective-permute-start(bf16[4,224,512]{2,1,0:T(8,128)(2,1)S(1)} %get-tuple-element.49), channel_id=1, source_target_pairs={{0,4},{4,0},{8,12},{12,8},{16,20},{20,16},{24,28},{28,24},{1,5},{5... | collective-permute-start | bytes 2752520 | tf_op jit(solution)/shard_map/ppermute | solution.py:267
  77.7 77.1 %collective-permute-start.17 = (bf16[4,192,512]{2,1,0:T(8,128)(2,1)S(1)}, bf16[4,192,512]{2,1,0:T(8,128)(2,1)S(1)}, u32[]{:S(2)}, u32[]{:S(2)}) collective-permute-start(bf16[4,192,512]{2,1,0:T(8,128)(2,1)S(1)} %get-tuple-element.51), channel_id=1, source_target_pairs={{0,4},{4,0},{8,12},{12,8},{16,20},{20,16},{24,28},{28,24},{1,5},{5... | collective-permute-start | bytes 2359304 | tf_op jit(solution)/shard_map/ppermute | solution.py:267
  81.9 69.6 %collective-permute-start.20 = (bf16[4,160,512]{2,1,0:T(8,128)(2,1)S(1)}, bf16[4,160,512]{2,1,0:T(8,128)(2,1)S(1)}, u32[]{:S(2)}, u32[]{:S(2)}) collective-permute-start(bf16[4,160,512]{2,1,0:T(8,128)(2,1)S(1)} %get-tuple-element.53), channel_id=1, source_target_pairs={{0,4},{4,0},{8,12},{12,8},{16,20},{20,16},{24,28},{28,24},{1,5},{5... | collective-permute-start | bytes 1966088 | tf_op jit(solution)/shard_map/ppermute | solution.py:267
  86.6 55.9 %collective-permute-start.23 = (bf16[4,96,512]{2,1,0:T(8,128)(2,1)S(1)}, bf16[4,96,512]{2,1,0:T(8,128)(2,1)S(1)}, u32[]{:S(2)}, u32[]{:S(2)}) collective-permute-start(bf16[4,96,512]{2,1,0:T(8,128)(2,1)S(1)} %get-tuple-element.55), channel_id=1, source_target_pairs={{0,4},{4,0},{8,12},{12,8},{16,20},{20,16},{24,28},{28,24},{1,5},{5... | collective-permute-start | bytes 1179656 | tf_op jit(solution)/shard_map/ppermute | solution.py:267
  90.1 54.2 %collective-permute-start.13 = (bf16[512,512]{1,0:T(8,128)(2,1)S(1)}, bf16[512,512]{1,0:T(8,128)(2,1)S(1)}, u32[]{:S(2)}, u32[]{:S(2)}) collective-permute-start(bf16[512,512]{1,0:T(8,128)(2,1)S(1)} %get-tuple-element.47), channel_id=1, source_target_pairs={{4,0},{8,4},{12,8},{16,12},{20,16},{24,20},{28,24},{5,1},{9,5},{13... | collective-permute-start | bytes 1572872 | tf_op jit(solution)/shard_map/ppermute | solution.py:326
  142.6 6.1 %collective-permute-start.24 = (bf16[2,96,512]{2,1,0:T(8,128)(2,1)S(1)}, bf16[2,96,512]{2,1,0:T(8,128)(2,1)S(1)}, u32[]{:S(2)}, u32[]{:S(2)}) collective-permute-start(bf16[2,96,512]{2,1,0:T(8,128)(2,1)S(1)} %slice.135), channel_id=1, source_target_pairs={{0,8},{4,12},{8,0},{12,4},{16,24},{20,28},{24,16},{28,20},{1,9},{5... | collective-permute-start | bytes 589832 | tf_op jit(solution)/shard_map/ppermute | solution.py:267
  148.8 5.9 %collective-permute-start.25 = (bf16[1,96,512]{2,1,0:T(8,128)(2,1)S(1)}, bf16[1,96,512]{2,1,0:T(8,128)(2,1)S(1)}, u32[]{:S(2)}, u32[]{:S(2)}) collective-permute-start(bf16[1,96,512]{2,1,0:T(8,128)(2,1)S(1)} %slice.187), channel_id=1, source_target_pairs={{0,16},{4,20},{8,24},{12,28},{16,0},{20,4},{24,8},{28,12},{1,17},{... | collective-permute-start | bytes 294920 | tf_op jit(solution)/shard_map/ppermute | solution.py:267
  151.8 12.5 %collective-permute-start.21 = (bf16[2,160,512]{2,1,0:T(8,128)(2,1)S(1)}, bf16[2,160,512]{2,1,0:T(8,128)(2,1)S(1)}, u32[]{:S(2)}, u32[]{:S(2)}) collective-permute-start(bf16[2,160,512]{2,1,0:T(8,128)(2,1)S(1)} %slice.131), channel_id=1, source_target_pairs={{0,8},{4,12},{8,0},{12,4},{16,24},{20,28},{24,16},{28,20},{1,9},{5... | collective-permute-start | bytes 983048 | tf_op jit(solution)/shard_map/ppermute | solution.py:267
  155.1 21.4 %collective-permute-start.18 = (bf16[2,192,512]{2,1,0:T(8,128)(2,1)S(1)}, bf16[2,192,512]{2,1,0:T(8,128)(2,1)S(1)}, u32[]{:S(2)}, u32[]{:S(2)}) collective-permute-start(bf16[2,192,512]{2,1,0:T(8,128)(2,1)S(1)} %slice.127), channel_id=1, source_target_pairs={{0,8},{4,12},{8,0},{12,4},{16,24},{20,28},{24,16},{28,20},{1,9},{5... | collective-permute-start | bytes 1179656 | tf_op jit(solution)/shard_map/ppermute | solution.py:267
  164.4 9.3 %collective-permute-start.22 = (bf16[1,160,512]{2,1,0:T(8,128)(2,1)S(1)}, bf16[1,160,512]{2,1,0:T(8,128)(2,1)S(1)}, u32[]{:S(2)}, u32[]{:S(2)}) collective-permute-start(bf16[1,160,512]{2,1,0:T(8,128)(2,1)S(1)} %slice.186), channel_id=1, source_target_pairs={{0,16},{4,20},{8,24},{12,28},{16,0},{20,4},{24,8},{28,12},{1,17},{... | collective-permute-start | bytes 491528 | tf_op jit(solution)/shard_map/ppermute | solution.py:267
  164.8 21.7 %collective-permute-start.15 = (bf16[2,224,512]{2,1,0:T(8,128)(2,1)S(1)}, bf16[2,224,512]{2,1,0:T(8,128)(2,1)S(1)}, u32[]{:S(2)}, u32[]{:S(2)}) collective-permute-start(bf16[2,224,512]{2,1,0:T(8,128)(2,1)S(1)} %slice.123), channel_id=1, source_target_pairs={{0,8},{4,12},{8,0},{12,4},{16,24},{20,28},{24,16},{28,20},{1,9},{5... | collective-permute-start | bytes 1376264 | tf_op jit(solution)/shard_map/ppermute | solution.py:267
  176.7 10.1 %collective-permute-start.19 = (bf16[1,192,512]{2,1,0:T(8,128)(2,1)S(1)}, bf16[1,192,512]{2,1,0:T(8,128)(2,1)S(1)}, u32[]{:S(2)}, u32[]{:S(2)}) collective-permute-start(bf16[1,192,512]{2,1,0:T(8,128)(2,1)S(1)} %slice.185), channel_id=1, source_target_pairs={{0,16},{4,20},{8,24},{12,28},{16,0},{20,4},{24,8},{28,12},{1,17},{... | collective-permute-start | bytes 589832 | tf_op jit(solution)/shard_map/ppermute | solution.py:267
  186.7 10.7 %collective-permute-start.16 = (bf16[1,224,512]{2,1,0:T(8,128)(2,1)S(1)}, bf16[1,224,512]{2,1,0:T(8,128)(2,1)S(1)}, u32[]{:S(2)}, u32[]{:S(2)}) collective-permute-start(bf16[1,224,512]{2,1,0:T(8,128)(2,1)S(1)} %slice.184), channel_id=1, source_target_pairs={{0,16},{4,20},{8,24},{12,28},{16,0},{20,4},{24,8},{28,12},{1,17},{... | collective-permute-start | bytes 688136 | tf_op jit(solution)/shard_map/ppermute | solution.py:267
  (4 other events, 12.7 us)

commit v2 on v1

v2 whole, which is shorter than its diff:
```python
import functools

import jax
import jax.numpy as jnp
from jax import lax
from jax.experimental import pallas as pl
from jax.experimental.pallas import tpu as pltpu
from jax.sharding import PartitionSpec as P

HEAD_SIZE = 128
WINDOW_KEYS = 512
SCALE = 168.0 ** (-0.5)
LOG2E = 1.4426950408889634
NEG = -1e30
TILE = WINDOW_KEYS // 2
LAGS = (1, 2, 3, 4, 5)
TAIL_ONE = True


def TAIL(item):
    return (item[0] + item[1], item[0])


LENS = (160, 144, 128, 112, 80, 48)
SWAP = (0, 0, 0, 0, 0, 0)
PIECES = (1, 1, 1, 1, 1, 1)
AHEAD = 1
AHEAD_FROM = 0
COST = None
F32 = jnp.float32
BF16 = jnp.bfloat16
VMEM_LIMIT = 8 * 1024 * 1024


def dot(a, b, contract_a, contract_b):
    return lax.dot_general(
        a, b, (((contract_a,), (contract_b,)), ((), ())), preferred_element_type=F32
    )


def vmem():
    return pl.BlockSpec(memory_space=pltpu.VMEM)


def hbm():
    return pl.BlockSpec(memory_space=pltpu.HBM)


def params(times=1):
    return pltpu.CompilerParams(vmem_limit_bytes=times * VMEM_LIMIT)


def cost(flops, nbytes, trans=0):
    return COST


def prepare_kernel(blocks, blk, lens, og_ref, *refs):
    off = 0
    for out, length in zip(refs, lens):
        out[...] = jnp.concatenate(
            [og_ref[:, t * blk + off : t * blk + off + length] for t in range(blocks)], axis=1
        )
        off += length


def prepare(og, blocks, lens):
    rows, width = og.shape
    return pl.pallas_call(
        functools.partial(prepare_kernel, blocks, width // blocks, lens),
        out_shape=[jax.ShapeDtypeStruct((rows, blocks * n), BF16) for n in lens],
        in_specs=[vmem()],
        out_specs=[vmem() for _ in lens],
        compiler_params=params(),
        cost_estimate=cost(0, 4 * rows * width),
        name="gather_columns",
    )(og)


def pack_kernel(k_ref, v_ref, out_ref):
    rows = k_ref.shape[0]
    out_ref[0] = k_ref[rows - WINDOW_KEYS :, :]
    out_ref[1] = v_ref[rows - WINDOW_KEYS :, :]


def pack(keys, values):
    return pl.pallas_call(
        pack_kernel,
        out_shape=jax.ShapeDtypeStruct((2, WINDOW_KEYS, keys.shape[1]), BF16),
        in_specs=[vmem(), vmem()],
        out_specs=vmem(),
        compiler_params=params(),
        cost_estimate=cost(0, 8 * WINDOW_KEYS * keys.shape[1]),
        name="pack_halo",
    )(keys, values)


def window(first, i, g, which, prev_ref, own_ref):
    cols = slice(g * HEAD_SIZE, (g + 1) * HEAD_SIZE)
    start = i * TILE
    if not first:
        return own_ref[start : start + 3 * TILE, cols]
    low = prev_ref[which, start:, cols]
    return jnp.concatenate([low, own_ref[: start + TILE, cols]], axis=0)


def forward_kernel(kv_local, group, first, *refs):
    if first:
        q_ref, k_ref, v_ref, prev_ref, attn_ref, prob_ref = refs
        has_prev = lax.axis_index("context") > 0
        base = 0
    else:
        q_ref, k_ref, v_ref, attn_ref, prob_ref = refs
        prev_ref = None
        base = q_ref.shape[0] - WINDOW_KEYS
    row = lax.broadcasted_iota(jnp.int32, (TILE, TILE), 0)
    col = lax.broadcasted_iota(jnp.int32, (TILE, TILE), 1)
    upper = col > row
    for g in range(kv_local):
        for i in range(2):
            k = window(first, i, g, 0, prev_ref, k_ref)
            v = window(first, i, g, 1, prev_ref, v_ref)
            for h in range(group):
                head = g * group + h
                hcols = slice(head * HEAD_SIZE, (head + 1) * HEAD_SIZE)
                q = q_ref[base + i * TILE : base + (i + 1) * TILE, hcols]
                s = dot(q, k, 1, 1)
                s0, s1, s2 = s[:, :TILE], s[:, TILE : 2 * TILE], s[:, 2 * TILE :]
                if first:
                    s0 = jnp.where(has_prev, s0, NEG)
                    if i == 0:
                        s1 = jnp.where(has_prev, s1, NEG)
                edge = jnp.where(upper, s0, s2)
                top = jnp.max(jnp.maximum(edge, s1), axis=1, keepdims=True)
                edge = jnp.exp2((edge - top) * (SCALE * LOG2E))
                mid = jnp.exp2((s1 - top) * (SCALE * LOG2E))
                inv = 1.0 / jnp.sum(edge + mid, axis=1, keepdims=True)
                edge = edge * inv
                p0 = jnp.where(upper, edge, 0.0).astype(BF16)
                p1 = (mid * inv).astype(BF16)
                p2 = jnp.where(upper, 0.0, edge).astype(BF16)
                prob_ref[g, i, h, :, :TILE] = p0
                prob_ref[g, i, h, :, TILE : 2 * TILE] = p1
                prob_ref[g, i, h, :, 2 * TILE :] = p2
                attn = dot(jnp.concatenate([p0, p1, p2], axis=1), v, 1, 0)
                attn_ref[i * TILE : (i + 1) * TILE, hcols] = attn.astype(BF16)


def forward(q, k, v, prev=None):
    first = prev is not None
    width = q.shape[1]
    kv_local = k.shape[1] // HEAD_SIZE
    group = width // k.shape[1]
    args = [q, k, v] + ([prev] if first else [])
    return pl.pallas_call(
        functools.partial(forward_kernel, kv_local, group, first),
        out_shape=[
            jax.ShapeDtypeStruct((WINDOW_KEYS, width), BF16),
            jax.ShapeDtypeStruct((kv_local, 2, group, TILE, 3 * TILE), BF16),
        ],
        in_specs=[vmem() for _ in args],
        out_specs=[vmem(), vmem()],
        compiler_params=params(),
        cost_estimate=cost(16 * WINDOW_KEYS * width * 3 * TILE, 8 * WINDOW_KEYS * width),
        name="attention_forward_first" if first else "attention_forward_second",
    )(*args)


def backward_kernel(kv_local, group, first, *refs):
    q_ref, k_ref, v_ref, do_ref, attn_ref, prob_ref = refs[:6]
    if first:
        prev_ref, dq_ref, halo_ref, own_ref, dk_acc, dv_acc = refs[6:]
        base = 0
    else:
        low_ref, dq_ref, done_ref, own_ref, dk_acc, dv_acc = refs[6:]
        prev_ref = None
        base = q_ref.shape[0] - WINDOW_KEYS
    for g in range(kv_local):
        for i in range(2):
            rows = slice(i * TILE, (i + 1) * TILE)
            wide_rows = slice(base + i * TILE, base + (i + 1) * TILE)
            k = window(first, i, g, 0, prev_ref, k_ref)
            v = window(first, i, g, 1, prev_ref, v_ref)
            dk = jnp.zeros((HEAD_SIZE, 3 * TILE), F32)
            dv = jnp.zeros((HEAD_SIZE, 3 * TILE), F32)
            for h in range(group):
                head = g * group + h
                hcols = slice(head * HEAD_SIZE, (head + 1) * HEAD_SIZE)
                q = q_ref[wide_rows, hcols]
                do = do_ref[wide_rows, hcols]
                delta = jnp.sum(
                    do.astype(F32) * attn_ref[rows, hcols].astype(F32), axis=1, keepdims=True
                )
                p = prob_ref[g, i, h]
                ds = (p.astype(F32) * (dot(do, v, 1, 1) - delta)).astype(BF16)
                dq_ref[rows, hcols] = (dot(ds, k, 1, 0) * SCALE).astype(BF16)
                dk += dot(q, ds, 0, 0)
                dv += dot(do, p, 0, 0)
            if i == 0:
                dk_acc[:, : 3 * TILE] = dk
                dv_acc[:, : 3 * TILE] = dv
            else:
                dk_acc[:, TILE : 3 * TILE] += dk[:, : 2 * TILE]
                dv_acc[:, TILE : 3 * TILE] += dv[:, : 2 * TILE]
                dk_acc[:, 3 * TILE :] = dk[:, 2 * TILE :]
                dv_acc[:, 3 * TILE :] = dv[:, 2 * TILE :]
        cols = slice(g * HEAD_SIZE, (g + 1) * HEAD_SIZE)
        for which, acc, factor in ((0, dk_acc, SCALE), (1, dv_acc, 1.0)):
            low = acc[:, :WINDOW_KEYS].T
            high = acc[:, WINDOW_KEYS:].T
            if factor != 1.0:
                low, high = low * factor, high * factor
            if first:
                halo_ref[which, :, cols] = low.astype(BF16)
            else:
                done_ref[which, :, cols] = (low + low_ref[which, :, cols]).astype(BF16)
            own_ref[which, :, cols] = high


def backward(q, k, v, do, attn, prob, prev=None, low=None):
    first = prev is not None
    width = q.shape[1]
    kv_width = k.shape[1]
    args = [q, k, v, do, attn, prob, prev if first else low]
    return pl.pallas_call(
        functools.partial(backward_kernel, kv_width // HEAD_SIZE, width // kv_width, first),
        out_shape=[
            jax.ShapeDtypeStruct((WINDOW_KEYS, width), BF16),
            jax.ShapeDtypeStruct((2, WINDOW_KEYS, kv_width), BF16),
            jax.ShapeDtypeStruct((2, WINDOW_KEYS, kv_width), F32),
        ],
        in_specs=[vmem() for _ in args],
        out_specs=[vmem() for _ in range(3)],
        scratch_shapes=[
            pltpu.VMEM((HEAD_SIZE, 4 * TILE), F32),
            pltpu.VMEM((HEAD_SIZE, 4 * TILE), F32),
        ],
        compiler_params=params(),
        cost_estimate=cost(16 * WINDOW_KEYS * width * 3 * TILE, 8 * WINDOW_KEYS * width),
        name="attention_backward_first" if first else "attention_backward_second",
    )(*args)


def join_kernel(done_ref, own_ref, got_ref, dk_ref, dv_ref):
    for which, out in ((0, dk_ref), (1, dv_ref)):
        rows = out.shape[0]
        out[: rows - WINDOW_KEYS, :] = done_ref[which]
        high = own_ref[which] + got_ref[which].astype(F32)
        out[rows - WINDOW_KEYS :, :] = high.astype(BF16)


def join(done, own, got, rows):
    shape = jax.ShapeDtypeStruct((rows, own.shape[2]), BF16)
    return pl.pallas_call(
        join_kernel,
        out_shape=[shape, shape],
        in_specs=[vmem()] * 3,
        out_specs=[vmem()] * 2,
        compiler_params=params(),
        cost_estimate=cost(0, 12 * WINDOW_KEYS * own.shape[2]),
        name="join_gradients",
    )(done, own, got)


def concat_kernel(low_ref, high_ref, out_ref):
    rows = low_ref.shape[0]
    out_ref[:rows, :] = low_ref[...]
    out_ref[rows:, :] = high_ref[...]


def concat(low, high):
    return pl.pallas_call(
        concat_kernel,
        out_shape=jax.ShapeDtypeStruct((2 * low.shape[0], low.shape[1]), BF16),
        in_specs=[vmem()] * 2,
        out_specs=vmem(),
        compiler_params=params(),
        cost_estimate=cost(0, 4 * low.shape[0] * low.shape[1]),
        name="join_halves",
    )(low, high)


def add_kernel(keep_ref, *refs):
    count, length = keep_ref.shape[:2]
    pieces = len(refs) - (1 if count == 1 else 2)
    got_refs, out_refs = refs[:pieces], refs[pieces:]
    size = length // pieces
    for i in range(count):
        for p, got_ref in enumerate(got_refs):
            rows = slice(p * size, (p + 1) * size)
            total = keep_ref[i, rows, :].astype(F32) + got_ref[i].astype(F32)
            if count == 1:
                out_refs[0][rows, :] = total.astype(BF16)
            else:
                out = out_refs[i % 2]
                out[i // 2, rows, :] = total.astype(out.dtype)


def add(keep, got):
    count, length, width = keep.shape
    if count == 1:
        out_shape = [jax.ShapeDtypeStruct((length, width), BF16)]
    else:
        half = (count // 2, length, width)
        out_shape = [jax.ShapeDtypeStruct(half, F32), jax.ShapeDtypeStruct(half, BF16)]
    return pl.pallas_call(
        add_kernel,
        out_shape=out_shape,
        in_specs=[vmem()] * (1 + len(got)),
        out_specs=[vmem() for _ in out_shape],
        compiler_params=params(),
        cost_estimate=cost(0, 8 * count * length * width),
        name="add_partials",
    )(keep, *got)


def projection_kernel(peers, blocks, off, length, start, last, bits, pieces, *refs):
    og_refs = refs[:peers]
    w_ref, low_ref, high_ref = refs[peers : peers + 3]
    refs = refs[peers + 3 :]
    if not start:
        acc_ref, refs = refs[0], refs[1:]
    out_ref, keep_ref = refs[:2]
    send_refs = refs[2 : 2 + pieces]
    w_vmem, attn_all, part, sem = refs[2 + pieces :]
    copy = pltpu.make_async_copy(w_ref.at[:, pl.ds(off, length), :], w_vmem, sem)
    copy.start()
    mine, context = lax.axis_index("mp"), lax.axis_index("context")
    rows, width = og_refs[0].shape[0], low_ref.shape[1]
    total = blocks * length
    for r in range(peers // 2):
        attn_all[r] = low_ref[r * rows : (r + 1) * rows, :]
        attn_all[r + peers // 2] = high_ref[r * rows : (r + 1) * rows, :]
    attn = jnp.concatenate([attn_all[mine ^ r] for r in range(peers)], axis=0)
    step = 256 if total % 256 == 0 else 128
    for s in range(0, total, step):
        og = jnp.concatenate([og_ref[:, s : s + step] for og_ref in og_refs], axis=0)
        part[s : s + step, :] = dot(og, attn, 0, 0)
    size = length // pieces
    for i in range(blocks // 2):
        target = sum(bit for k, bit in enumerate(bits[1:]) if i >> k & 1) ^ context
        at = pl.multiple_of(target * length, 8)
        keep_ref[i] = part[pl.ds(at, length), :].astype(keep_ref.dtype)
        for p, send_ref in enumerate(send_refs):
            at = pl.multiple_of((target ^ bits[0]) * length + p * size, 8)
            send_ref[i] = part[pl.ds(at, size), :].astype(BF16)
    copy.wait()
    w = w_vmem[...].reshape(total, width)
    for r in range(peers):
        out = dot(og_refs[r][...], w, 1, 0)
        if not start:
            out = out + acc_ref[r]
        if last:
            out_ref[mine ^ r] = out.astype(BF16)
        else:
            out_ref[r] = out


def projection(ogs, w, low, high, acc, blocks, off, length, last, bits, pieces):
    peers = len(ogs)
    rows, total = ogs[0].shape
    width = low.shape[1]
    start = acc is None
    args = [*ogs, w, low, high] + ([] if start else [acc])
    specs = [vmem()] * peers + [hbm()] + [vmem()] * (2 if start else 3)
    keep = jax.ShapeDtypeStruct((blocks // 2, length, width), BF16)
    send = jax.ShapeDtypeStruct((blocks // 2, length // pieces, width), BF16)
    return pl.pallas_call(
        functools.partial(
            projection_kernel, peers, blocks, off, length, start, last, bits, pieces
        ),
        out_shape=[
            jax.ShapeDtypeStruct((peers, rows, width), BF16 if last else F32),
            keep,
            *[send] * pieces,
        ],
        in_specs=specs,
        out_specs=[vmem()] * (2 + pieces),
        scratch_shapes=[
            pltpu.VMEM((blocks, length, width), BF16),
            pltpu.VMEM((peers, rows, width), BF16),
            pltpu.VMEM((total, width), F32),
            pltpu.SemaphoreType.DMA,
        ],
        compiler_params=params(4 if start and last else 1),
        cost_estimate=cost(4 * peers * rows * total * width, 4 * rows * peers * total),
        name="projection",
    )(*args)


def chunk_plan(blk, contexts):
    bits = [1 << k for k in range(contexts.bit_length() - 1)]
    if blk != 672:
        return (blk,), (bits,), (1,)
    swapped = [bits[1], bits[0], *bits[2:]]
    return LENS, [swapped if swap else bits for swap in SWAP], PIECES


def exchange(x, axis, by):
    return lax.ppermute(x, axis, [(i, i ^ by) for i in range(lax.axis_size(axis))])


def after(done, x):
    return lax.optimization_barrier((x, done))[0]


def shards(queries, keys, values, out_grad, out_weight):
    shard, width = queries.shape
    contexts = lax.axis_size("context")
    peers = lax.axis_size("mp")
    blk = out_weight.shape[0] // contexts
    lens, orders, pieces = chunk_plan(blk, contexts)
    chunks = len(lens)
    weight = out_weight.reshape(contexts, blk, width)

    sibling = exchange(out_grad, "mp", 1)
    own = prepare(out_grad, contexts, lens)
    far = [[exchange(og, "mp", by) for by in range(2, peers, 2)] for og in own]
    halo = pack(after(own[0], keys), values)
    halo = lax.ppermute(halo, "context", [(i, i + 1) for i in range(contexts - 1)])

    attn_high, prob_high = forward(queries, keys, values)
    siblings = prepare(after(attn_high, sibling), contexts, lens)
    halo = after(siblings[0], halo)
    attn_low, prob_low = forward(queries, keys, values, halo)
    done = attn_low

    pending, reduced = [], [None] * chunks

    def reduce_step(item, done):
        chunk, stage, keep, got = item
        got = [after(done, piece) for piece in got]
        if keep.shape[0] == 1:
            reduced[chunk] = add(keep, got)[0]
            return reduced[chunk], None
        keep, send = add(keep, got)
        stage += 1
        return send, (chunk, stage, keep, [exchange(send, "context", orders[chunk][stage])])

    def reduce_round(pending, done):
        later = []
        for item in pending:
            done, item = reduce_step(item, done)
            if item is not None:
                later.append(item)
        return later, done

    def fetch(j, done):
        theirs = [after(done, og) for og in far[j]]
        return theirs, [exchange(og, "mp", 1) for og in theirs], theirs[-1]

    fetched = []
    acc, off = None, 0
    for j, length in enumerate(lens):
        want = min(chunks, j + 1 + (AHEAD if j >= AHEAD_FROM else 0))
        while len(fetched) < want:
            *item, done = fetch(len(fetched), done)
            fetched.append(item)
        theirs, theirs_sibling = fetched[j]
        parts = [own[j], after(done, siblings[j])]
        for og, og_sibling in zip(theirs, theirs_sibling):
            parts += [og, after(done, og_sibling)]
        acc, keep, *send = projection(
            parts, weight, attn_low, attn_high, acc, contexts, off, length, j == chunks - 1,
            orders[j], pieces[j],
        )
        done = acc
        off += length
        got = [exchange(piece, "context", orders[j][0]) for piece in send]
        pending.append((j, 0, keep, got))
        if j < chunks - 1:
            ready = [item for item in pending if item[0] + LAGS[item[1]] <= j]
            rest = [item for item in pending if item[0] + LAGS[item[1]] > j]
            ready, done = reduce_round(ready, done)
            pending = ready + rest

    dout = acc.reshape(shard, width)
    dq_low, halo_grad, own_low = backward(queries, keys, values, dout, attn_low, prob_low, halo)
    halo_grad = lax.ppermute(halo_grad, "context", [(i + 1, i) for i in range(contexts - 1)])
    dq_high, kv_low, own_high = backward(
        queries, keys, values, dout, attn_high, prob_high, low=own_low
    )
    dq = concat(dq_low, dq_high)
    done = own_high
    while pending:
        pending.sort(key=TAIL)
        count = 1 if TAIL_ONE else len(pending)
        ready, done = reduce_round(pending[:count], done)
        pending = ready + pending[count:]
    weight_grad = jnp.concatenate(reduced, axis=0)
    dk, dv = join(kv_low, own_high, halo_grad, shard)
    return dq, dk, dv, weight_grad


def solution(mesh):
    return jax.shard_map(
        shards,
        mesh=mesh,
        in_specs=(
            P("context", "mp"),
            P("context", "mp"),
            P("context", "mp"),
            P(("context", "mp"), None),
            P(None, "mp"),
        ),
        out_specs=(P("context", "mp"), P("context", "mp"), P("context", "mp"), P("context", "mp")),
        check_vma=False,
    )
```

time: 199 us -> 135 us (0.68)
  waiting for transfers between devices: 124 us -> 51 us
  starting transfers between devices: 26.1 us -> 43.8 us
  other arithmetic: 6.7 us -> 0 us
  local copies, waits for them, and re-layouts: 5.59 us -> 2.77 us
    ppermute x24 -> x31, waiting for transfers between devices: 124 us -> 45.6 us  [exchange(): lax.ppermute(x, axis, [(i, i ^ by) for i in range(lax.axis_size(axis))])]
    ppermute x24 -> x31, starting transfers between devices: 20.4 us -> 39 us  [exchange(): lax.ppermute(x, axis, [(i, i ^ by) for i in range(lax.axis_size(axis))])]
    ppermute x1, waiting for transfers between devices: 0.01 us -> 5.38 us  [shards(): lax.ppermute(halo, 'context', [(i, i + 1) for i in range(contexts - 1)])]
    concatenate x7 -> x0, other arithmetic: 4.89 us -> none  [the longest x1 1.04 us: shards(): query_grad = jnp.concatenate([dq_low, dq_high], axis=0)]
    pallas_call x3 -> x25, Pallas kernels: 7.52 us -> 11.3 us  [the longest x2 5.89 us: backward(): pl.pallas_call(functools.partial(backward_kernel, kv_width // HEAD_SIZE,...]
    pallas_call x4 -> x6, Pallas kernels: 19 us -> 16 us  [projection(): pl.pallas_call(functools.partial(projection_kernel, peers, blocks, off, l...]
    slice x12 -> x0, local copies, waits for them, and re-layouts: 2.16 us -> none  [the longest x2 1.83 us: shards(): value_window = jnp.concatenate([halo[:, kv_width:], values[:half]], axis=0)]
  transfers between devices with their start and end apart: 26 -> 33, of which waited for: 12 -> 14; matrix products, arithmetic and copies ran while one was open for 4% -> 0% of each run, Pallas kernels for 17% -> 27%
where the time goes in v2:
time: 135 us; the launch traced here: 134 us
  waiting for transfers between devices  51 us (38%)
  starting transfers between devices  43.8 us (32%)
  Pallas kernels  35.8 us (27%)
  local copies, waits for them, and re-layouts  2.77 us (2%)
    ppermute x31, waiting for transfers between devices, exchange(): lax.ppermute(x, axis, [(i, i ^ by) for i in range(lax.axis_size(axis))])  45.6 us
    ppermute x31, starting transfers between devices, exchange(): lax.ppermute(x, axis, [(i, i ^ by) for i in range(lax.axis_size(axis))])  39 us
    pallas_call x6, Pallas kernels, projection(): pl.pallas_call(functools.partial(projection_kernel, peers, blocks, off, l...  16 us
    pallas_call x2, Pallas kernels, forward(): pl.pallas_call(functools.partial(forward_kernel, kv_local, group, first),...  8.46 us
    pallas_call x2, Pallas kernels, backward(): pl.pallas_call(functools.partial(backward_kernel, kv_width // HEAD_SIZE,...  5.89 us
    ppermute x1, waiting for transfers between devices, shards(): lax.ppermute(halo, 'context', [(i, i + 1) for i in range(contexts - 1)])  5.38 us
    ppermute x1, starting transfers between devices, shards(): lax.ppermute(halo, 'context', [(i, i + 1) for i in range(contexts - 1)])  3.43 us
    unnamed x17, local copies, waits for them, and re-layouts  2.77 us
  transfers between devices with their start and end apart: 33, of which 14 were waited for; matrix products, arithmetic and copies ran while one was open for 0% of the time, Pallas kernels for 27%

profile of v2, /device:TPU:0, one launch (start us, length us, event | category | flops | bytes accessed | tf_op | source)
XLA Modules:
  0.0 134.4 jit_solution(14996188525658984965)
XLA Ops:
  1.2 1.9 %copy-done.4 = bf16[256,5376]{1,0:T(8,128)(2,1)S(1)} copy-done((bf16[256,5376]{1,0:T(8,128)(2,1)S(1)}, bf16[256,5376]{1,0:T(8,128)(2,1)}, u32[]{:S(2)}) %copy-start.4) | copy-done | bytes 2752536
  4.2 2.7 %collective-permute-start.4 = (bf16[256,1280]{1,0:T(8,128)(2,1)S(1)}, bf16[256,1280]{1,0:T(8,128)(2,1)S(1)}, u32[]{:S(2)}, u32[]{:S(2)}) collective-permute-start(bf16[256,1280]{1,0:T(8,128)(2,1)S(1)} %get-tuple-element.119.refs_0_), channel_id=1, source_target_pairs={{0,2},{1,3},{2,0},{3,1},{4,6},{5,7},{6,4},{7,5},{8,10},{9,11},{10,... | collective-permute-start | bytes 1966088 | tf_op jit(solution)/shard_map/ppermute | solution.py:399
  6.9 3.4 %collective-permute-start.5 = (bf16[2,512,256]{2,1,0:T(8,128)(2,1)S(1)}, bf16[2,512,256]{2,1,0:T(8,128)(2,1)S(1)}, u32[]{:S(2)}, u32[]{:S(2)}) collective-permute-start(bf16[2,512,256]{2,1,0:T(8,128)(2,1)S(1)} %pack_halo.1), channel_id=1, source_target_pairs={{0,4},{4,8},{8,12},{12,16},{16,20},{20,24},{24,28},{1,5},{5,9},{9,... | collective-permute-start | bytes 1572872 | tf_op jit(solution)/shard_map/ppermute | solution.py:419
  10.9 4.2 %attention_forward_second.1 = (bf16[512,512]{1,0:T(8,128)(2,1)S(1)}, bf16[2,2,2,256,768]{4,3,2,1,0:T(8,128)(2,1)S(1)}) custom-call(bf16[1024,512]{1,0:T(8,128)(2,1)S(1)} %copy-done.1, bf16[1024,256]{1,0:T(8,128)(2,1)S(1)} %copy-done.2, bf16[1024,256]{1,0:T(8,128)(2,1)S(1)} %copy-done.3), custom_call_target="tpu_custom_call" | custom-call | tf_op jit(solution)/shard_map/attention_forward_second/pallas_call | solution.py:154
  16.3 5.4 %collective-permute-done.5.refs_3_.refs_6_ = bf16[2,512,256]{2,1,0:T(8,128)(2,1)S(1)} collective-permute-done((bf16[2,512,256]{2,1,0:T(8,128)(2,1)S(1)}, bf16[2,512,256]{2,1,0:T(8,128)(2,1)S(1)}, u32[]{:S(2)}, u32[]{:S(2)}) %collective-permute-start.5) | collective-permute-done | bytes 524320 | tf_op jit(solution)/shard_map/ppermute | solution.py:419
  21.7 4.2 %attention_forward_first.1 = (bf16[512,512]{1,0:T(8,128)(2,1)S(1)}, bf16[2,2,2,256,768]{4,3,2,1,0:T(8,128)(2,1)S(1)}) custom-call(bf16[1024,512]{1,0:T(8,128)(2,1)S(1)} %copy-done.1, bf16[1024,256]{1,0:T(8,128)(2,1)S(1)} %copy-done.2, bf16[1024,256]{1,0:T(8,128)(2,1)S(1)} %copy-done.3, bf16[2,512,256]{2,1,0:T(8,128)(2,1)S(1)} %collective-permute-done.5.refs_3_.refs_6_), custom_call_target="tpu_custom_call" | custom-call | tf_op jit(solution)/shard_map/attention_forward_first/pallas_call | solution.py:154
  26.6 8.5 %collective-permute-done.3.refs_2_ = bf16[256,1152]{1,0:T(8,128)(2,1)S(1)} collective-permute-done((bf16[256,1152]{1,0:T(8,128)(2,1)S(1)}, bf16[256,1152]{1,0:T(8,128)(2,1)S(1)}, u32[]{:S(2)}, u32[]{:S(2)}) %collective-permute-start.3) | collective-permute-done | bytes 589856 | tf_op jit(solution)/shard_map/ppermute | solution.py:399
  35.1 3.6 %projection.6 = (f32[4,256,512]{2,1,0:T(8,128)S(1)}, bf16[4,160,512]{2,1,0:T(8,128)(2,1)S(1)}, bf16[4,160,512]{2,1,0:T(8,128)(2,1)S(1)}) custom-call(bf16[256,1280]{1,0:T(8,128)(2,1)S(1)} %get-tuple-element.119.refs_0_, bf16[256,1280]{1,0:T(8,128)(2,1)S(1)} %get-tuple-element.126.refs_1_, bf16[256,1280]{1,0:T(8,128)(2,1)S(1)} %collective-permute-done.4.refs_2_, ...), custom_call_target="tpu_custom_call" | custom-call | tf_op jit(solution)/shard_map/projection/pallas_call | solution.py:367
  38.6 2.0 %collective-permute-start.9 = (bf16[4,160,512]{2,1,0:T(8,128)(2,1)S(1)}, bf16[4,160,512]{2,1,0:T(8,128)(2,1)S(1)}, u32[]{:S(2)}, u32[]{:S(2)}) collective-permute-start(bf16[4,160,512]{2,1,0:T(8,128)(2,1)S(1)} %get-tuple-element.135), channel_id=1, source_target_pairs={{0,4},{4,0},{8,12},{12,8},{16,20},{20,16},{24,28},{28,24},{1,5},{5... | collective-permute-start | bytes 1966088 | tf_op jit(solution)/shard_map/ppermute | solution.py:399
  42.2 4.1 %collective-permute-done.2.refs_2_ = bf16[256,1024]{1,0:T(8,128)(2,1)S(1)} collective-permute-done((bf16[256,1024]{1,0:T(8,128)(2,1)S(1)}, bf16[256,1024]{1,0:T(8,128)(2,1)S(1)}, u32[]{:S(2)}, u32[]{:S(2)}) %collective-permute-start.2) | collective-permute-done | bytes 524320 | tf_op jit(solution)/shard_map/ppermute | solution.py:399
  46.3 3.2 %projection.7 = (f32[4,256,512]{2,1,0:T(8,128)S(1)}, bf16[4,144,512]{2,1,0:T(8,128)(2,1)S(1)}, bf16[4,144,512]{2,1,0:T(8,128)(2,1)S(1)}) custom-call(bf16[256,1152]{1,0:T(8,128)(2,1)S(1)} %get-tuple-element.116.refs_0_, bf16[256,1152]{1,0:T(8,128)(2,1)S(1)} %get-tuple-element.130.refs_1_, bf16[256,1152]{1,0:T(8,128)(2,1)S(1)} %collective-permute-done.3.refs_2_, ...), custom_call_target="tpu_custom_call" | custom-call | tf_op jit(solution)/shard_map/projection/pallas_call | solution.py:367
  49.5 2.0 %collective-permute-start.8 = (bf16[4,144,512]{2,1,0:T(8,128)(2,1)S(1)}, bf16[4,144,512]{2,1,0:T(8,128)(2,1)S(1)}, u32[]{:S(2)}, u32[]{:S(2)}) collective-permute-start(bf16[4,144,512]{2,1,0:T(8,128)(2,1)S(1)} %get-tuple-element.133), channel_id=1, source_target_pairs={{0,4},{4,0},{8,12},{12,8},{16,20},{20,16},{24,28},{28,24},{1,5},{5... | collective-permute-start | bytes 1769480 | tf_op jit(solution)/shard_map/ppermute | solution.py:399
  51.6 4.7 %collective-permute-done.9.refs_0_ = bf16[4,160,512]{2,1,0:T(8,128)(2,1)S(1)} collective-permute-done((bf16[4,160,512]{2,1,0:T(8,128)(2,1)S(1)}, bf16[4,160,512]{2,1,0:T(8,128)(2,1)S(1)}, u32[]{:S(2)}, u32[]{:S(2)}) %collective-permute-start.9) | collective-permute-done | bytes 655392 | tf_op jit(solution)/shard_map/ppermute | solution.py:399
  56.5 2.1 %collective-permute-start.10 = (bf16[2,160,512]{2,1,0:T(8,128)(2,1)S(1)}, bf16[2,160,512]{2,1,0:T(8,128)(2,1)S(1)}, u32[]{:S(2)}, u32[]{:S(2)}) collective-permute-start(bf16[2,160,512]{2,1,0:T(8,128)(2,1)S(1)} %get-tuple-element.139), channel_id=1, source_target_pairs={{0,8},{4,12},{8,0},{12,4},{16,24},{20,28},{24,16},{28,20},{1,9},{5... | collective-permute-start | bytes 983048 | tf_op jit(solution)/shard_map/ppermute | solution.py:399
  60.1 2.8 %projection.8 = (f32[4,256,512]{2,1,0:T(8,128)S(1)}, bf16[4,128,512]{2,1,0:T(8,128)(2,1)S(1)}, bf16[4,128,512]{2,1,0:T(8,128)(2,1)S(1)}) custom-call(bf16[256,1024]{1,0:T(8,128)(2,1)S(1)} %get-tuple-element.118.refs_0_, bf16[256,1024]{1,0:T(8,128)(2,1)S(1)} %get-tuple-element.142.refs_1_, bf16[256,1024]{1,0:T(8,128)(2,1)S(1)} %collective-permute-done.2.refs_2_, ...), custom_call_target="tpu_custom_call" | custom-call | tf_op jit(solution)/shard_map/projection/pallas_call | solution.py:367
  64.5 2.4 %collective-permute-done.10.refs_0_ = bf16[2,160,512]{2,1,0:T(8,128)(2,1)S(1)} collective-permute-done((bf16[2,160,512]{2,1,0:T(8,128)(2,1)S(1)}, bf16[2,160,512]{2,1,0:T(8,128)(2,1)S(1)}, u32[]{:S(2)}, u32[]{:S(2)}) %collective-permute-start.10) | collective-permute-done | bytes 327712 | tf_op jit(solution)/shard_map/ppermute | solution.py:399
  67.0 1.9 %collective-permute-done.8.refs_0_ = bf16[4,144,512]{2,1,0:T(8,128)(2,1)S(1)} collective-permute-done((bf16[4,144,512]{2,1,0:T(8,128)(2,1)S(1)}, bf16[4,144,512]{2,1,0:T(8,128)(2,1)S(1)}, u32[]{:S(2)}, u32[]{:S(2)}) %collective-permute-start.8) | collective-permute-done | bytes 589856 | tf_op jit(solution)/shard_map/ppermute | solution.py:399
  69.0 2.1 %collective-permute-start.16 = (bf16[2,144,512]{2,1,0:T(8,128)(2,1)S(1)}, bf16[2,144,512]{2,1,0:T(8,128)(2,1)S(1)}, u32[]{:S(2)}, u32[]{:S(2)}) collective-permute-start(bf16[2,144,512]{2,1,0:T(8,128)(2,1)S(1)} %get-tuple-element.148), channel_id=1, source_target_pairs={{0,8},{4,12},{8,0},{12,4},{16,24},{20,28},{24,16},{28,20},{1,9},{5... | collective-permute-start | bytes 884744 | tf_op jit(solution)/shard_map/ppermute | solution.py:399
  71.1 2.6 %collective-permute-start.17 = (bf16[1,160,512]{2,1,0:T(8,128)(2,1)S(1)}, bf16[1,160,512]{2,1,0:T(8,128)(2,1)S(1)}, u32[]{:S(2)}, u32[]{:S(2)}) collective-permute-start(bf16[1,160,512]{2,1,0:T(8,128)(2,1)S(1)} %get-tuple-element.146), channel_id=1, source_target_pairs={{0,16},{4,20},{8,24},{12,28},{16,0},{20,4},{24,8},{28,12},{1,17},{... | collective-permute-start | bytes 491528 | tf_op jit(solution)/shard_map/ppermute | solution.py:399
  73.7 2.7 %projection.9 = (f32[4,256,512]{2,1,0:T(8,128)S(1)}, bf16[4,112,512]{2,1,0:T(8,128)(2,1)S(1)}, bf16[4,112,512]{2,1,0:T(8,128)(2,1)S(1)}) custom-call(bf16[256,896]{1,0:T(8,128)(2,1)S(1)} %get-tuple-element.113.refs_0_, bf16[256,896]{1,0:T(8,128)(2,1)S(1)} %get-tuple-element.150.refs_1_, bf16[256,896]{1,0:T(8,128)(2,1)S(1)} %collective-permute-done.11.refs_2_, ...), custom_call_target="tpu_custom_call" | custom-call | tf_op jit(solution)/shard_map/projection/pallas_call | solution.py:367
  78.0 2.0 %collective-permute-done.17.refs_0_ = bf16[1,160,512]{2,1,0:T(8,128)(2,1)S(1)} collective-permute-done((bf16[1,160,512]{2,1,0:T(8,128)(2,1)S(1)}, bf16[1,160,512]{2,1,0:T(8,128)(2,1)S(1)}, u32[]{:S(2)}, u32[]{:S(2)}) %collective-permute-start.17) | collective-permute-done | bytes 163872 | tf_op jit(solution)/shard_map/ppermute | solution.py:399
  81.8 3.5 %collective-permute-start.18 = (bf16[2,128,512]{2,1,0:T(8,128)(2,1)S(1)}, bf16[2,128,512]{2,1,0:T(8,128)(2,1)S(1)}, u32[]{:S(2)}, u32[]{:S(2)}) collective-permute-start(bf16[2,128,512]{2,1,0:T(8,128)(2,1)S(1)} %get-tuple-element.164), channel_id=1, source_target_pairs={{0,8},{4,12},{8,0},{12,4},{16,24},{20,28},{24,16},{28,20},{1,9},{5... | collective-permute-start | bytes 786440 | tf_op jit(solution)/shard_map/ppermute | solution.py:399
  85.7 2.3 %projection.10 = (f32[4,256,512]{2,1,0:T(8,128)S(1)}, bf16[4,80,512]{2,1,0:T(8,128)(2,1)S(1)}, bf16[4,80,512]{2,1,0:T(8,128)(2,1)S(1)}) custom-call(bf16[256,640]{1,0:T(8,128)(2,1)S(1)} %get-tuple-element.115.refs_0_, bf16[256,640]{1,0:T(8,128)(2,1)S(1)} %get-tuple-element.168.refs_1_, bf16[256,640]{1,0:T(8,128)(2,1)S(1)} %collective-permute-done.1.refs_2_, ...), custom_call_target="tpu_custom_call" | custom-call | tf_op jit(solution)/shard_map/projection/pallas_call | solution.py:367
  89.5 2.1 %collective-permute-done.19.refs_0_ = bf16[1,144,512]{2,1,0:T(8,128)(2,1)S(1)} collective-permute-done((bf16[1,144,512]{2,1,0:T(8,128)(2,1)S(1)}, bf16[1,144,512]{2,1,0:T(8,128)(2,1)S(1)}, u32[]{:S(2)}, u32[]{:S(2)}) %collective-permute-start.19) | collective-permute-done | bytes 147488 | tf_op jit(solution)/shard_map/ppermute | solution.py:399
  92.6 1.8 %collective-permute-start.25 = (bf16[2,112,512]{2,1,0:T(8,128)(2,1)S(1)}, bf16[2,112,512]{2,1,0:T(8,128)(2,1)S(1)}, u32[]{:S(2)}, u32[]{:S(2)}) collective-permute-start(bf16[2,112,512]{2,1,0:T(8,128)(2,1)S(1)} %get-tuple-element.175), channel_id=1, source_target_pairs={{0,8},{4,12},{8,0},{12,4},{16,24},{20,28},{24,16},{28,20},{1,9},{5... | collective-permute-start | bytes 688136 | tf_op jit(solution)/shard_map/ppermute | solution.py:399
  97.3 2.9 %attention_backward_first.1 = (bf16[512,512]{1,0:T(8,128)(2,1)S(1)}, bf16[2,512,256]{2,1,0:T(8,128)(2,1)S(1)}, f32[2,512,256]{2,1,0:T(8,128)S(1)}) custom-call(bf16[1024,512]{1,0:T(8,128)(2,1)S(1)} %copy-done.1, bf16[1024,256]{1,0:T(8,128)(2,1)S(1)} %copy-done.2, bf16[1024,256]{1,0:T(8,128)(2,1)S(1)} %copy-done.3, bf16[1024,512]{1,0:T(8,128)(2,1)S(1)} %bitcast.8, ...), custom_call_target="tpu_custom_call" | custom-call | tf_op jit(solution)/shard_map/attention_backward_first/pallas_call | solution.py:224
  101.6 2.7 %collective-permute-start.30 = (bf16[4,48,512]{2,1,0:T(8,128)(2,1)S(1)}, bf16[4,48,512]{2,1,0:T(8,128)(2,1)S(1)}, u32[]{:S(2)}, u32[]{:S(2)}) collective-permute-start(bf16[4,48,512]{2,1,0:T(8,128)(2,1)S(1)} %get-tuple-element.205), channel_id=1, source_target_pairs={{0,4},{4,0},{8,12},{12,8},{16,20},{20,16},{24,28},{28,24},{1,5},{5... | collective-permute-start | bytes 589832 | tf_op jit(solution)/shard_map/ppermute | solution.py:399
  104.3 2.9 %attention_backward_second.1 = (bf16[512,512]{1,0:T(8,128)(2,1)S(1)}, bf16[2,512,256]{2,1,0:T(8,128)(2,1)S(1)}, f32[2,512,256]{2,1,0:T(8,128)S(1)}) custom-call(bf16[1024,512]{1,0:T(8,128)(2,1)S(1)} %copy-done.1, bf16[1024,256]{1,0:T(8,128)(2,1)S(1)} %copy-done.2, bf16[1024,256]{1,0:T(8,128)(2,1)S(1)} %copy-done.3, bf16[1024,512]{1,0:T(8,128)(2,1)S(1)} %bitcast.9, ...), custom_call_target="tpu_custom_call" | custom-call | tf_op jit(solution)/shard_map/attention_backward_second/pallas_call | solution.py:224
  110.9 7.8 %collective-permute-done.26.refs_0_ = bf16[1,112,512]{2,1,0:T(8,128)(2,1)S(1)} collective-permute-done((bf16[1,112,512]{2,1,0:T(8,128)(2,1)S(1)}, bf16[1,112,512]{2,1,0:T(8,128)(2,1)S(1)}, u32[]{:S(2)}, u32[]{:S(2)}) %collective-permute-start.26) | collective-permute-done | bytes 114720 | tf_op jit(solution)/shard_map/ppermute | solution.py:399
  118.7 2.5 %collective-permute-done.28.refs_0_ = bf16[2,80,512]{2,1,0:T(8,128)(2,1)S(1)} collective-permute-done((bf16[2,80,512]{2,1,0:T(8,128)(2,1)S(1)}, bf16[2,80,512]{2,1,0:T(8,128)(2,1)S(1)}, u32[]{:S(2)}, u32[]{:S(2)}) %collective-permute-start.28) | collective-permute-done | bytes 163872 | tf_op jit(solution)/shard_map/ppermute | solution.py:399
  122.6 5.6 %collective-permute-done.29.refs_0_ = bf16[1,80,512]{2,1,0:T(8,128)(2,1)S(1)} collective-permute-done((bf16[1,80,512]{2,1,0:T(8,128)(2,1)S(1)}, bf16[1,80,512]{2,1,0:T(8,128)(2,1)S(1)}, u32[]{:S(2)}, u32[]{:S(2)}) %collective-permute-start.29) | collective-permute-done | bytes 81952 | tf_op jit(solution)/shard_map/ppermute | solution.py:399
  130.6 2.9 %collective-permute-done.32.refs_0_ = bf16[1,48,512]{2,1,0:T(8,128)(2,1)S(1)} collective-permute-done((bf16[1,48,512]{2,1,0:T(8,128)(2,1)S(1)}, bf16[1,48,512]{2,1,0:T(8,128)(2,1)S(1)}, u32[]{:S(2)}, u32[]{:S(2)}) %collective-permute-start.32) | collective-permute-done | bytes 49184 | tf_op jit(solution)/shard_map/ppermute | solution.py:399
  (85 shorter events, 27.7 us)
Async XLA Ops:
  0.7 14.5 %collective-permute-start = (bf16[256,5376]{1,0:T(8,128)(2,1)}, bf16[256,5376]{1,0:T(8,128)(2,1)S(1)}, u32[]{:S(2)}, u32[]{:S(2)}) collective-permute-start(bf16[256,5376]{1,0:T(8,128)(2,1)} %og_ref.1), channel_id=1, source_target_pairs={{0,1},{1,0},{2,3},{3,2},{4,5},{5,4},{6,7},{7,6},{8,9},{9,8},{10,11... | collective-permute-start | bytes 8257544 | tf_op jit(solution)/shard_map/ppermute | solution.py:399
  4.2 21.7 %collective-permute-start.4 = (bf16[256,1280]{1,0:T(8,128)(2,1)S(1)}, bf16[256,1280]{1,0:T(8,128)(2,1)S(1)}, u32[]{:S(2)}, u32[]{:S(2)}) collective-permute-start(bf16[256,1280]{1,0:T(8,128)(2,1)S(1)} %get-tuple-element.119.refs_0_), channel_id=1, source_target_pairs={{0,2},{1,3},{2,0},{3,1},{4,6},{5,7},{6,4},{7,5},{8,10},{9,11},{10,... | collective-permute-start | bytes 1966088 | tf_op jit(solution)/shard_map/ppermute | solution.py:399
  6.9 14.8 %collective-permute-start.5 = (bf16[2,512,256]{2,1,0:T(8,128)(2,1)S(1)}, bf16[2,512,256]{2,1,0:T(8,128)(2,1)S(1)}, u32[]{:S(2)}, u32[]{:S(2)}) collective-permute-start(bf16[2,512,256]{2,1,0:T(8,128)(2,1)S(1)} %pack_halo.1), channel_id=1, source_target_pairs={{0,4},{4,8},{8,12},{12,16},{16,20},{20,24},{24,28},{1,5},{5,9},{9,... | collective-permute-start | bytes 1572872 | tf_op jit(solution)/shard_map/ppermute | solution.py:419
  10.3 24.7 %collective-permute-start.3 = (bf16[256,1152]{1,0:T(8,128)(2,1)S(1)}, bf16[256,1152]{1,0:T(8,128)(2,1)S(1)}, u32[]{:S(2)}, u32[]{:S(2)}) collective-permute-start(bf16[256,1152]{1,0:T(8,128)(2,1)S(1)} %get-tuple-element.116.refs_0_), channel_id=1, source_target_pairs={{0,2},{1,3},{2,0},{3,1},{4,6},{5,7},{6,4},{7,5},{8,10},{9,11},{10,... | collective-permute-start | bytes 1769480 | tf_op jit(solution)/shard_map/ppermute | solution.py:399
  26.0 9.1 %collective-permute-start.6 = (bf16[256,1280]{1,0:T(8,128)(2,1)S(1)}, bf16[256,1280]{1,0:T(8,128)(2,1)S(1)}, u32[]{:S(2)}, u32[]{:S(2)}) collective-permute-start(bf16[256,1280]{1,0:T(8,128)(2,1)S(1)} %collective-permute-done.4.refs_2_), channel_id=1, source_target_pairs={{0,1},{1,0},{2,3},{3,2},{4,5},{5,4},{6,7},{7,6},{8,9},{9,8},{10,11... | collective-permute-start | bytes 1966088 | tf_op jit(solution)/shard_map/ppermute | solution.py:399
  26.0 20.3 %collective-permute-start.2 = (bf16[256,1024]{1,0:T(8,128)(2,1)S(1)}, bf16[256,1024]{1,0:T(8,128)(2,1)S(1)}, u32[]{:S(2)}, u32[]{:S(2)}) collective-permute-start(bf16[256,1024]{1,0:T(8,128)(2,1)S(1)} %get-tuple-element.118.refs_0_), channel_id=1, source_target_pairs={{0,2},{1,3},{2,0},{3,1},{4,6},{5,7},{6,4},{7,5},{8,10},{9,11},{10,... | collective-permute-start | bytes 1572872 | tf_op jit(solution)/shard_map/ppermute | solution.py:399
  35.1 11.2 %collective-permute-start.7 = (bf16[256,1152]{1,0:T(8,128)(2,1)S(1)}, bf16[256,1152]{1,0:T(8,128)(2,1)S(1)}, u32[]{:S(2)}, u32[]{:S(2)}) collective-permute-start(bf16[256,1152]{1,0:T(8,128)(2,1)S(1)} %collective-permute-done.3.refs_2_), channel_id=1, source_target_pairs={{0,1},{1,0},{2,3},{3,2},{4,5},{5,4},{6,7},{7,6},{8,9},{9,8},{10,11... | collective-permute-start | bytes 1769480 | tf_op jit(solution)/shard_map/ppermute | solution.py:399
  38.6 17.6 %collective-permute-start.9 = (bf16[4,160,512]{2,1,0:T(8,128)(2,1)S(1)}, bf16[4,160,512]{2,1,0:T(8,128)(2,1)S(1)}, u32[]{:S(2)}, u32[]{:S(2)}) collective-permute-start(bf16[4,160,512]{2,1,0:T(8,128)(2,1)S(1)} %get-tuple-element.135), channel_id=1, source_target_pairs={{0,4},{4,0},{8,12},{12,8},{16,20},{20,16},{24,28},{28,24},{1,5},{5... | collective-permute-start | bytes 1966088 | tf_op jit(solution)/shard_map/ppermute | solution.py:399
  40.7 15.7 %collective-permute-start.11 = (bf16[256,896]{1,0:T(8,128)(2,1)S(1)}, bf16[256,896]{1,0:T(8,128)(2,1)S(1)}, u32[]{:S(2)}, u32[]{:S(2)}) collective-permute-start(bf16[256,896]{1,0:T(8,128)(2,1)S(1)} %get-tuple-element.113.refs_0_), channel_id=1, source_target_pairs={{0,2},{1,3},{2,0},{3,1},{4,6},{5,7},{6,4},{7,5},{8,10},{9,11},{10,... | collective-permute-start | bytes 1376264 | tf_op jit(solution)/shard_map/ppermute | solution.py:399
  46.3 13.8 %collective-permute-start.12 = (bf16[256,1024]{1,0:T(8,128)(2,1)S(1)}, bf16[256,1024]{1,0:T(8,128)(2,1)S(1)}, u32[]{:S(2)}, u32[]{:S(2)}) collective-permute-start(bf16[256,1024]{1,0:T(8,128)(2,1)S(1)} %collective-permute-done.2.refs_2_), channel_id=1, source_target_pairs={{0,1},{1,0},{2,3},{3,2},{4,5},{5,4},{6,7},{7,6},{8,9},{9,8},{10,11... | collective-permute-start | bytes 1572872 | tf_op jit(solution)/shard_map/ppermute | solution.py:399
  49.5 19.3 %collective-permute-start.8 = (bf16[4,144,512]{2,1,0:T(8,128)(2,1)S(1)}, bf16[4,144,512]{2,1,0:T(8,128)(2,1)S(1)}, u32[]{:S(2)}, u32[]{:S(2)}) collective-permute-start(bf16[4,144,512]{2,1,0:T(8,128)(2,1)S(1)} %get-tuple-element.133), channel_id=1, source_target_pairs={{0,4},{4,0},{8,12},{12,8},{16,20},{20,16},{24,28},{28,24},{1,5},{5... | collective-permute-start | bytes 1769480 | tf_op jit(solution)/shard_map/ppermute | solution.py:399
  56.4 17.3 %collective-permute-start.13 = (bf16[256,896]{1,0:T(8,128)(2,1)S(1)}, bf16[256,896]{1,0:T(8,128)(2,1)S(1)}, u32[]{:S(2)}, u32[]{:S(2)}) collective-permute-start(bf16[256,896]{1,0:T(8,128)(2,1)S(1)} %collective-permute-done.11.refs_2_), channel_id=1, source_target_pairs={{0,1},{1,0},{2,3},{3,2},{4,5},{5,4},{6,7},{7,6},{8,9},{9,8},{10,11... | collective-permute-start | bytes 1376264 | tf_op jit(solution)/shard_map/ppermute | solution.py:399
  56.5 10.4 %collective-permute-start.10 = (bf16[2,160,512]{2,1,0:T(8,128)(2,1)S(1)}, bf16[2,160,512]{2,1,0:T(8,128)(2,1)S(1)}, u32[]{:S(2)}, u32[]{:S(2)}) collective-permute-start(bf16[2,160,512]{2,1,0:T(8,128)(2,1)S(1)} %get-tuple-element.139), channel_id=1, source_target_pairs={{0,8},{4,12},{8,0},{12,4},{16,24},{20,28},{24,16},{28,20},{1,9},{5... | collective-permute-start | bytes 983048 | tf_op jit(solution)/shard_map/ppermute | solution.py:399
  58.6 15.1 %collective-permute-start.1 = (bf16[256,640]{1,0:T(8,128)(2,1)S(1)}, bf16[256,640]{1,0:T(8,128)(2,1)S(1)}, u32[]{:S(2)}, u32[]{:S(2)}) collective-permute-start(bf16[256,640]{1,0:T(8,128)(2,1)S(1)} %get-tuple-element.115.refs_0_), channel_id=1, source_target_pairs={{0,2},{1,3},{2,0},{3,1},{4,6},{5,7},{6,4},{7,5},{8,10},{9,11},{10,... | collective-permute-start | bytes 983048 | tf_op jit(solution)/shard_map/ppermute | solution.py:399
  62.9 18.7 %collective-permute-start.15 = (bf16[4,128,512]{2,1,0:T(8,128)(2,1)S(1)}, bf16[4,128,512]{2,1,0:T(8,128)(2,1)S(1)}, u32[]{:S(2)}, u32[]{:S(2)}) collective-permute-start(bf16[4,128,512]{2,1,0:T(8,128)(2,1)S(1)} %get-tuple-element.155), channel_id=1, source_target_pairs={{0,4},{4,0},{8,12},{12,8},{16,20},{20,16},{24,28},{28,24},{1,5},{5... | collective-permute-start | bytes 1572872 | tf_op jit(solution)/shard_map/ppermute | solution.py:399
  69.0 12.6 %collective-permute-start.16 = (bf16[2,144,512]{2,1,0:T(8,128)(2,1)S(1)}, bf16[2,144,512]{2,1,0:T(8,128)(2,1)S(1)}, u32[]{:S(2)}, u32[]{:S(2)}) collective-permute-start(bf16[2,144,512]{2,1,0:T(8,128)(2,1)S(1)} %get-tuple-element.148), channel_id=1, source_target_pairs={{0,8},{4,12},{8,0},{12,4},{16,24},{20,28},{24,16},{28,20},{1,9},{5... | collective-permute-start | bytes 884744 | tf_op jit(solution)/shard_map/ppermute | solution.py:399
  71.1 8.9 %collective-permute-start.17 = (bf16[1,160,512]{2,1,0:T(8,128)(2,1)S(1)}, bf16[1,160,512]{2,1,0:T(8,128)(2,1)S(1)}, u32[]{:S(2)}, u32[]{:S(2)}) collective-permute-start(bf16[1,160,512]{2,1,0:T(8,128)(2,1)S(1)} %get-tuple-element.146), channel_id=1, source_target_pairs={{0,16},{4,20},{8,24},{12,28},{16,0},{20,4},{24,8},{28,12},{1,17},{... | collective-permute-start | bytes 491528 | tf_op jit(solution)/shard_map/ppermute | solution.py:399
  76.4 16.0 %collective-permute-start.14 = (bf16[4,112,512]{2,1,0:T(8,128)(2,1)S(1)}, bf16[4,112,512]{2,1,0:T(8,128)(2,1)S(1)}, u32[]{:S(2)}, u32[]{:S(2)}) collective-permute-start(bf16[4,112,512]{2,1,0:T(8,128)(2,1)S(1)} %get-tuple-element.153), channel_id=1, source_target_pairs={{0,4},{4,0},{8,12},{12,8},{16,20},{20,16},{24,28},{28,24},{1,5},{5... | collective-permute-start | bytes 1376264 | tf_op jit(solution)/shard_map/ppermute | solution.py:399
  78.0 7.7 %collective-permute-start.21 = (bf16[256,640]{1,0:T(8,128)(2,1)S(1)}, bf16[256,640]{1,0:T(8,128)(2,1)S(1)}, u32[]{:S(2)}, u32[]{:S(2)}) collective-permute-start(bf16[256,640]{1,0:T(8,128)(2,1)S(1)} %collective-permute-done.1.refs_2_), channel_id=1, source_target_pairs={{0,1},{1,0},{2,3},{3,2},{4,5},{5,4},{6,7},{7,6},{8,9},{9,8},{10,11... | collective-permute-start | bytes 983048 | tf_op jit(solution)/shard_map/ppermute | solution.py:399
  80.0 5.7 %collective-permute-start.20 = (bf16[256,384]{1,0:T(8,128)(2,1)S(1)}, bf16[256,384]{1,0:T(8,128)(2,1)S(1)}, u32[]{:S(2)}, u32[]{:S(2)}) collective-permute-start(bf16[256,384]{1,0:T(8,128)(2,1)S(1)} %get-tuple-element.109.refs_0_), channel_id=1, source_target_pairs={{0,2},{1,3},{2,0},{3,1},{4,6},{5,7},{6,4},{7,5},{8,10},{9,11},{10,... | collective-permute-start | bytes 589832 | tf_op jit(solution)/shard_map/ppermute | solution.py:399
  81.8 10.6 %collective-permute-start.18 = (bf16[2,128,512]{2,1,0:T(8,128)(2,1)S(1)}, bf16[2,128,512]{2,1,0:T(8,128)(2,1)S(1)}, u32[]{:S(2)}, u32[]{:S(2)}) collective-permute-start(bf16[2,128,512]{2,1,0:T(8,128)(2,1)S(1)} %get-tuple-element.164), channel_id=1, source_target_pairs={{0,8},{4,12},{8,0},{12,4},{16,24},{20,28},{24,16},{28,20},{1,9},{5... | collective-permute-start | bytes 786440 | tf_op jit(solution)/shard_map/ppermute | solution.py:399
  85.3 6.3 %collective-permute-start.19 = (bf16[1,144,512]{2,1,0:T(8,128)(2,1)S(1)}, bf16[1,144,512]{2,1,0:T(8,128)(2,1)S(1)}, u32[]{:S(2)}, u32[]{:S(2)}) collective-permute-start(bf16[1,144,512]{2,1,0:T(8,128)(2,1)S(1)} %get-tuple-element.161), channel_id=1, source_target_pairs={{0,16},{4,20},{8,24},{12,28},{16,0},{20,4},{24,8},{28,12},{1,17},{... | collective-permute-start | bytes 442376 | tf_op jit(solution)/shard_map/ppermute | solution.py:399
  88.0 19.4 %collective-permute-start.27 = (bf16[4,80,512]{2,1,0:T(8,128)(2,1)S(1)}, bf16[4,80,512]{2,1,0:T(8,128)(2,1)S(1)}, u32[]{:S(2)}, u32[]{:S(2)}) collective-permute-start(bf16[4,80,512]{2,1,0:T(8,128)(2,1)S(1)} %get-tuple-element.196), channel_id=1, source_target_pairs={{0,4},{4,0},{8,12},{12,8},{16,20},{20,16},{24,28},{28,24},{1,5},{5... | collective-permute-start | bytes 983048 | tf_op jit(solution)/shard_map/ppermute | solution.py:399
  89.5 6.3 %collective-permute-start.22 = (bf16[256,384]{1,0:T(8,128)(2,1)S(1)}, bf16[256,384]{1,0:T(8,128)(2,1)S(1)}, u32[]{:S(2)}, u32[]{:S(2)}) collective-permute-start(bf16[256,384]{1,0:T(8,128)(2,1)S(1)} %collective-permute-done.20.refs_2_), channel_id=1, source_target_pairs={{0,1},{1,0},{2,3},{3,2},{4,5},{5,4},{6,7},{7,6},{8,9},{9,8},{10,11... | collective-permute-start | bytes 589832 | tf_op jit(solution)/shard_map/ppermute | solution.py:399
  92.6 14.7 %collective-permute-start.25 = (bf16[2,112,512]{2,1,0:T(8,128)(2,1)S(1)}, bf16[2,112,512]{2,1,0:T(8,128)(2,1)S(1)}, u32[]{:S(2)}, u32[]{:S(2)}) collective-permute-start(bf16[2,112,512]{2,1,0:T(8,128)(2,1)S(1)} %get-tuple-element.175), channel_id=1, source_target_pairs={{0,8},{4,12},{8,0},{12,4},{16,24},{20,28},{24,16},{28,20},{1,9},{5... | collective-permute-start | bytes 688136 | tf_op jit(solution)/shard_map/ppermute | solution.py:399
  94.3 12.9 %collective-permute-start.24 = (bf16[1,128,512]{2,1,0:T(8,128)(2,1)S(1)}, bf16[1,128,512]{2,1,0:T(8,128)(2,1)S(1)}, u32[]{:S(2)}, u32[]{:S(2)}) collective-permute-start(bf16[1,128,512]{2,1,0:T(8,128)(2,1)S(1)} %get-tuple-element.173), channel_id=1, source_target_pairs={{0,16},{4,20},{8,24},{12,28},{16,0},{20,4},{24,8},{28,12},{1,17},{... | collective-permute-start | bytes 393224 | tf_op jit(solution)/shard_map/ppermute | solution.py:399
  100.3 29.3 %collective-permute-start.23 = (bf16[2,512,256]{2,1,0:T(8,128)(2,1)S(1)}, bf16[2,512,256]{2,1,0:T(8,128)(2,1)S(1)}, u32[]{:S(2)}, u32[]{:S(2)}) collective-permute-start(bf16[2,512,256]{2,1,0:T(8,128)(2,1)S(1)} %get-tuple-element.186), channel_id=1, source_target_pairs={{4,0},{8,4},{12,8},{16,12},{20,16},{24,20},{28,24},{5,1},{9,5},{13... | collective-permute-start | bytes 1572872 | tf_op jit(solution)/shard_map/ppermute | solution.py:478
  101.6 19.8 %collective-permute-start.30 = (bf16[4,48,512]{2,1,0:T(8,128)(2,1)S(1)}, bf16[4,48,512]{2,1,0:T(8,128)(2,1)S(1)}, u32[]{:S(2)}, u32[]{:S(2)}) collective-permute-start(bf16[4,48,512]{2,1,0:T(8,128)(2,1)S(1)} %get-tuple-element.205), channel_id=1, source_target_pairs={{0,4},{4,0},{8,12},{12,8},{16,20},{20,16},{24,28},{28,24},{1,5},{5... | collective-permute-start | bytes 589832 | tf_op jit(solution)/shard_map/ppermute | solution.py:399
  107.4 13.8 %collective-permute-start.28 = (bf16[2,80,512]{2,1,0:T(8,128)(2,1)S(1)}, bf16[2,80,512]{2,1,0:T(8,128)(2,1)S(1)}, u32[]{:S(2)}, u32[]{:S(2)}) collective-permute-start(bf16[2,80,512]{2,1,0:T(8,128)(2,1)S(1)} %get-tuple-element.198), channel_id=1, source_target_pairs={{0,8},{4,12},{8,0},{12,4},{16,24},{20,28},{24,16},{28,20},{1,9},{5... | collective-permute-start | bytes 491528 | tf_op jit(solution)/shard_map/ppermute | solution.py:399
  110.1 8.6 %collective-permute-start.26 = (bf16[1,112,512]{2,1,0:T(8,128)(2,1)S(1)}, bf16[1,112,512]{2,1,0:T(8,128)(2,1)S(1)}, u32[]{:S(2)}, u32[]{:S(2)}) collective-permute-start(bf16[1,112,512]{2,1,0:T(8,128)(2,1)S(1)} %get-tuple-element.194), channel_id=1, source_target_pairs={{0,16},{4,20},{8,24},{12,28},{16,0},{20,4},{24,8},{28,12},{1,17},{... | collective-permute-start | bytes 344072 | tf_op jit(solution)/shard_map/ppermute | solution.py:399
  121.3 7.0 %collective-permute-start.29 = (bf16[1,80,512]{2,1,0:T(8,128)(2,1)S(1)}, bf16[1,80,512]{2,1,0:T(8,128)(2,1)S(1)}, u32[]{:S(2)}, u32[]{:S(2)}) collective-permute-start(bf16[1,80,512]{2,1,0:T(8,128)(2,1)S(1)} %get-tuple-element.203), channel_id=1, source_target_pairs={{0,16},{4,20},{8,24},{12,28},{16,0},{20,4},{24,8},{28,12},{1,17},{... | collective-permute-start | bytes 245768 | tf_op jit(solution)/shard_map/ppermute | solution.py:399
  121.4 6.8 %collective-permute-start.31 = (bf16[2,48,512]{2,1,0:T(8,128)(2,1)S(1)}, bf16[2,48,512]{2,1,0:T(8,128)(2,1)S(1)}, u32[]{:S(2)}, u32[]{:S(2)}) collective-permute-start(bf16[2,48,512]{2,1,0:T(8,128)(2,1)S(1)} %get-tuple-element.207), channel_id=1, source_target_pairs={{0,8},{4,12},{8,0},{12,4},{16,24},{20,28},{24,16},{28,20},{1,9},{5... | collective-permute-start | bytes 294920 | tf_op jit(solution)/shard_map/ppermute | solution.py:399
  (7 other events, 54.8 us)

commit v3 on v2

--- a/solution.py
+++ b/solution.py
@@ -13,20 +13,12 @@
 LOG2E = 1.4426950408889634
 NEG = -1e30
 TILE = WINDOW_KEYS // 2
-LAGS = (1, 2, 3, 4, 5)
-TAIL_ONE = True
-
-
-def TAIL(item):
-    return (item[0] + item[1], item[0])
-
-
-LENS = (160, 144, 128, 112, 80, 48)
-SWAP = (0, 0, 0, 0, 0, 0)
-PIECES = (1, 1, 1, 1, 1, 1)
-AHEAD = 1
-AHEAD_FROM = 0
-COST = None
+LENS = (144, 144, 128, 112, 80, 64)
+STEPS = (
+    "y0", "y1", "p0", "y2", "p1", "1.0", "y3", "p2", "2.0", "1.1", "y4", "3.0", "p3",
+    "2.1", "1.2", "y5", "p4", "p5", "3.1", "1.3", "2.2", "first", "3.2", "2.3", "1.4",
+    "second", "1.5", "2.4", "3.3", "2.5", "3.4", "3.5",
+)
 F32 = jnp.float32
 BF16 = jnp.bfloat16
 VMEM_LIMIT = 8 * 1024 * 1024
@@ -48,10 +40,6 @@
 
 def params(times=1):
     return pltpu.CompilerParams(vmem_limit_bytes=times * VMEM_LIMIT)
-
-
-def cost(flops, nbytes, trans=0):
-    return COST
 
 
 def prepare_kernel(blocks, blk, lens, og_ref, *refs):
@@ -71,7 +59,6 @@
         in_specs=[vmem()],
         out_specs=[vmem() for _ in lens],
         compiler_params=params(),
-        cost_estimate=cost(0, 4 * rows * width),
         name="gather_columns",
     )(og)
 
@@ -89,7 +76,6 @@
         in_specs=[vmem(), vmem()],
         out_specs=vmem(),
         compiler_params=params(),
-        cost_estimate=cost(0, 8 * WINDOW_KEYS * keys.shape[1]),
         name="pack_halo",
     )(keys, values)
 
@@ -160,7 +146,6 @@
         in_specs=[vmem() for _ in args],
         out_specs=[vmem(), vmem()],
         compiler_params=params(),
-        cost_estimate=cost(16 * WINDOW_KEYS * width * 3 * TILE, 8 * WINDOW_KEYS * width),
         name="attention_forward_first" if first else "attention_forward_second",
     )(*args)
 
@@ -235,7 +220,6 @@
             pltpu.VMEM((HEAD_SIZE, 4 * TILE), F32),
         ],
         compiler_params=params(),
-        cost_estimate=cost(16 * WINDOW_KEYS * width * 3 * TILE, 8 * WINDOW_KEYS * width),
         name="attention_backward_first" if first else "attention_backward_second",
     )(*args)
 
@@ -256,7 +240,6 @@
         in_specs=[vmem()] * 3,
         out_specs=[vmem()] * 2,
         compiler_params=params(),
-        cost_estimate=cost(0, 12 * WINDOW_KEYS * own.shape[2]),
         name="join_gradients",
     )(done, own, got)
 
@@ -274,20 +257,19 @@
         in_specs=[vmem()] * 2,
         out_specs=vmem(),
         compiler_params=params(),
-        cost_estimate=cost(0, 4 * low.shape[0] * low.shape[1]),
         name="join_halves",
     )(low, high)
 
 
-def add_kernel(keep_ref, *refs):
-    count, length = keep_ref.shape[:2]
-    pieces = len(refs) - (1 if count == 1 else 2)
-    got_refs, out_refs = refs[:pieces], refs[pieces:]
-    size = length // pieces
-    for i in range(count):
-        for p, got_ref in enumerate(got_refs):
-            rows = slice(p * size, (p + 1) * size)
-            total = keep_ref[i, rows, :].astype(F32) + got_ref[i].astype(F32)
+def add_kernel(parts, *refs):
+    keep_refs, got_refs, out_refs = refs[:parts], refs[parts : 2 * parts], refs[2 * parts :]
+    at = 0
+    for keep_ref, got_ref in zip(keep_refs, got_refs):
+        count, length = keep_ref.shape[:2]
+        rows = slice(at, at + length)
+        at += length
+        for i in range(count):
+            total = keep_ref[i].astype(F32) + got_ref[i].astype(F32)
             if count == 1:
                 out_refs[0][rows, :] = total.astype(BF16)
             else:
@@ -295,33 +277,31 @@
                 out[i // 2, rows, :] = total.astype(out.dtype)
 
 
-def add(keep, got):
-    count, length, width = keep.shape
+def add(keeps, gots):
+    count, _, width = keeps[0].shape
+    length = sum(keep.shape[1] for keep in keeps)
     if count == 1:
         out_shape = [jax.ShapeDtypeStruct((length, width), BF16)]
     else:
         half = (count // 2, length, width)
         out_shape = [jax.ShapeDtypeStruct(half, F32), jax.ShapeDtypeStruct(half, BF16)]
     return pl.pallas_call(
-        add_kernel,
+        functools.partial(add_kernel, len(keeps)),
         out_shape=out_shape,
-        in_specs=[vmem()] * (1 + len(got)),
+        in_specs=[vmem()] * (2 * len(keeps)),
         out_specs=[vmem() for _ in out_shape],
         compiler_params=params(),
-        cost_estimate=cost(0, 8 * count * length * width),
         name="add_partials",
-    )(keep, *got)
-
-
-def projection_kernel(peers, blocks, off, length, start, last, bits, pieces, *refs):
+    )(*keeps, *gots)
+
+
+def projection_kernel(peers, blocks, off, length, start, last, bits, *refs):
     og_refs = refs[:peers]
     w_ref, low_ref, high_ref = refs[peers : peers + 3]
     refs = refs[peers + 3 :]
     if not start:
         acc_ref, refs = refs[0], refs[1:]
-    out_ref, keep_ref = refs[:2]
-    send_refs = refs[2 : 2 + pieces]
-    w_vmem, attn_all, part, sem = refs[2 + pieces :]
+    out_ref, keep_ref, send_ref, w_vmem, attn_all, part, sem = refs
     copy = pltpu.make_async_copy(w_ref.at[:, pl.ds(off, length), :], w_vmem, sem)
     copy.start()
     mine, context = lax.axis_index("mp"), lax.axis_index("context")
@@ -335,14 +315,12 @@
     for s in range(0, total, step):
         og = jnp.concatenate([og_ref[:, s : s + step] for og_ref in og_refs], axis=0)
         part[s : s + step, :] = dot(og, attn, 0, 0)
-    size = length // pieces
     for i in range(blocks // 2):
         target = sum(bit for k, bit in enumerate(bits[1:]) if i >> k & 1) ^ context
         at = pl.multiple_of(target * length, 8)
         keep_ref[i] = part[pl.ds(at, length), :].astype(keep_ref.dtype)
-        for p, send_ref in enumerate(send_refs):
-            at = pl.multiple_of((target ^ bits[0]) * length + p * size, 8)
-            send_ref[i] = part[pl.ds(at, size), :].astype(BF16)
+        at = pl.multiple_of((target ^ bits[0]) * length, 8)
+        send_ref[i] = part[pl.ds(at, length), :].astype(BF16)
     copy.wait()
     w = w_vmem[...].reshape(total, width)
     for r in range(peers):
@@ -355,26 +333,25 @@
             out_ref[r] = out
 
 
-def projection(ogs, w, low, high, acc, blocks, off, length, last, bits, pieces):
+def projection(ogs, w, low, high, acc, blocks, off, length, last, bits):
     peers = len(ogs)
     rows, total = ogs[0].shape
     width = low.shape[1]
     start = acc is None
     args = [*ogs, w, low, high] + ([] if start else [acc])
     specs = [vmem()] * peers + [hbm()] + [vmem()] * (2 if start else 3)
-    keep = jax.ShapeDtypeStruct((blocks // 2, length, width), BF16)
-    send = jax.ShapeDtypeStruct((blocks // 2, length // pieces, width), BF16)
+    half = jax.ShapeDtypeStruct((blocks // 2, length, width), BF16)
     return pl.pallas_call(
         functools.partial(
-            projection_kernel, peers, blocks, off, length, start, last, bits, pieces
+            projection_kernel, peers, blocks, off, length, start, last, bits
         ),
         out_shape=[
             jax.ShapeDtypeStruct((peers, rows, width), BF16 if last else F32),
-            keep,
-            *[send] * pieces,
+            half,
+            half,
         ],
         in_specs=specs,
-        out_specs=[vmem()] * (2 + pieces),
+        out_specs=[vmem()] * 3,
         scratch_shapes=[
             pltpu.VMEM((blocks, length, width), BF16),
             pltpu.VMEM((peers, rows, width), BF16),
@@ -382,17 +359,18 @@
             pltpu.SemaphoreType.DMA,
         ],
         compiler_params=params(4 if start and last else 1),
-        cost_estimate=cost(4 * peers * rows * total * width, 4 * rows * peers * total),
         name="projection",
     )(*args)
 
 
-def chunk_plan(blk, contexts):
+def plan(blk, contexts):
     bits = [1 << k for k in range(contexts.bit_length() - 1)]
-    if blk != 672:
-        return (blk,), (bits,), (1,)
-    swapped = [bits[1], bits[0], *bits[2:]]
-    return LENS, [swapped if swap else bits for swap in SWAP], PIECES
+    if blk == 672 and contexts == 8:
+        groups = [[[chunk] for chunk in range(len(LENS))]] * len(bits)
+        return LENS, [bits] * len(LENS), groups, STEPS
+    groups = [[[0]]] * len(bits)
+    steps = ["y0", "p0", "first", "second"] + [f"{k + 1}.0" for k in range(len(bits))]
+    return (blk,), [bits], groups, steps
 
 
 def exchange(x, axis, by):
@@ -408,14 +386,14 @@
     contexts = lax.axis_size("context")
     peers = lax.axis_size("mp")
     blk = out_weight.shape[0] // contexts
-    lens, orders, pieces = chunk_plan(blk, contexts)
+    lens, orders, groups, steps = plan(blk, contexts)
     chunks = len(lens)
     weight = out_weight.reshape(contexts, blk, width)
 
+    own = prepare(out_grad, contexts, lens)
+    halo = pack(after(own[0], keys), values)
     sibling = exchange(out_grad, "mp", 1)
-    own = prepare(out_grad, contexts, lens)
     far = [[exchange(og, "mp", by) for by in range(2, peers, 2)] for og in own]
-    halo = pack(after(own[0], keys), values)
     halo = lax.ppermute(halo, "context", [(i, i + 1) for i in range(contexts - 1)])
 
     attn_high, prob_high = forward(queries, keys, values)
@@ -424,70 +402,60 @@
     attn_low, prob_low = forward(queries, keys, values, halo)
     done = attn_low
 
-    pending, reduced = [], [None] * chunks
-
-    def reduce_step(item, done):
-        chunk, stage, keep, got = item
-        got = [after(done, piece) for piece in got]
-        if keep.shape[0] == 1:
-            reduced[chunk] = add(keep, got)[0]
-            return reduced[chunk], None
-        keep, send = add(keep, got)
-        stage += 1
-        return send, (chunk, stage, keep, [exchange(send, "context", orders[chunk][stage])])
-
-    def reduce_round(pending, done):
-        later = []
-        for item in pending:
-            done, item = reduce_step(item, done)
-            if item is not None:
-                later.append(item)
-        return later, done
-
-    def fetch(j, done):
-        theirs = [after(done, og) for og in far[j]]
-        return theirs, [exchange(og, "mp", 1) for og in theirs], theirs[-1]
-
-    fetched = []
-    acc, off = None, 0
-    for j, length in enumerate(lens):
-        want = min(chunks, j + 1 + (AHEAD if j >= AHEAD_FROM else 0))
-        while len(fetched) < want:
-            *item, done = fetch(len(fetched), done)
-            fetched.append(item)
-        theirs, theirs_sibling = fetched[j]
-        parts = [own[j], after(done, siblings[j])]
-        for og, og_sibling in zip(theirs, theirs_sibling):
-            parts += [og, after(done, og_sibling)]
-        acc, keep, *send = projection(
-            parts, weight, attn_low, attn_high, acc, contexts, off, length, j == chunks - 1,
-            orders[j], pieces[j],
-        )
-        done = acc
-        off += length
-        got = [exchange(piece, "context", orders[j][0]) for piece in send]
-        pending.append((j, 0, keep, got))
-        if j < chunks - 1:
-            ready = [item for item in pending if item[0] + LAGS[item[1]] <= j]
-            rest = [item for item in pending if item[0] + LAGS[item[1]] > j]
-            ready, done = reduce_round(ready, done)
-            pending = ready + rest
-
-    dout = acc.reshape(shard, width)
-    dq_low, halo_grad, own_low = backward(queries, keys, values, dout, attn_low, prob_low, halo)
-    halo_grad = lax.ppermute(halo_grad, "context", [(i + 1, i) for i in range(contexts - 1)])
-    dq_high, kv_low, own_high = backward(
-        queries, keys, values, dout, attn_high, prob_high, low=own_low
-    )
-    dq = concat(dq_low, dq_high)
-    done = own_high
-    while pending:
-        pending.sort(key=TAIL)
-        count = 1 if TAIL_ONE else len(pending)
-        ready, done = reduce_round(pending[:count], done)
-        pending = ready + pending[count:]
-    weight_grad = jnp.concatenate(reduced, axis=0)
-    dk, dv = join(kv_low, own_high, halo_grad, shard)
+    stages = len(orders[0])
+    fetched, item, grads = {}, {}, {}
+    acc, offs = None, [sum(lens[:j]) for j in range(chunks)]
+    for step in steps:
+        if step[0] == "y":
+            theirs = [after(done, og) for og in far[int(step[1:])]]
+            fetched[int(step[1:])] = theirs, [exchange(og, "mp", 1) for og in theirs]
+            done = theirs[-1]
+        elif step[0] == "p":
+            j = int(step[1:])
+            parts = [own[j], after(done, siblings[j])]
+            for og, og_sibling in zip(*fetched[j]):
+                parts += [og, after(done, og_sibling)]
+            acc, keep, send = projection(
+                parts, weight, attn_low, attn_high, acc, contexts, offs[j], lens[j],
+                j == chunks - 1, orders[j],
+            )
+            item[0, j] = keep, exchange(send, "context", orders[j][0]), orders[j]
+            done = acc
+        elif step == "first":
+            dout = acc.reshape(shard, width)
+            dq_low, halo_grad, own_low = backward(
+                queries, keys, values, after(done, dout), attn_low, prob_low, halo
+            )
+            pairs = [(i + 1, i) for i in range(contexts - 1)]
+            halo_grad = lax.ppermute(halo_grad, "context", pairs)
+            done = own_low
+        elif step == "second":
+            dq_high, kv_low, own_high = backward(
+                queries, keys, values, after(done, dout), attn_high, prob_high, low=own_low
+            )
+            done = own_high
+        elif step == "halves":
+            dq = concat(after(done, dq_low), dq_high)
+            done = dq
+        elif step == "join":
+            dk, dv = join(kv_low, own_high, after(done, halo_grad), shard)
+            done = dk
+        else:
+            stage, group = [int(n) for n in step.split(".")]
+            members = [item[stage - 1, g] for g in groups[stage - 1][group]]
+            keeps, gots = [m[0] for m in members], [after(done, m[1]) for m in members]
+            order = members[0][2]
+            if stage == stages:
+                item[stage, group] = done = add(keeps, gots)[0]
+            else:
+                keep, done = add(keeps, gots)
+                item[stage, group] = keep, exchange(done, "context", order[stage]), order
+    final = [item[stages, g] for g in range(len(groups[-1]))]
+    weight_grad = final[0] if len(final) == 1 else jnp.concatenate(final, axis=0)
+    if "halves" not in steps:
+        dq = concat(dq_low, dq_high)
+    if "join" not in steps:
+        dk, dv = join(kv_low, own_high, halo_grad, shard)
     return dq, dk, dv, weight_grad
 
 

time: 135 us -> 129 us (0.956)
  waiting for transfers between devices: 51 us -> 42.2 us
  starting transfers between devices: 43.8 us -> 47.3 us
    ppermute x31, waiting for transfers between devices: 45.6 us -> 36.9 us  [exchange(): lax.ppermute(x, axis, [(i, i ^ by) for i in range(lax.axis_size(axis))])]
    ppermute x31, starting transfers between devices: 39 us -> 42.6 us  [exchange(): lax.ppermute(x, axis, [(i, i ^ by) for i in range(lax.axis_size(axis))])]
  transfers between devices with their start and end apart: 33 -> 33, of which waited for: 14 -> 12; matrix products, arithmetic and copies ran while one was open for 0% -> 0% of each run, Pallas kernels for 27% -> 27%
where the time goes in v3:
time: 129 us
  starting transfers between devices  47.3 us (37%)
  waiting for transfers between devices  42.2 us (33%)
  Pallas kernels  36.1 us (28%)
  local copies, waits for them, and re-layouts  1.94 us (2%)
    ppermute x31, starting transfers between devices, exchange(): lax.ppermute(x, axis, [(i, i ^ by) for i in range(lax.axis_size(axis))])  42.6 us
    ppermute x31, waiting for transfers between devices, exchange(): lax.ppermute(x, axis, [(i, i ^ by) for i in range(lax.axis_size(axis))])  36.9 us
    pallas_call x6, Pallas kernels, projection(): pl.pallas_call(functools.partial(projection_kernel, peers, blocks, off, l...  16 us
    pallas_call x2, Pallas kernels, forward(): pl.pallas_call(functools.partial(forward_kernel, kv_local, group, first),...  8.45 us
    pallas_call x2, Pallas kernels, backward(): pl.pallas_call(functools.partial(backward_kernel, kv_width // HEAD_SIZE,...  5.88 us
    ppermute x1, waiting for transfers between devices, shards(): lax.ppermute(halo, 'context', [(i, i + 1) for i in range(contexts - 1)])  5.29 us
    ppermute x1, starting transfers between devices, shards(): lax.ppermute(halo, 'context', [(i, i + 1) for i in range(contexts - 1)])  3.43 us
  transfers between devices with their start and end apart: 33, of which 12 were waited for; matrix products, arithmetic and copies ran while one was open for 0% of the time, Pallas kernels for 27%

profile of v3, /device:TPU:0, one launch (start us, length us, event | category | flops | bytes accessed | tf_op | source)
XLA Modules:
  0.0 128.6 jit_solution(7758123670122361927)
XLA Ops:
  1.2 1.9 %copy-done.4 = bf16[256,5376]{1,0:T(8,128)(2,1)S(1)} copy-done((bf16[256,5376]{1,0:T(8,128)(2,1)S(1)}, bf16[256,5376]{1,0:T(8,128)(2,1)}, u32[]{:S(2)}) %copy-start.4) | copy-done | bytes 2752536
  4.3 2.7 %collective-permute-start.4 = (bf16[256,1152]{1,0:T(8,128)(2,1)S(1)}, bf16[256,1152]{1,0:T(8,128)(2,1)S(1)}, u32[]{:S(2)}, u32[]{:S(2)}) collective-permute-start(bf16[256,1152]{1,0:T(8,128)(2,1)S(1)} %get-tuple-element.120.refs_0_), channel_id=1, source_target_pairs={{0,2},{1,3},{2,0},{3,1},{4,6},{5,7},{6,4},{7,5},{8,10},{9,11},{10,... | collective-permute-start | bytes 1769480 | tf_op jit(solution)/shard_map/ppermute | solution.py:377
  7.0 3.4 %collective-permute-start.5 = (bf16[2,512,256]{2,1,0:T(8,128)(2,1)S(1)}, bf16[2,512,256]{2,1,0:T(8,128)(2,1)S(1)}, u32[]{:S(2)}, u32[]{:S(2)}) collective-permute-start(bf16[2,512,256]{2,1,0:T(8,128)(2,1)S(1)} %pack_halo.1), channel_id=1, source_target_pairs={{0,4},{4,8},{8,12},{12,16},{16,20},{20,24},{24,28},{1,5},{5,9},{9,... | collective-permute-start | bytes 1572872 | tf_op jit(solution)/shard_map/ppermute | solution.py:397
  11.0 4.2 %attention_forward_second.1 = (bf16[512,512]{1,0:T(8,128)(2,1)S(1)}, bf16[2,2,2,256,768]{4,3,2,1,0:T(8,128)(2,1)S(1)}) custom-call(bf16[1024,512]{1,0:T(8,128)(2,1)S(1)} %copy-done.1, bf16[1024,256]{1,0:T(8,128)(2,1)S(1)} %copy-done.2, bf16[1024,256]{1,0:T(8,128)(2,1)S(1)} %copy-done.3), custom_call_target="tpu_custom_call" | custom-call | tf_op jit(solution)/shard_map/attention_forward_second/pallas_call | solution.py:140
  16.5 5.3 %collective-permute-done.5.refs_3_.refs_6_ = bf16[2,512,256]{2,1,0:T(8,128)(2,1)S(1)} collective-permute-done((bf16[2,512,256]{2,1,0:T(8,128)(2,1)S(1)}, bf16[2,512,256]{2,1,0:T(8,128)(2,1)S(1)}, u32[]{:S(2)}, u32[]{:S(2)}) %collective-permute-start.5) | collective-permute-done | bytes 524320 | tf_op jit(solution)/shard_map/ppermute | solution.py:397
  21.8 4.2 %attention_forward_first.1 = (bf16[512,512]{1,0:T(8,128)(2,1)S(1)}, bf16[2,2,2,256,768]{4,3,2,1,0:T(8,128)(2,1)S(1)}) custom-call(bf16[1024,512]{1,0:T(8,128)(2,1)S(1)} %copy-done.1, bf16[1024,256]{1,0:T(8,128)(2,1)S(1)} %copy-done.2, bf16[1024,256]{1,0:T(8,128)(2,1)S(1)} %copy-done.3, bf16[2,512,256]{2,1,0:T(8,128)(2,1)S(1)} %collective-permute-done.5.refs_3_.refs_6_), custom_call_target="tpu_custom_call" | custom-call | tf_op jit(solution)/shard_map/attention_forward_first/pallas_call | solution.py:140
  26.7 7.1 %collective-permute-done.3.refs_2_ = bf16[256,1152]{1,0:T(8,128)(2,1)S(1)} collective-permute-done((bf16[256,1152]{1,0:T(8,128)(2,1)S(1)}, bf16[256,1152]{1,0:T(8,128)(2,1)S(1)}, u32[]{:S(2)}, u32[]{:S(2)}) %collective-permute-start.3) | collective-permute-done | bytes 589856 | tf_op jit(solution)/shard_map/ppermute | solution.py:377
  33.8 3.4 %projection.6 = (f32[4,256,512]{2,1,0:T(8,128)S(1)}, bf16[4,144,512]{2,1,0:T(8,128)(2,1)S(1)}, bf16[4,144,512]{2,1,0:T(8,128)(2,1)S(1)}) custom-call(bf16[256,1152]{1,0:T(8,128)(2,1)S(1)} %get-tuple-element.120.refs_0_, bf16[256,1152]{1,0:T(8,128)(2,1)S(1)} %get-tuple-element.128.refs_1_, bf16[256,1152]{1,0:T(8,128)(2,1)S(1)} %collective-permute-done.4.refs_2_, ...), custom_call_target="tpu_custom_call" | custom-call | tf_op jit(solution)/shard_map/projection/pallas_call | solution.py:344
  37.2 2.0 %collective-permute-start.7 = (bf16[4,144,512]{2,1,0:T(8,128)(2,1)S(1)}, bf16[4,144,512]{2,1,0:T(8,128)(2,1)S(1)}, u32[]{:S(2)}, u32[]{:S(2)}) collective-permute-start(bf16[4,144,512]{2,1,0:T(8,128)(2,1)S(1)} %get-tuple-element.131), channel_id=1, source_target_pairs={{0,4},{4,0},{8,12},{12,8},{16,20},{20,16},{24,28},{28,24},{1,5},{5... | collective-permute-start | bytes 1769480 | tf_op jit(solution)/shard_map/ppermute | solution.py:377
  40.7 4.3 %collective-permute-done.8.refs_2_ = bf16[256,1024]{1,0:T(8,128)(2,1)S(1)} collective-permute-done((bf16[256,1024]{1,0:T(8,128)(2,1)S(1)}, bf16[256,1024]{1,0:T(8,128)(2,1)S(1)}, u32[]{:S(2)}, u32[]{:S(2)}) %collective-permute-start.8) | collective-permute-done | bytes 524320 | tf_op jit(solution)/shard_map/ppermute | solution.py:377
  45.0 3.2 %projection.7 = (f32[4,256,512]{2,1,0:T(8,128)S(1)}, bf16[4,144,512]{2,1,0:T(8,128)(2,1)S(1)}, bf16[4,144,512]{2,1,0:T(8,128)(2,1)S(1)}) custom-call(bf16[256,1152]{1,0:T(8,128)(2,1)S(1)} %get-tuple-element.122.refs_0_, bf16[256,1152]{1,0:T(8,128)(2,1)S(1)} %get-tuple-element.135.refs_1_, bf16[256,1152]{1,0:T(8,128)(2,1)S(1)} %collective-permute-done.3.refs_2_, ...), custom_call_target="tpu_custom_call" | custom-call | tf_op jit(solution)/shard_map/projection/pallas_call | solution.py:344
  48.2 2.0 %collective-permute-start.12 = (bf16[4,144,512]{2,1,0:T(8,128)(2,1)S(1)}, bf16[4,144,512]{2,1,0:T(8,128)(2,1)S(1)}, u32[]{:S(2)}, u32[]{:S(2)}) collective-permute-start(bf16[4,144,512]{2,1,0:T(8,128)(2,1)S(1)} %get-tuple-element.146), channel_id=1, source_target_pairs={{0,4},{4,0},{8,12},{12,8},{16,20},{20,16},{24,28},{28,24},{1,5},{5... | collective-permute-start | bytes 1769480 | tf_op jit(solution)/shard_map/ppermute | solution.py:377
  50.3 3.1 %collective-permute-done.7.refs_1_ = bf16[4,144,512]{2,1,0:T(8,128)(2,1)S(1)} collective-permute-done((bf16[4,144,512]{2,1,0:T(8,128)(2,1)S(1)}, bf16[4,144,512]{2,1,0:T(8,128)(2,1)S(1)}, u32[]{:S(2)}, u32[]{:S(2)}) %collective-permute-start.7) | collective-permute-done | bytes 589856 | tf_op jit(solution)/shard_map/ppermute | solution.py:377
  54.5 1.8 %collective-permute-start.13 = (bf16[2,144,512]{2,1,0:T(8,128)(2,1)S(1)}, bf16[2,144,512]{2,1,0:T(8,128)(2,1)S(1)}, u32[]{:S(2)}, u32[]{:S(2)}) collective-permute-start(bf16[2,144,512]{2,1,0:T(8,128)(2,1)S(1)} %get-tuple-element.139), channel_id=1, source_target_pairs={{0,8},{4,12},{8,0},{12,4},{16,24},{20,28},{24,16},{28,20},{1,9},{5... | collective-permute-start | bytes 884744 | tf_op jit(solution)/shard_map/ppermute | solution.py:377
  57.8 2.8 %projection.8 = (f32[4,256,512]{2,1,0:T(8,128)S(1)}, bf16[4,128,512]{2,1,0:T(8,128)(2,1)S(1)}, bf16[4,128,512]{2,1,0:T(8,128)(2,1)S(1)}) custom-call(bf16[256,1024]{1,0:T(8,128)(2,1)S(1)} %get-tuple-element.117.refs_0_, bf16[256,1024]{1,0:T(8,128)(2,1)S(1)} %get-tuple-element.141.refs_1_, bf16[256,1024]{1,0:T(8,128)(2,1)S(1)} %collective-permute-done.8.refs_2_, ...), custom_call_target="tpu_custom_call" | custom-call | tf_op jit(solution)/shard_map/projection/pallas_call | solution.py:344
  62.2 1.8 %collective-permute-done.13.refs_1_ = bf16[2,144,512]{2,1,0:T(8,128)(2,1)S(1)} collective-permute-done((bf16[2,144,512]{2,1,0:T(8,128)(2,1)S(1)}, bf16[2,144,512]{2,1,0:T(8,128)(2,1)S(1)}, u32[]{:S(2)}, u32[]{:S(2)}) %collective-permute-start.13) | collective-permute-done | bytes 294944 | tf_op jit(solution)/shard_map/ppermute | solution.py:377
  64.0 2.8 %collective-permute-start.15 = (bf16[1,144,512]{2,1,0:T(8,128)(2,1)S(1)}, bf16[1,144,512]{2,1,0:T(8,128)(2,1)S(1)}, u32[]{:S(2)}, u32[]{:S(2)}) collective-permute-start(bf16[1,144,512]{2,1,0:T(8,128)(2,1)S(1)} %get-tuple-element.150), channel_id=1, source_target_pairs={{0,16},{4,20},{8,24},{12,28},{16,0},{20,4},{24,8},{28,12},{1,17},{... | collective-permute-start | bytes 442376 | tf_op jit(solution)/shard_map/ppermute | solution.py:377
  67.0 1.6 %collective-permute-start.14 = (bf16[2,144,512]{2,1,0:T(8,128)(2,1)S(1)}, bf16[2,144,512]{2,1,0:T(8,128)(2,1)S(1)}, u32[]{:S(2)}, u32[]{:S(2)}) collective-permute-start(bf16[2,144,512]{2,1,0:T(8,128)(2,1)S(1)} %get-tuple-element.153), channel_id=1, source_target_pairs={{0,8},{4,12},{8,0},{12,4},{16,24},{20,28},{24,16},{28,20},{1,9},{5... | collective-permute-start | bytes 884744 | tf_op jit(solution)/shard_map/ppermute | solution.py:377
  70.2 3.7 %collective-permute-done.15.refs_1_ = bf16[1,144,512]{2,1,0:T(8,128)(2,1)S(1)} collective-permute-done((bf16[1,144,512]{2,1,0:T(8,128)(2,1)S(1)}, bf16[1,144,512]{2,1,0:T(8,128)(2,1)S(1)}, u32[]{:S(2)}, u32[]{:S(2)}) %collective-permute-start.15) | collective-permute-done | bytes 147488 | tf_op jit(solution)/shard_map/ppermute | solution.py:377
  73.9 2.7 %projection.9 = (f32[4,256,512]{2,1,0:T(8,128)S(1)}, bf16[4,112,512]{2,1,0:T(8,128)(2,1)S(1)}, bf16[4,112,512]{2,1,0:T(8,128)(2,1)S(1)}) custom-call(bf16[256,896]{1,0:T(8,128)(2,1)S(1)} %get-tuple-element.119.refs_0_, bf16[256,896]{1,0:T(8,128)(2,1)S(1)} %get-tuple-element.158.refs_1_, bf16[256,896]{1,0:T(8,128)(2,1)S(1)} %collective-permute-done.2.refs_2_, ...), custom_call_target="tpu_custom_call" | custom-call | tf_op jit(solution)/shard_map/projection/pallas_call | solution.py:344
  76.6 1.6 %collective-permute-start.21 = (bf16[4,112,512]{2,1,0:T(8,128)(2,1)S(1)}, bf16[4,112,512]{2,1,0:T(8,128)(2,1)S(1)}, u32[]{:S(2)}, u32[]{:S(2)}) collective-permute-start(bf16[4,112,512]{2,1,0:T(8,128)(2,1)S(1)} %get-tuple-element.174), channel_id=1, source_target_pairs={{0,4},{4,0},{8,12},{12,8},{16,20},{20,16},{24,28},{28,24},{1,5},{5... | collective-permute-start | bytes 1376264 | tf_op jit(solution)/shard_map/ppermute | solution.py:377
  79.6 3.4 %collective-permute-start.22 = (bf16[1,144,512]{2,1,0:T(8,128)(2,1)S(1)}, bf16[1,144,512]{2,1,0:T(8,128)(2,1)S(1)}, u32[]{:S(2)}, u32[]{:S(2)}) collective-permute-start(bf16[1,144,512]{2,1,0:T(8,128)(2,1)S(1)} %get-tuple-element.162), channel_id=1, source_target_pairs={{0,16},{4,20},{8,24},{12,28},{16,0},{20,4},{24,8},{28,12},{1,17},{... | collective-permute-start | bytes 442376 | tf_op jit(solution)/shard_map/ppermute | solution.py:377
  83.0 2.3 %projection.10 = (f32[4,256,512]{2,1,0:T(8,128)S(1)}, bf16[4,80,512]{2,1,0:T(8,128)(2,1)S(1)}, bf16[4,80,512]{2,1,0:T(8,128)(2,1)S(1)}) custom-call(bf16[256,640]{1,0:T(8,128)(2,1)S(1)} %get-tuple-element.115.refs_0_, bf16[256,640]{1,0:T(8,128)(2,1)S(1)} %get-tuple-element.166.refs_1_, bf16[256,640]{1,0:T(8,128)(2,1)S(1)} %collective-permute-done.16.refs_2_, ...), custom_call_target="tpu_custom_call" | custom-call | tf_op jit(solution)/shard_map/projection/pallas_call | solution.py:344
  86.0 1.6 %projection.11 = (bf16[4,256,512]{2,1,0:T(8,128)(2,1)S(1)}, bf16[4,64,512]{2,1,0:T(8,128)(2,1)S(1)}, bf16[4,64,512]{2,1,0:T(8,128)(2,1)S(1)}) custom-call(bf16[256,512]{1,0:T(8,128)(2,1)S(1)} %get-tuple-element.111.refs_0_, bf16[256,512]{1,0:T(8,128)(2,1)S(1)} %get-tuple-element.169.refs_1_, bf16[256,512]{1,0:T(8,128)(2,1)S(1)} %collective-permute-done.1.refs_2_, ...), custom_call_target="tpu_custom_call" | custom-call | tf_op jit(solution)/shard_map/projection/pallas_call | solution.py:344
  89.2 3.7 %collective-permute-start.24 = (bf16[2,112,512]{2,1,0:T(8,128)(2,1)S(1)}, bf16[2,112,512]{2,1,0:T(8,128)(2,1)S(1)}, u32[]{:S(2)}, u32[]{:S(2)}) collective-permute-start(bf16[2,112,512]{2,1,0:T(8,128)(2,1)S(1)} %get-tuple-element.178), channel_id=1, source_target_pairs={{0,8},{4,12},{8,0},{12,4},{16,24},{20,28},{24,16},{28,20},{1,9},{5... | collective-permute-start | bytes 688136 | tf_op jit(solution)/shard_map/ppermute | solution.py:377
  94.4 2.9 %attention_backward_first.1 = (bf16[512,512]{1,0:T(8,128)(2,1)S(1)}, bf16[2,512,256]{2,1,0:T(8,128)(2,1)S(1)}, f32[2,512,256]{2,1,0:T(8,128)S(1)}) custom-call(bf16[1024,512]{1,0:T(8,128)(2,1)S(1)} %copy-done.1, bf16[1024,256]{1,0:T(8,128)(2,1)S(1)} %copy-done.2, bf16[1024,256]{1,0:T(8,128)(2,1)S(1)} %copy-done.3, bf16[1024,512]{1,0:T(8,128)(2,1)S(1)} %bitcast.8, ...), custom_call_target="tpu_custom_call" | custom-call | tf_op jit(solution)/shard_map/attention_backward_first/pallas_call | solution.py:209
  98.7 2.9 %collective-permute-done.25.refs_1_ = bf16[1,128,512]{2,1,0:T(8,128)(2,1)S(1)} collective-permute-done((bf16[1,128,512]{2,1,0:T(8,128)(2,1)S(1)}, bf16[1,128,512]{2,1,0:T(8,128)(2,1)S(1)}, u32[]{:S(2)}, u32[]{:S(2)}) %collective-permute-start.25) | collective-permute-done | bytes 131104 | tf_op jit(solution)/shard_map/ppermute | solution.py:377
  102.5 2.9 %attention_backward_second.1 = (bf16[512,512]{1,0:T(8,128)(2,1)S(1)}, bf16[2,512,256]{2,1,0:T(8,128)(2,1)S(1)}, f32[2,512,256]{2,1,0:T(8,128)S(1)}) custom-call(bf16[1024,512]{1,0:T(8,128)(2,1)S(1)} %copy-done.1, bf16[1024,256]{1,0:T(8,128)(2,1)S(1)} %copy-done.2, bf16[1024,256]{1,0:T(8,128)(2,1)S(1)} %copy-done.3, bf16[1024,512]{1,0:T(8,128)(2,1)S(1)} %bitcast.9, ...), custom_call_target="tpu_custom_call" | custom-call | tf_op jit(solution)/shard_map/attention_backward_second/pallas_call | solution.py:209
  105.5 5.7 %collective-permute-start.31 = (bf16[2,64,512]{2,1,0:T(8,128)(2,1)S(1)}, bf16[2,64,512]{2,1,0:T(8,128)(2,1)S(1)}, u32[]{:S(2)}, u32[]{:S(2)}) collective-permute-start(bf16[2,64,512]{2,1,0:T(8,128)(2,1)S(1)} %get-tuple-element.207), channel_id=1, source_target_pairs={{0,8},{4,12},{8,0},{12,4},{16,24},{20,28},{24,16},{28,20},{1,9},{5... | collective-permute-start | bytes 393224 | tf_op jit(solution)/shard_map/ppermute | solution.py:377
  112.3 8.2 %collective-permute-done.28.refs_1_ = bf16[2,80,512]{2,1,0:T(8,128)(2,1)S(1)} collective-permute-done((bf16[2,80,512]{2,1,0:T(8,128)(2,1)S(1)}, bf16[2,80,512]{2,1,0:T(8,128)(2,1)S(1)}, u32[]{:S(2)}, u32[]{:S(2)}) %collective-permute-start.28) | collective-permute-done | bytes 163872 | tf_op jit(solution)/shard_map/ppermute | solution.py:377
  122.0 1.7 %collective-permute-start.32 = (bf16[1,64,512]{2,1,0:T(8,128)(2,1)S(1)}, bf16[1,64,512]{2,1,0:T(8,128)(2,1)S(1)}, u32[]{:S(2)}, u32[]{:S(2)}) collective-permute-start(bf16[1,64,512]{2,1,0:T(8,128)(2,1)S(1)} %get-tuple-element.214), channel_id=1, source_target_pairs={{0,16},{4,20},{8,24},{12,28},{16,0},{20,4},{24,8},{28,12},{1,17},{... | collective-permute-start | bytes 196616 | tf_op jit(solution)/shard_map/ppermute | solution.py:377
  123.7 2.9 %collective-permute-done.30.refs_1_ = bf16[1,80,512]{2,1,0:T(8,128)(2,1)S(1)} collective-permute-done((bf16[1,80,512]{2,1,0:T(8,128)(2,1)S(1)}, bf16[1,80,512]{2,1,0:T(8,128)(2,1)S(1)}, u32[]{:S(2)}, u32[]{:S(2)}) %collective-permute-start.30) | collective-permute-done | bytes 81952 | tf_op jit(solution)/shard_map/ppermute | solution.py:377
  (85 shorter events, 23.6 us)
Async XLA Ops:
  0.7 14.6 %collective-permute-start = (bf16[256,5376]{1,0:T(8,128)(2,1)}, bf16[256,5376]{1,0:T(8,128)(2,1)S(1)}, u32[]{:S(2)}, u32[]{:S(2)}) collective-permute-start(bf16[256,5376]{1,0:T(8,128)(2,1)} %og_ref.1), channel_id=1, source_target_pairs={{0,1},{1,0},{2,3},{3,2},{4,5},{5,4},{6,7},{7,6},{8,9},{9,8},{10,11... | collective-permute-start | bytes 8257544 | tf_op jit(solution)/shard_map/ppermute | solution.py:377
  4.3 21.7 %collective-permute-start.4 = (bf16[256,1152]{1,0:T(8,128)(2,1)S(1)}, bf16[256,1152]{1,0:T(8,128)(2,1)S(1)}, u32[]{:S(2)}, u32[]{:S(2)}) collective-permute-start(bf16[256,1152]{1,0:T(8,128)(2,1)S(1)} %get-tuple-element.120.refs_0_), channel_id=1, source_target_pairs={{0,2},{1,3},{2,0},{3,1},{4,6},{5,7},{6,4},{7,5},{8,10},{9,11},{10,... | collective-permute-start | bytes 1769480 | tf_op jit(solution)/shard_map/ppermute | solution.py:377
  7.0 14.8 %collective-permute-start.5 = (bf16[2,512,256]{2,1,0:T(8,128)(2,1)S(1)}, bf16[2,512,256]{2,1,0:T(8,128)(2,1)S(1)}, u32[]{:S(2)}, u32[]{:S(2)}) collective-permute-start(bf16[2,512,256]{2,1,0:T(8,128)(2,1)S(1)} %pack_halo.1), channel_id=1, source_target_pairs={{0,4},{4,8},{8,12},{12,16},{16,20},{20,24},{24,28},{1,5},{5,9},{9,... | collective-permute-start | bytes 1572872 | tf_op jit(solution)/shard_map/ppermute | solution.py:397
  10.4 23.3 %collective-permute-start.3 = (bf16[256,1152]{1,0:T(8,128)(2,1)S(1)}, bf16[256,1152]{1,0:T(8,128)(2,1)S(1)}, u32[]{:S(2)}, u32[]{:S(2)}) collective-permute-start(bf16[256,1152]{1,0:T(8,128)(2,1)S(1)} %get-tuple-element.122.refs_0_), channel_id=1, source_target_pairs={{0,2},{1,3},{2,0},{3,1},{4,6},{5,7},{6,4},{7,5},{8,10},{9,11},{10,... | collective-permute-start | bytes 1769480 | tf_op jit(solution)/shard_map/ppermute | solution.py:377
  26.0 7.7 %collective-permute-start.6 = (bf16[256,1152]{1,0:T(8,128)(2,1)S(1)}, bf16[256,1152]{1,0:T(8,128)(2,1)S(1)}, u32[]{:S(2)}, u32[]{:S(2)}) collective-permute-start(bf16[256,1152]{1,0:T(8,128)(2,1)S(1)} %collective-permute-done.4.refs_2_), channel_id=1, source_target_pairs={{0,1},{1,0},{2,3},{3,2},{4,5},{5,4},{6,7},{7,6},{8,9},{9,8},{10,11... | collective-permute-start | bytes 1769480 | tf_op jit(solution)/shard_map/ppermute | solution.py:377
  26.1 18.9 %collective-permute-start.8 = (bf16[256,1024]{1,0:T(8,128)(2,1)S(1)}, bf16[256,1024]{1,0:T(8,128)(2,1)S(1)}, u32[]{:S(2)}, u32[]{:S(2)}) collective-permute-start(bf16[256,1024]{1,0:T(8,128)(2,1)S(1)} %get-tuple-element.117.refs_0_), channel_id=1, source_target_pairs={{0,2},{1,3},{2,0},{3,1},{4,6},{5,7},{6,4},{7,5},{8,10},{9,11},{10,... | collective-permute-start | bytes 1572872 | tf_op jit(solution)/shard_map/ppermute | solution.py:377
  33.8 11.2 %collective-permute-start.9 = (bf16[256,1152]{1,0:T(8,128)(2,1)S(1)}, bf16[256,1152]{1,0:T(8,128)(2,1)S(1)}, u32[]{:S(2)}, u32[]{:S(2)}) collective-permute-start(bf16[256,1152]{1,0:T(8,128)(2,1)S(1)} %collective-permute-done.3.refs_2_), channel_id=1, source_target_pairs={{0,1},{1,0},{2,3},{3,2},{4,5},{5,4},{6,7},{7,6},{8,9},{9,8},{10,11... | collective-permute-start | bytes 1769480 | tf_op jit(solution)/shard_map/ppermute | solution.py:377
  37.2 16.2 %collective-permute-start.7 = (bf16[4,144,512]{2,1,0:T(8,128)(2,1)S(1)}, bf16[4,144,512]{2,1,0:T(8,128)(2,1)S(1)}, u32[]{:S(2)}, u32[]{:S(2)}) collective-permute-start(bf16[4,144,512]{2,1,0:T(8,128)(2,1)S(1)} %get-tuple-element.131), channel_id=1, source_target_pairs={{0,4},{4,0},{8,12},{12,8},{16,20},{20,16},{24,28},{28,24},{1,5},{5... | collective-permute-start | bytes 1769480 | tf_op jit(solution)/shard_map/ppermute | solution.py:377
  39.2 15.3 %collective-permute-start.2 = (bf16[256,896]{1,0:T(8,128)(2,1)S(1)}, bf16[256,896]{1,0:T(8,128)(2,1)S(1)}, u32[]{:S(2)}, u32[]{:S(2)}) collective-permute-start(bf16[256,896]{1,0:T(8,128)(2,1)S(1)} %get-tuple-element.119.refs_0_), channel_id=1, source_target_pairs={{0,2},{1,3},{2,0},{3,1},{4,6},{5,7},{6,4},{7,5},{8,10},{9,11},{10,... | collective-permute-start | bytes 1376264 | tf_op jit(solution)/shard_map/ppermute | solution.py:377
  45.0 12.8 %collective-permute-start.10 = (bf16[256,1024]{1,0:T(8,128)(2,1)S(1)}, bf16[256,1024]{1,0:T(8,128)(2,1)S(1)}, u32[]{:S(2)}, u32[]{:S(2)}) collective-permute-start(bf16[256,1024]{1,0:T(8,128)(2,1)S(1)} %collective-permute-done.8.refs_2_), channel_id=1, source_target_pairs={{0,1},{1,0},{2,3},{3,2},{4,5},{5,4},{6,7},{7,6},{8,9},{9,8},{10,11... | collective-permute-start | bytes 1572872 | tf_op jit(solution)/shard_map/ppermute | solution.py:377
  48.2 18.6 %collective-permute-start.12 = (bf16[4,144,512]{2,1,0:T(8,128)(2,1)S(1)}, bf16[4,144,512]{2,1,0:T(8,128)(2,1)S(1)}, u32[]{:S(2)}, u32[]{:S(2)}) collective-permute-start(bf16[4,144,512]{2,1,0:T(8,128)(2,1)S(1)} %get-tuple-element.146), channel_id=1, source_target_pairs={{0,4},{4,0},{8,12},{12,8},{16,20},{20,16},{24,28},{28,24},{1,5},{5... | collective-permute-start | bytes 1769480 | tf_op jit(solution)/shard_map/ppermute | solution.py:377
  54.5 19.4 %collective-permute-start.17 = (bf16[256,896]{1,0:T(8,128)(2,1)S(1)}, bf16[256,896]{1,0:T(8,128)(2,1)S(1)}, u32[]{:S(2)}, u32[]{:S(2)}) collective-permute-start(bf16[256,896]{1,0:T(8,128)(2,1)S(1)} %collective-permute-done.2.refs_2_), channel_id=1, source_target_pairs={{0,1},{1,0},{2,3},{3,2},{4,5},{5,4},{6,7},{7,6},{8,9},{9,8},{10,11... | collective-permute-start | bytes 1376264 | tf_op jit(solution)/shard_map/ppermute | solution.py:377
  54.5 9.5 %collective-permute-start.13 = (bf16[2,144,512]{2,1,0:T(8,128)(2,1)S(1)}, bf16[2,144,512]{2,1,0:T(8,128)(2,1)S(1)}, u32[]{:S(2)}, u32[]{:S(2)}) collective-permute-start(bf16[2,144,512]{2,1,0:T(8,128)(2,1)S(1)} %get-tuple-element.139), channel_id=1, source_target_pairs={{0,8},{4,12},{8,0},{12,4},{16,24},{20,28},{24,16},{28,20},{1,9},{5... | collective-permute-start | bytes 884744 | tf_op jit(solution)/shard_map/ppermute | solution.py:377
  56.3 12.3 %collective-permute-start.16 = (bf16[256,640]{1,0:T(8,128)(2,1)S(1)}, bf16[256,640]{1,0:T(8,128)(2,1)S(1)}, u32[]{:S(2)}, u32[]{:S(2)}) collective-permute-start(bf16[256,640]{1,0:T(8,128)(2,1)S(1)} %get-tuple-element.115.refs_0_), channel_id=1, source_target_pairs={{0,2},{1,3},{2,0},{3,1},{4,6},{5,7},{6,4},{7,5},{8,10},{9,11},{10,... | collective-permute-start | bytes 983048 | tf_op jit(solution)/shard_map/ppermute | solution.py:377
  60.6 17.6 %collective-permute-start.11 = (bf16[4,128,512]{2,1,0:T(8,128)(2,1)S(1)}, bf16[4,128,512]{2,1,0:T(8,128)(2,1)S(1)}, u32[]{:S(2)}, u32[]{:S(2)}) collective-permute-start(bf16[4,128,512]{2,1,0:T(8,128)(2,1)S(1)} %get-tuple-element.144), channel_id=1, source_target_pairs={{0,4},{4,0},{8,12},{12,8},{16,20},{20,16},{24,28},{28,24},{1,5},{5... | collective-permute-start | bytes 1572872 | tf_op jit(solution)/shard_map/ppermute | solution.py:377
  64.0 9.8 %collective-permute-start.15 = (bf16[1,144,512]{2,1,0:T(8,128)(2,1)S(1)}, bf16[1,144,512]{2,1,0:T(8,128)(2,1)S(1)}, u32[]{:S(2)}, u32[]{:S(2)}) collective-permute-start(bf16[1,144,512]{2,1,0:T(8,128)(2,1)S(1)} %get-tuple-element.150), channel_id=1, source_target_pairs={{0,16},{4,20},{8,24},{12,28},{16,0},{20,4},{24,8},{28,12},{1,17},{... | collective-permute-start | bytes 442376 | tf_op jit(solution)/shard_map/ppermute | solution.py:377
  67.0 11.2 %collective-permute-start.14 = (bf16[2,144,512]{2,1,0:T(8,128)(2,1)S(1)}, bf16[2,144,512]{2,1,0:T(8,128)(2,1)S(1)}, u32[]{:S(2)}, u32[]{:S(2)}) collective-permute-start(bf16[2,144,512]{2,1,0:T(8,128)(2,1)S(1)} %get-tuple-element.153), channel_id=1, source_target_pairs={{0,8},{4,12},{8,0},{12,4},{16,24},{20,28},{24,16},{28,20},{1,9},{5... | collective-permute-start | bytes 884744 | tf_op jit(solution)/shard_map/ppermute | solution.py:377
  68.6 9.7 %collective-permute-start.1 = (bf16[256,512]{1,0:T(8,128)(2,1)S(1)}, bf16[256,512]{1,0:T(8,128)(2,1)S(1)}, u32[]{:S(2)}, u32[]{:S(2)}) collective-permute-start(bf16[256,512]{1,0:T(8,128)(2,1)S(1)} %get-tuple-element.111.refs_0_), channel_id=1, source_target_pairs={{0,2},{1,3},{2,0},{3,1},{4,6},{5,7},{6,4},{7,5},{8,10},{9,11},{10,... | collective-permute-start | bytes 786440 | tf_op jit(solution)/shard_map/ppermute | solution.py:377
  76.6 12.6 %collective-permute-start.21 = (bf16[4,112,512]{2,1,0:T(8,128)(2,1)S(1)}, bf16[4,112,512]{2,1,0:T(8,128)(2,1)S(1)}, u32[]{:S(2)}, u32[]{:S(2)}) collective-permute-start(bf16[4,112,512]{2,1,0:T(8,128)(2,1)S(1)} %get-tuple-element.174), channel_id=1, source_target_pairs={{0,4},{4,0},{8,12},{12,8},{16,20},{20,16},{24,28},{28,24},{1,5},{5... | collective-permute-start | bytes 1376264 | tf_op jit(solution)/shard_map/ppermute | solution.py:377
  78.4 7.6 %collective-permute-start.19 = (bf16[256,512]{1,0:T(8,128)(2,1)S(1)}, bf16[256,512]{1,0:T(8,128)(2,1)S(1)}, u32[]{:S(2)}, u32[]{:S(2)}) collective-permute-start(bf16[256,512]{1,0:T(8,128)(2,1)S(1)} %collective-permute-done.1.refs_2_), channel_id=1, source_target_pairs={{0,1},{1,0},{2,3},{3,2},{4,5},{5,4},{6,7},{7,6},{8,9},{9,8},{10,11... | collective-permute-start | bytes 786440 | tf_op jit(solution)/shard_map/ppermute | solution.py:377
  79.0 14.0 %collective-permute-start.20 = (bf16[2,128,512]{2,1,0:T(8,128)(2,1)S(1)}, bf16[2,128,512]{2,1,0:T(8,128)(2,1)S(1)}, u32[]{:S(2)}, u32[]{:S(2)}) collective-permute-start(bf16[2,128,512]{2,1,0:T(8,128)(2,1)S(1)} %get-tuple-element.164), channel_id=1, source_target_pairs={{0,8},{4,12},{8,0},{12,4},{16,24},{20,28},{24,16},{28,20},{1,9},{5... | collective-permute-start | bytes 786440 | tf_op jit(solution)/shard_map/ppermute | solution.py:377
  79.6 9.5 %collective-permute-start.22 = (bf16[1,144,512]{2,1,0:T(8,128)(2,1)S(1)}, bf16[1,144,512]{2,1,0:T(8,128)(2,1)S(1)}, u32[]{:S(2)}, u32[]{:S(2)}) collective-permute-start(bf16[1,144,512]{2,1,0:T(8,128)(2,1)S(1)} %get-tuple-element.162), channel_id=1, source_target_pairs={{0,16},{4,20},{8,24},{12,28},{16,0},{20,4},{24,8},{28,12},{1,17},{... | collective-permute-start | bytes 442376 | tf_op jit(solution)/shard_map/ppermute | solution.py:377
  85.3 16.3 %collective-permute-start.23 = (bf16[4,80,512]{2,1,0:T(8,128)(2,1)S(1)}, bf16[4,80,512]{2,1,0:T(8,128)(2,1)S(1)}, u32[]{:S(2)}, u32[]{:S(2)}) collective-permute-start(bf16[4,80,512]{2,1,0:T(8,128)(2,1)S(1)} %get-tuple-element.185), channel_id=1, source_target_pairs={{0,4},{4,0},{8,12},{12,8},{16,20},{20,16},{24,28},{28,24},{1,5},{5... | collective-permute-start | bytes 983048 | tf_op jit(solution)/shard_map/ppermute | solution.py:377
  87.6 17.8 %collective-permute-start.29 = (bf16[4,64,512]{2,1,0:T(8,128)(2,1)S(1)}, bf16[4,64,512]{2,1,0:T(8,128)(2,1)S(1)}, u32[]{:S(2)}, u32[]{:S(2)}) collective-permute-start(bf16[4,64,512]{2,1,0:T(8,128)(2,1)S(1)} %get-tuple-element.205), channel_id=1, source_target_pairs={{0,4},{4,0},{8,12},{12,8},{16,20},{20,16},{24,28},{28,24},{1,5},{5... | collective-permute-start | bytes 786440 | tf_op jit(solution)/shard_map/ppermute | solution.py:377
  89.2 12.3 %collective-permute-start.24 = (bf16[2,112,512]{2,1,0:T(8,128)(2,1)S(1)}, bf16[2,112,512]{2,1,0:T(8,128)(2,1)S(1)}, u32[]{:S(2)}, u32[]{:S(2)}) collective-permute-start(bf16[2,112,512]{2,1,0:T(8,128)(2,1)S(1)} %get-tuple-element.178), channel_id=1, source_target_pairs={{0,8},{4,12},{8,0},{12,4},{16,24},{20,28},{24,16},{28,20},{1,9},{5... | collective-permute-start | bytes 688136 | tf_op jit(solution)/shard_map/ppermute | solution.py:377
  93.0 8.6 %collective-permute-start.25 = (bf16[1,128,512]{2,1,0:T(8,128)(2,1)S(1)}, bf16[1,128,512]{2,1,0:T(8,128)(2,1)S(1)}, u32[]{:S(2)}, u32[]{:S(2)}) collective-permute-start(bf16[1,128,512]{2,1,0:T(8,128)(2,1)S(1)} %get-tuple-element.180), channel_id=1, source_target_pairs={{0,16},{4,20},{8,24},{12,28},{16,0},{20,4},{24,8},{28,12},{1,17},{... | collective-permute-start | bytes 393224 | tf_op jit(solution)/shard_map/ppermute | solution.py:377
  97.4 30.0 %collective-permute-start.26 = (bf16[2,512,256]{2,1,0:T(8,128)(2,1)S(1)}, bf16[2,512,256]{2,1,0:T(8,128)(2,1)S(1)}, u32[]{:S(2)}, u32[]{:S(2)}) collective-permute-start(bf16[2,512,256]{2,1,0:T(8,128)(2,1)S(1)} %get-tuple-element.199), channel_id=1, source_target_pairs={{4,0},{8,4},{12,8},{16,12},{20,16},{24,20},{28,24},{5,1},{9,5},{13... | collective-permute-start | bytes 1572872 | tf_op jit(solution)/shard_map/ppermute | solution.py:430
  101.7 18.8 %collective-permute-start.28 = (bf16[2,80,512]{2,1,0:T(8,128)(2,1)S(1)}, bf16[2,80,512]{2,1,0:T(8,128)(2,1)S(1)}, u32[]{:S(2)}, u32[]{:S(2)}) collective-permute-start(bf16[2,80,512]{2,1,0:T(8,128)(2,1)S(1)} %get-tuple-element.193), channel_id=1, source_target_pairs={{0,8},{4,12},{8,0},{12,4},{16,24},{20,28},{24,16},{28,20},{1,9},{5... | collective-permute-start | bytes 491528 | tf_op jit(solution)/shard_map/ppermute | solution.py:377
  105.5 16.4 %collective-permute-start.31 = (bf16[2,64,512]{2,1,0:T(8,128)(2,1)S(1)}, bf16[2,64,512]{2,1,0:T(8,128)(2,1)S(1)}, u32[]{:S(2)}, u32[]{:S(2)}) collective-permute-start(bf16[2,64,512]{2,1,0:T(8,128)(2,1)S(1)} %get-tuple-element.207), channel_id=1, source_target_pairs={{0,8},{4,12},{8,0},{12,4},{16,24},{20,28},{24,16},{28,20},{1,9},{5... | collective-permute-start | bytes 393224 | tf_op jit(solution)/shard_map/ppermute | solution.py:377
  111.2 9.5 %collective-permute-start.27 = (bf16[1,112,512]{2,1,0:T(8,128)(2,1)S(1)}, bf16[1,112,512]{2,1,0:T(8,128)(2,1)S(1)}, u32[]{:S(2)}, u32[]{:S(2)}) collective-permute-start(bf16[1,112,512]{2,1,0:T(8,128)(2,1)S(1)} %get-tuple-element.191), channel_id=1, source_target_pairs={{0,16},{4,20},{8,24},{12,28},{16,0},{20,4},{24,8},{28,12},{1,17},{... | collective-permute-start | bytes 344072 | tf_op jit(solution)/shard_map/ppermute | solution.py:377
  120.6 6.1 %collective-permute-start.30 = (bf16[1,80,512]{2,1,0:T(8,128)(2,1)S(1)}, bf16[1,80,512]{2,1,0:T(8,128)(2,1)S(1)}, u32[]{:S(2)}, u32[]{:S(2)}) collective-permute-start(bf16[1,80,512]{2,1,0:T(8,128)(2,1)S(1)} %get-tuple-element.209), channel_id=1, source_target_pairs={{0,16},{4,20},{8,24},{12,28},{16,0},{20,4},{24,8},{28,12},{1,17},{... | collective-permute-start | bytes 245768 | tf_op jit(solution)/shard_map/ppermute | solution.py:377
  122.0 5.4 %collective-permute-start.32 = (bf16[1,64,512]{2,1,0:T(8,128)(2,1)S(1)}, bf16[1,64,512]{2,1,0:T(8,128)(2,1)S(1)}, u32[]{:S(2)}, u32[]{:S(2)}) collective-permute-start(bf16[1,64,512]{2,1,0:T(8,128)(2,1)S(1)} %get-tuple-element.214), channel_id=1, source_target_pairs={{0,16},{4,20},{8,24},{12,28},{16,0},{20,4},{24,8},{28,12},{1,17},{... | collective-permute-start | bytes 196616 | tf_op jit(solution)/shard_map/ppermute | solution.py:377
  (7 other events, 53.6 us)

commit v4 on v3

--- a/solution.py
+++ b/solution.py
@@ -43,12 +43,25 @@
 
 
 def prepare_kernel(blocks, blk, lens, og_ref, *refs):
-    off = 0
-    for out, length in zip(refs, lens):
-        out[...] = jnp.concatenate(
-            [og_ref[:, t * blk + off : t * blk + off + length] for t in range(blocks)], axis=1
+    *out_refs, rows_vmem, sems = refs
+    size = og_ref.shape[0] // 4
+    copies = []
+    for n in range(4):
+        rows = pl.ds(n * size, size)
+        copies.append(
+            pltpu.make_async_copy(og_ref.at[rows, :], rows_vmem.at[rows, :], sems.at[n])
         )
-        off += length
+        copies[-1].start()
+    for n, copy in enumerate(copies):
+        copy.wait()
+        rows = slice(n * size, (n + 1) * size)
+        off = 0
+        for out, length in zip(out_refs, lens):
+            at = [t * blk + off for t in range(blocks)]
+            out[rows, :] = jnp.concatenate(
+                [rows_vmem[rows, start : start + length] for start in at], axis=1
+            )
+            off += length
 
 
 def prepare(og, blocks, lens):
@@ -56,8 +69,9 @@
     return pl.pallas_call(
         functools.partial(prepare_kernel, blocks, width // blocks, lens),
         out_shape=[jax.ShapeDtypeStruct((rows, blocks * n), BF16) for n in lens],
-        in_specs=[vmem()],
+        in_specs=[hbm()],
         out_specs=[vmem() for _ in lens],
+        scratch_shapes=[pltpu.VMEM((rows, width), BF16), pltpu.SemaphoreType.DMA((4,))],
         compiler_params=params(),
         name="gather_columns",
     )(og)

time: 129 us -> 130 us (level)
  Pallas kernels: 36.1 us -> 38.6 us
  waiting for transfers between devices: 42.2 us -> 40.7 us
    pallas_call x2, Pallas kernels: 2.49 us -> 5.13 us  [prepare(): pl.pallas_call(functools.partial(prepare_kernel, blocks, width // blocks,...]
    ppermute x1, waiting for transfers between devices: 5.29 us -> 3.89 us  [shards(): lax.ppermute(halo, 'context', [(i, i + 1) for i in range(contexts - 1)])]
  transfers between devices with their start and end apart: 33 -> 33, of which waited for: 12 -> 12; matrix products, arithmetic and copies ran while one was open for 0% -> 0% of each run, Pallas kernels for 27% -> 29%
where the time goes in v4:
time: 130 us
  starting transfers between devices  47.8 us (37%)
  waiting for transfers between devices  40.7 us (31%)
  Pallas kernels  38.6 us (30%)
  local copies, waits for them, and re-layouts  1.94 us (1%)
    ppermute x31, starting transfers between devices, exchange(): lax.ppermute(x, axis, [(i, i ^ by) for i in range(lax.axis_size(axis))])  42.8 us
    ppermute x31, waiting for transfers between devices, exchange(): lax.ppermute(x, axis, [(i, i ^ by) for i in range(lax.axis_size(axis))])  36.8 us
    pallas_call x6, Pallas kernels, projection(): pl.pallas_call(functools.partial(projection_kernel, peers, blocks, off, l...  15.9 us
    pallas_call x2, Pallas kernels, forward(): pl.pallas_call(functools.partial(forward_kernel, kv_local, group, first),...  8.44 us
    pallas_call x2, Pallas kernels, backward(): pl.pallas_call(functools.partial(backward_kernel, kv_width // HEAD_SIZE,...  5.89 us
    pallas_call x2, Pallas kernels, prepare(): pl.pallas_call(functools.partial(prepare_kernel, blocks, width // blocks,...  5.13 us
    ppermute x1, waiting for transfers between devices, shards(): lax.ppermute(halo, 'context', [(i, i + 1) for i in range(contexts - 1)])  3.89 us
    ppermute x1, starting transfers between devices, shards(): lax.ppermute(halo, 'context', [(i, i + 1) for i in range(contexts - 1)])  3.43 us
  transfers between devices with their start and end apart: 33, of which 12 were waited for; matrix products, arithmetic and copies ran while one was open for 0% of the time, Pallas kernels for 29%

profile of v4, /device:TPU:0, one launch (start us, length us, event | category | flops | bytes accessed | tf_op | source)
XLA Modules:
  0.0 130.0 jit_solution(18271762389073290661)
XLA Ops:
  1.2 1.9 %copy-done.4 = bf16[256,5376]{1,0:T(8,128)(2,1)S(1)} copy-done((bf16[256,5376]{1,0:T(8,128)(2,1)S(1)}, bf16[256,5376]{1,0:T(8,128)(2,1)}, u32[]{:S(2)}) %copy-start.4) | copy-done | bytes 2752536
  3.0 2.5 %gather_columns.2 = (bf16[256,1152]{1,0:T(8,128)(2,1)S(1)}, bf16[256,1152]{1,0:T(8,128)(2,1)S(1)}, bf16[256,1024]{1,0:T(8,128)(2,1)S(1)}, bf16[256,896]{1,0:T(8,...) custom-call(bf16[256,5376]{1,0:T(8,128)(2,1)S(1)} %copy-done.4), custom_call_target="tpu_custom_call" | custom-call | tf_op jit(solution)/shard_map/gather_columns/pallas_call | solution.py:69
  5.5 2.7 %collective-permute-start.4 = (bf16[256,1152]{1,0:T(8,128)(2,1)S(1)}, bf16[256,1152]{1,0:T(8,128)(2,1)S(1)}, u32[]{:S(2)}, u32[]{:S(2)}) collective-permute-start(bf16[256,1152]{1,0:T(8,128)(2,1)S(1)} %get-tuple-element.120.refs_0_), channel_id=1, source_target_pairs={{0,2},{1,3},{2,0},{3,1},{4,6},{5,7},{6,4},{7,5},{8,10},{9,11},{10,... | collective-permute-start | bytes 1769480 | tf_op jit(solution)/shard_map/ppermute | solution.py:391
  8.2 3.4 %collective-permute-start.5 = (bf16[2,512,256]{2,1,0:T(8,128)(2,1)S(1)}, bf16[2,512,256]{2,1,0:T(8,128)(2,1)S(1)}, u32[]{:S(2)}, u32[]{:S(2)}) collective-permute-start(bf16[2,512,256]{2,1,0:T(8,128)(2,1)S(1)} %pack_halo.1), channel_id=1, source_target_pairs={{0,4},{4,8},{8,12},{12,16},{16,20},{20,24},{24,28},{1,5},{5,9},{9,... | collective-permute-start | bytes 1572872 | tf_op jit(solution)/shard_map/ppermute | solution.py:411
  12.2 4.2 %attention_forward_second.1 = (bf16[512,512]{1,0:T(8,128)(2,1)S(1)}, bf16[2,2,2,256,768]{4,3,2,1,0:T(8,128)(2,1)S(1)}) custom-call(bf16[1024,512]{1,0:T(8,128)(2,1)S(1)} %copy-done.1, bf16[1024,256]{1,0:T(8,128)(2,1)S(1)} %copy-done.2, bf16[1024,256]{1,0:T(8,128)(2,1)S(1)} %copy-done.3), custom_call_target="tpu_custom_call" | custom-call | tf_op jit(solution)/shard_map/attention_forward_second/pallas_call | solution.py:154
  16.5 2.7 %gather_columns.3 = (bf16[256,1152]{1,0:T(8,128)(2,1)S(1)}, bf16[256,1152]{1,0:T(8,128)(2,1)S(1)}, bf16[256,1024]{1,0:T(8,128)(2,1)S(1)}, bf16[256,896]{1,0:T(8,...) custom-call(bf16[256,5376]{1,0:T(8,128)(2,1)S(1)} %collective-permute-done.og_ref), custom_call_target="tpu_custom_call" | custom-call | tf_op jit(solution)/shard_map/gather_columns/pallas_call | solution.py:69
  19.1 3.9 %collective-permute-done.5.refs_3_.refs_6_ = bf16[2,512,256]{2,1,0:T(8,128)(2,1)S(1)} collective-permute-done((bf16[2,512,256]{2,1,0:T(8,128)(2,1)S(1)}, bf16[2,512,256]{2,1,0:T(8,128)(2,1)S(1)}, u32[]{:S(2)}, u32[]{:S(2)}) %collective-permute-start.5) | collective-permute-done | bytes 524320 | tf_op jit(solution)/shard_map/ppermute | solution.py:411
  23.0 4.2 %attention_forward_first.1 = (bf16[512,512]{1,0:T(8,128)(2,1)S(1)}, bf16[2,2,2,256,768]{4,3,2,1,0:T(8,128)(2,1)S(1)}) custom-call(bf16[1024,512]{1,0:T(8,128)(2,1)S(1)} %copy-done.1, bf16[1024,256]{1,0:T(8,128)(2,1)S(1)} %copy-done.2, bf16[1024,256]{1,0:T(8,128)(2,1)S(1)} %copy-done.3, bf16[2,512,256]{2,1,0:T(8,128)(2,1)S(1)} %collective-permute-done.5.refs_3_.refs_6_), custom_call_target="tpu_custom_call" | custom-call | tf_op jit(solution)/shard_map/attention_forward_first/pallas_call | solution.py:154
  27.9 7.1 %collective-permute-done.3.refs_2_ = bf16[256,1152]{1,0:T(8,128)(2,1)S(1)} collective-permute-done((bf16[256,1152]{1,0:T(8,128)(2,1)S(1)}, bf16[256,1152]{1,0:T(8,128)(2,1)S(1)}, u32[]{:S(2)}, u32[]{:S(2)}) %collective-permute-start.3) | collective-permute-done | bytes 589856 | tf_op jit(solution)/shard_map/ppermute | solution.py:391
  35.0 3.2 %projection.6 = (f32[4,256,512]{2,1,0:T(8,128)S(1)}, bf16[4,144,512]{2,1,0:T(8,128)(2,1)S(1)}, bf16[4,144,512]{2,1,0:T(8,128)(2,1)S(1)}) custom-call(bf16[256,1152]{1,0:T(8,128)(2,1)S(1)} %get-tuple-element.120.refs_0_, bf16[256,1152]{1,0:T(8,128)(2,1)S(1)} %get-tuple-element.128.refs_1_, bf16[256,1152]{1,0:T(8,128)(2,1)S(1)} %collective-permute-done.4.refs_2_, ...), custom_call_target="tpu_custom_call" | custom-call | tf_op jit(solution)/shard_map/projection/pallas_call | solution.py:358
  38.2 2.0 %collective-permute-start.7 = (bf16[4,144,512]{2,1,0:T(8,128)(2,1)S(1)}, bf16[4,144,512]{2,1,0:T(8,128)(2,1)S(1)}, u32[]{:S(2)}, u32[]{:S(2)}) collective-permute-start(bf16[4,144,512]{2,1,0:T(8,128)(2,1)S(1)} %get-tuple-element.131), channel_id=1, source_target_pairs={{0,4},{4,0},{8,12},{12,8},{16,20},{20,16},{24,28},{28,24},{1,5},{5... | collective-permute-start | bytes 1769480 | tf_op jit(solution)/shard_map/ppermute | solution.py:391
  41.8 4.4 %collective-permute-done.8.refs_2_ = bf16[256,1024]{1,0:T(8,128)(2,1)S(1)} collective-permute-done((bf16[256,1024]{1,0:T(8,128)(2,1)S(1)}, bf16[256,1024]{1,0:T(8,128)(2,1)S(1)}, u32[]{:S(2)}, u32[]{:S(2)}) %collective-permute-start.8) | collective-permute-done | bytes 524320 | tf_op jit(solution)/shard_map/ppermute | solution.py:391
  46.2 3.2 %projection.7 = (f32[4,256,512]{2,1,0:T(8,128)S(1)}, bf16[4,144,512]{2,1,0:T(8,128)(2,1)S(1)}, bf16[4,144,512]{2,1,0:T(8,128)(2,1)S(1)}) custom-call(bf16[256,1152]{1,0:T(8,128)(2,1)S(1)} %get-tuple-element.122.refs_0_, bf16[256,1152]{1,0:T(8,128)(2,1)S(1)} %get-tuple-element.135.refs_1_, bf16[256,1152]{1,0:T(8,128)(2,1)S(1)} %collective-permute-done.3.refs_2_, ...), custom_call_target="tpu_custom_call" | custom-call | tf_op jit(solution)/shard_map/projection/pallas_call | solution.py:358
  49.5 2.0 %collective-permute-start.12 = (bf16[4,144,512]{2,1,0:T(8,128)(2,1)S(1)}, bf16[4,144,512]{2,1,0:T(8,128)(2,1)S(1)}, u32[]{:S(2)}, u32[]{:S(2)}) collective-permute-start(bf16[4,144,512]{2,1,0:T(8,128)(2,1)S(1)} %get-tuple-element.146), channel_id=1, source_target_pairs={{0,4},{4,0},{8,12},{12,8},{16,20},{20,16},{24,28},{28,24},{1,5},{5... | collective-permute-start | bytes 1769480 | tf_op jit(solution)/shard_map/ppermute | solution.py:391
  51.5 3.0 %collective-permute-done.7.refs_1_ = bf16[4,144,512]{2,1,0:T(8,128)(2,1)S(1)} collective-permute-done((bf16[4,144,512]{2,1,0:T(8,128)(2,1)S(1)}, bf16[4,144,512]{2,1,0:T(8,128)(2,1)S(1)}, u32[]{:S(2)}, u32[]{:S(2)}) %collective-permute-start.7) | collective-permute-done | bytes 589856 | tf_op jit(solution)/shard_map/ppermute | solution.py:391
  55.7 1.8 %collective-permute-start.13 = (bf16[2,144,512]{2,1,0:T(8,128)(2,1)S(1)}, bf16[2,144,512]{2,1,0:T(8,128)(2,1)S(1)}, u32[]{:S(2)}, u32[]{:S(2)}) collective-permute-start(bf16[2,144,512]{2,1,0:T(8,128)(2,1)S(1)} %get-tuple-element.139), channel_id=1, source_target_pairs={{0,8},{4,12},{8,0},{12,4},{16,24},{20,28},{24,16},{28,20},{1,9},{5... | collective-permute-start | bytes 884744 | tf_op jit(solution)/shard_map/ppermute | solution.py:391
  59.1 3.0 %projection.8 = (f32[4,256,512]{2,1,0:T(8,128)S(1)}, bf16[4,128,512]{2,1,0:T(8,128)(2,1)S(1)}, bf16[4,128,512]{2,1,0:T(8,128)(2,1)S(1)}) custom-call(bf16[256,1024]{1,0:T(8,128)(2,1)S(1)} %get-tuple-element.117.refs_0_, bf16[256,1024]{1,0:T(8,128)(2,1)S(1)} %get-tuple-element.141.refs_1_, bf16[256,1024]{1,0:T(8,128)(2,1)S(1)} %collective-permute-done.8.refs_2_, ...), custom_call_target="tpu_custom_call" | custom-call | tf_op jit(solution)/shard_map/projection/pallas_call | solution.py:358
  65.3 2.8 %collective-permute-start.15 = (bf16[1,144,512]{2,1,0:T(8,128)(2,1)S(1)}, bf16[1,144,512]{2,1,0:T(8,128)(2,1)S(1)}, u32[]{:S(2)}, u32[]{:S(2)}) collective-permute-start(bf16[1,144,512]{2,1,0:T(8,128)(2,1)S(1)} %get-tuple-element.150), channel_id=1, source_target_pairs={{0,16},{4,20},{8,24},{12,28},{16,0},{20,4},{24,8},{28,12},{1,17},{... | collective-permute-start | bytes 442376 | tf_op jit(solution)/shard_map/ppermute | solution.py:391
  68.2 1.6 %collective-permute-start.14 = (bf16[2,144,512]{2,1,0:T(8,128)(2,1)S(1)}, bf16[2,144,512]{2,1,0:T(8,128)(2,1)S(1)}, u32[]{:S(2)}, u32[]{:S(2)}) collective-permute-start(bf16[2,144,512]{2,1,0:T(8,128)(2,1)S(1)} %get-tuple-element.153), channel_id=1, source_target_pairs={{0,8},{4,12},{8,0},{12,4},{16,24},{20,28},{24,16},{28,20},{1,9},{5... | collective-permute-start | bytes 884744 | tf_op jit(solution)/shard_map/ppermute | solution.py:391
  71.4 3.7 %collective-permute-done.15.refs_1_ = bf16[1,144,512]{2,1,0:T(8,128)(2,1)S(1)} collective-permute-done((bf16[1,144,512]{2,1,0:T(8,128)(2,1)S(1)}, bf16[1,144,512]{2,1,0:T(8,128)(2,1)S(1)}, u32[]{:S(2)}, u32[]{:S(2)}) %collective-permute-start.15) | collective-permute-done | bytes 147488 | tf_op jit(solution)/shard_map/ppermute | solution.py:391
  75.1 2.7 %projection.9 = (f32[4,256,512]{2,1,0:T(8,128)S(1)}, bf16[4,112,512]{2,1,0:T(8,128)(2,1)S(1)}, bf16[4,112,512]{2,1,0:T(8,128)(2,1)S(1)}) custom-call(bf16[256,896]{1,0:T(8,128)(2,1)S(1)} %get-tuple-element.119.refs_0_, bf16[256,896]{1,0:T(8,128)(2,1)S(1)} %get-tuple-element.158.refs_1_, bf16[256,896]{1,0:T(8,128)(2,1)S(1)} %collective-permute-done.2.refs_2_, ...), custom_call_target="tpu_custom_call" | custom-call | tf_op jit(solution)/shard_map/projection/pallas_call | solution.py:358
  80.8 3.4 %collective-permute-start.22 = (bf16[1,144,512]{2,1,0:T(8,128)(2,1)S(1)}, bf16[1,144,512]{2,1,0:T(8,128)(2,1)S(1)}, u32[]{:S(2)}, u32[]{:S(2)}) collective-permute-start(bf16[1,144,512]{2,1,0:T(8,128)(2,1)S(1)} %get-tuple-element.162), channel_id=1, source_target_pairs={{0,16},{4,20},{8,24},{12,28},{16,0},{20,4},{24,8},{28,12},{1,17},{... | collective-permute-start | bytes 442376 | tf_op jit(solution)/shard_map/ppermute | solution.py:391
  84.2 2.1 %projection.10 = (f32[4,256,512]{2,1,0:T(8,128)S(1)}, bf16[4,80,512]{2,1,0:T(8,128)(2,1)S(1)}, bf16[4,80,512]{2,1,0:T(8,128)(2,1)S(1)}) custom-call(bf16[256,640]{1,0:T(8,128)(2,1)S(1)} %get-tuple-element.115.refs_0_, bf16[256,640]{1,0:T(8,128)(2,1)S(1)} %get-tuple-element.166.refs_1_, bf16[256,640]{1,0:T(8,128)(2,1)S(1)} %collective-permute-done.16.refs_2_, ...), custom_call_target="tpu_custom_call" | custom-call | tf_op jit(solution)/shard_map/projection/pallas_call | solution.py:358
  87.2 1.6 %projection.11 = (bf16[4,256,512]{2,1,0:T(8,128)(2,1)S(1)}, bf16[4,64,512]{2,1,0:T(8,128)(2,1)S(1)}, bf16[4,64,512]{2,1,0:T(8,128)(2,1)S(1)}) custom-call(bf16[256,512]{1,0:T(8,128)(2,1)S(1)} %get-tuple-element.111.refs_0_, bf16[256,512]{1,0:T(8,128)(2,1)S(1)} %get-tuple-element.169.refs_1_, bf16[256,512]{1,0:T(8,128)(2,1)S(1)} %collective-permute-done.1.refs_2_, ...), custom_call_target="tpu_custom_call" | custom-call | tf_op jit(solution)/shard_map/projection/pallas_call | solution.py:358
  90.3 3.9 %collective-permute-start.24 = (bf16[2,112,512]{2,1,0:T(8,128)(2,1)S(1)}, bf16[2,112,512]{2,1,0:T(8,128)(2,1)S(1)}, u32[]{:S(2)}, u32[]{:S(2)}) collective-permute-start(bf16[2,112,512]{2,1,0:T(8,128)(2,1)S(1)} %get-tuple-element.178), channel_id=1, source_target_pairs={{0,8},{4,12},{8,0},{12,4},{16,24},{20,28},{24,16},{28,20},{1,9},{5... | collective-permute-start | bytes 688136 | tf_op jit(solution)/shard_map/ppermute | solution.py:391
  95.7 3.0 %attention_backward_first.1 = (bf16[512,512]{1,0:T(8,128)(2,1)S(1)}, bf16[2,512,256]{2,1,0:T(8,128)(2,1)S(1)}, f32[2,512,256]{2,1,0:T(8,128)S(1)}) custom-call(bf16[1024,512]{1,0:T(8,128)(2,1)S(1)} %copy-done.1, bf16[1024,256]{1,0:T(8,128)(2,1)S(1)} %copy-done.2, bf16[1024,256]{1,0:T(8,128)(2,1)S(1)} %copy-done.3, bf16[1024,512]{1,0:T(8,128)(2,1)S(1)} %bitcast.8, ...), custom_call_target="tpu_custom_call" | custom-call | tf_op jit(solution)/shard_map/attention_backward_first/pallas_call | solution.py:223
  100.2 2.6 %collective-permute-done.25.refs_1_ = bf16[1,128,512]{2,1,0:T(8,128)(2,1)S(1)} collective-permute-done((bf16[1,128,512]{2,1,0:T(8,128)(2,1)S(1)}, bf16[1,128,512]{2,1,0:T(8,128)(2,1)S(1)}, u32[]{:S(2)}, u32[]{:S(2)}) %collective-permute-start.25) | collective-permute-done | bytes 131104 | tf_op jit(solution)/shard_map/ppermute | solution.py:391
  104.0 2.9 %attention_backward_second.1 = (bf16[512,512]{1,0:T(8,128)(2,1)S(1)}, bf16[2,512,256]{2,1,0:T(8,128)(2,1)S(1)}, f32[2,512,256]{2,1,0:T(8,128)S(1)}) custom-call(bf16[1024,512]{1,0:T(8,128)(2,1)S(1)} %copy-done.1, bf16[1024,256]{1,0:T(8,128)(2,1)S(1)} %copy-done.2, bf16[1024,256]{1,0:T(8,128)(2,1)S(1)} %copy-done.3, bf16[1024,512]{1,0:T(8,128)(2,1)S(1)} %bitcast.9, ...), custom_call_target="tpu_custom_call" | custom-call | tf_op jit(solution)/shard_map/attention_backward_second/pallas_call | solution.py:223
  107.0 5.4 %collective-permute-start.31 = (bf16[2,64,512]{2,1,0:T(8,128)(2,1)S(1)}, bf16[2,64,512]{2,1,0:T(8,128)(2,1)S(1)}, u32[]{:S(2)}, u32[]{:S(2)}) collective-permute-start(bf16[2,64,512]{2,1,0:T(8,128)(2,1)S(1)} %get-tuple-element.207), channel_id=1, source_target_pairs={{0,8},{4,12},{8,0},{12,4},{16,24},{20,28},{24,16},{28,20},{1,9},{5... | collective-permute-start | bytes 393224 | tf_op jit(solution)/shard_map/ppermute | solution.py:391
  113.5 8.2 %collective-permute-done.28.refs_1_ = bf16[2,80,512]{2,1,0:T(8,128)(2,1)S(1)} collective-permute-done((bf16[2,80,512]{2,1,0:T(8,128)(2,1)S(1)}, bf16[2,80,512]{2,1,0:T(8,128)(2,1)S(1)}, u32[]{:S(2)}, u32[]{:S(2)}) %collective-permute-start.28) | collective-permute-done | bytes 163872 | tf_op jit(solution)/shard_map/ppermute | solution.py:391
  123.2 1.7 %collective-permute-start.32 = (bf16[1,64,512]{2,1,0:T(8,128)(2,1)S(1)}, bf16[1,64,512]{2,1,0:T(8,128)(2,1)S(1)}, u32[]{:S(2)}, u32[]{:S(2)}) collective-permute-start(bf16[1,64,512]{2,1,0:T(8,128)(2,1)S(1)} %get-tuple-element.214), channel_id=1, source_target_pairs={{0,16},{4,20},{8,24},{12,28},{16,0},{20,4},{24,8},{28,12},{1,17},{... | collective-permute-start | bytes 196616 | tf_op jit(solution)/shard_map/ppermute | solution.py:391
  125.0 3.1 %collective-permute-done.30.refs_1_ = bf16[1,80,512]{2,1,0:T(8,128)(2,1)S(1)} collective-permute-done((bf16[1,80,512]{2,1,0:T(8,128)(2,1)S(1)}, bf16[1,80,512]{2,1,0:T(8,128)(2,1)S(1)}, u32[]{:S(2)}, u32[]{:S(2)}) %collective-permute-start.30) | collective-permute-done | bytes 81952 | tf_op jit(solution)/shard_map/ppermute | solution.py:391
  (85 shorter events, 24.9 us)
Async XLA Ops:
  0.7 15.8 %collective-permute-start = (bf16[256,5376]{1,0:T(8,128)(2,1)}, bf16[256,5376]{1,0:T(8,128)(2,1)S(1)}, u32[]{:S(2)}, u32[]{:S(2)}) collective-permute-start(bf16[256,5376]{1,0:T(8,128)(2,1)} %og_ref.1), channel_id=1, source_target_pairs={{0,1},{1,0},{2,3},{3,2},{4,5},{5,4},{6,7},{7,6},{8,9},{9,8},{10,11... | collective-permute-start | bytes 8257544 | tf_op jit(solution)/shard_map/ppermute | solution.py:391
  5.5 21.7 %collective-permute-start.4 = (bf16[256,1152]{1,0:T(8,128)(2,1)S(1)}, bf16[256,1152]{1,0:T(8,128)(2,1)S(1)}, u32[]{:S(2)}, u32[]{:S(2)}) collective-permute-start(bf16[256,1152]{1,0:T(8,128)(2,1)S(1)} %get-tuple-element.120.refs_0_), channel_id=1, source_target_pairs={{0,2},{1,3},{2,0},{3,1},{4,6},{5,7},{6,4},{7,5},{8,10},{9,11},{10,... | collective-permute-start | bytes 1769480 | tf_op jit(solution)/shard_map/ppermute | solution.py:391
  8.2 14.8 %collective-permute-start.5 = (bf16[2,512,256]{2,1,0:T(8,128)(2,1)S(1)}, bf16[2,512,256]{2,1,0:T(8,128)(2,1)S(1)}, u32[]{:S(2)}, u32[]{:S(2)}) collective-permute-start(bf16[2,512,256]{2,1,0:T(8,128)(2,1)S(1)} %pack_halo.1), channel_id=1, source_target_pairs={{0,4},{4,8},{8,12},{12,16},{16,20},{20,24},{24,28},{1,5},{5,9},{9,... | collective-permute-start | bytes 1572872 | tf_op jit(solution)/shard_map/ppermute | solution.py:411
  11.7 23.3 %collective-permute-start.3 = (bf16[256,1152]{1,0:T(8,128)(2,1)S(1)}, bf16[256,1152]{1,0:T(8,128)(2,1)S(1)}, u32[]{:S(2)}, u32[]{:S(2)}) collective-permute-start(bf16[256,1152]{1,0:T(8,128)(2,1)S(1)} %get-tuple-element.122.refs_0_), channel_id=1, source_target_pairs={{0,2},{1,3},{2,0},{3,1},{4,6},{5,7},{6,4},{7,5},{8,10},{9,11},{10,... | collective-permute-start | bytes 1769480 | tf_op jit(solution)/shard_map/ppermute | solution.py:391
  27.3 7.7 %collective-permute-start.6 = (bf16[256,1152]{1,0:T(8,128)(2,1)S(1)}, bf16[256,1152]{1,0:T(8,128)(2,1)S(1)}, u32[]{:S(2)}, u32[]{:S(2)}) collective-permute-start(bf16[256,1152]{1,0:T(8,128)(2,1)S(1)} %collective-permute-done.4.refs_2_), channel_id=1, source_target_pairs={{0,1},{1,0},{2,3},{3,2},{4,5},{5,4},{6,7},{7,6},{8,9},{9,8},{10,11... | collective-permute-start | bytes 1769480 | tf_op jit(solution)/shard_map/ppermute | solution.py:391
  27.3 18.9 %collective-permute-start.8 = (bf16[256,1024]{1,0:T(8,128)(2,1)S(1)}, bf16[256,1024]{1,0:T(8,128)(2,1)S(1)}, u32[]{:S(2)}, u32[]{:S(2)}) collective-permute-start(bf16[256,1024]{1,0:T(8,128)(2,1)S(1)} %get-tuple-element.117.refs_0_), channel_id=1, source_target_pairs={{0,2},{1,3},{2,0},{3,1},{4,6},{5,7},{6,4},{7,5},{8,10},{9,11},{10,... | collective-permute-start | bytes 1572872 | tf_op jit(solution)/shard_map/ppermute | solution.py:391
  35.0 11.2 %collective-permute-start.9 = (bf16[256,1152]{1,0:T(8,128)(2,1)S(1)}, bf16[256,1152]{1,0:T(8,128)(2,1)S(1)}, u32[]{:S(2)}, u32[]{:S(2)}) collective-permute-start(bf16[256,1152]{1,0:T(8,128)(2,1)S(1)} %collective-permute-done.3.refs_2_), channel_id=1, source_target_pairs={{0,1},{1,0},{2,3},{3,2},{4,5},{5,4},{6,7},{7,6},{8,9},{9,8},{10,11... | collective-permute-start | bytes 1769480 | tf_op jit(solution)/shard_map/ppermute | solution.py:391
  38.2 16.3 %collective-permute-start.7 = (bf16[4,144,512]{2,1,0:T(8,128)(2,1)S(1)}, bf16[4,144,512]{2,1,0:T(8,128)(2,1)S(1)}, u32[]{:S(2)}, u32[]{:S(2)}) collective-permute-start(bf16[4,144,512]{2,1,0:T(8,128)(2,1)S(1)} %get-tuple-element.131), channel_id=1, source_target_pairs={{0,4},{4,0},{8,12},{12,8},{16,20},{20,16},{24,28},{28,24},{1,5},{5... | collective-permute-start | bytes 1769480 | tf_op jit(solution)/shard_map/ppermute | solution.py:391
  40.3 15.5 %collective-permute-start.2 = (bf16[256,896]{1,0:T(8,128)(2,1)S(1)}, bf16[256,896]{1,0:T(8,128)(2,1)S(1)}, u32[]{:S(2)}, u32[]{:S(2)}) collective-permute-start(bf16[256,896]{1,0:T(8,128)(2,1)S(1)} %get-tuple-element.119.refs_0_), channel_id=1, source_target_pairs={{0,2},{1,3},{2,0},{3,1},{4,6},{5,7},{6,4},{7,5},{8,10},{9,11},{10,... | collective-permute-start | bytes 1376264 | tf_op jit(solution)/shard_map/ppermute | solution.py:391
  46.2 12.8 %collective-permute-start.10 = (bf16[256,1024]{1,0:T(8,128)(2,1)S(1)}, bf16[256,1024]{1,0:T(8,128)(2,1)S(1)}, u32[]{:S(2)}, u32[]{:S(2)}) collective-permute-start(bf16[256,1024]{1,0:T(8,128)(2,1)S(1)} %collective-permute-done.8.refs_2_), channel_id=1, source_target_pairs={{0,1},{1,0},{2,3},{3,2},{4,5},{5,4},{6,7},{7,6},{8,9},{9,8},{10,11... | collective-permute-start | bytes 1572872 | tf_op jit(solution)/shard_map/ppermute | solution.py:391
  49.5 18.6 %collective-permute-start.12 = (bf16[4,144,512]{2,1,0:T(8,128)(2,1)S(1)}, bf16[4,144,512]{2,1,0:T(8,128)(2,1)S(1)}, u32[]{:S(2)}, u32[]{:S(2)}) collective-permute-start(bf16[4,144,512]{2,1,0:T(8,128)(2,1)S(1)} %get-tuple-element.146), channel_id=1, source_target_pairs={{0,4},{4,0},{8,12},{12,8},{16,20},{20,16},{24,28},{28,24},{1,5},{5... | collective-permute-start | bytes 1769480 | tf_op jit(solution)/shard_map/ppermute | solution.py:391
  55.7 19.4 %collective-permute-start.17 = (bf16[256,896]{1,0:T(8,128)(2,1)S(1)}, bf16[256,896]{1,0:T(8,128)(2,1)S(1)}, u32[]{:S(2)}, u32[]{:S(2)}) collective-permute-start(bf16[256,896]{1,0:T(8,128)(2,1)S(1)} %collective-permute-done.2.refs_2_), channel_id=1, source_target_pairs={{0,1},{1,0},{2,3},{3,2},{4,5},{5,4},{6,7},{7,6},{8,9},{9,8},{10,11... | collective-permute-start | bytes 1376264 | tf_op jit(solution)/shard_map/ppermute | solution.py:391
  55.7 9.5 %collective-permute-start.13 = (bf16[2,144,512]{2,1,0:T(8,128)(2,1)S(1)}, bf16[2,144,512]{2,1,0:T(8,128)(2,1)S(1)}, u32[]{:S(2)}, u32[]{:S(2)}) collective-permute-start(bf16[2,144,512]{2,1,0:T(8,128)(2,1)S(1)} %get-tuple-element.139), channel_id=1, source_target_pairs={{0,8},{4,12},{8,0},{12,4},{16,24},{20,28},{24,16},{28,20},{1,9},{5... | collective-permute-start | bytes 884744 | tf_op jit(solution)/shard_map/ppermute | solution.py:391
  57.5 12.3 %collective-permute-start.16 = (bf16[256,640]{1,0:T(8,128)(2,1)S(1)}, bf16[256,640]{1,0:T(8,128)(2,1)S(1)}, u32[]{:S(2)}, u32[]{:S(2)}) collective-permute-start(bf16[256,640]{1,0:T(8,128)(2,1)S(1)} %get-tuple-element.115.refs_0_), channel_id=1, source_target_pairs={{0,2},{1,3},{2,0},{3,1},{4,6},{5,7},{6,4},{7,5},{8,10},{9,11},{10,... | collective-permute-start | bytes 983048 | tf_op jit(solution)/shard_map/ppermute | solution.py:391
  62.1 17.4 %collective-permute-start.11 = (bf16[4,128,512]{2,1,0:T(8,128)(2,1)S(1)}, bf16[4,128,512]{2,1,0:T(8,128)(2,1)S(1)}, u32[]{:S(2)}, u32[]{:S(2)}) collective-permute-start(bf16[4,128,512]{2,1,0:T(8,128)(2,1)S(1)} %get-tuple-element.144), channel_id=1, source_target_pairs={{0,4},{4,0},{8,12},{12,8},{16,20},{20,16},{24,28},{28,24},{1,5},{5... | collective-permute-start | bytes 1572872 | tf_op jit(solution)/shard_map/ppermute | solution.py:391
  65.3 9.8 %collective-permute-start.15 = (bf16[1,144,512]{2,1,0:T(8,128)(2,1)S(1)}, bf16[1,144,512]{2,1,0:T(8,128)(2,1)S(1)}, u32[]{:S(2)}, u32[]{:S(2)}) collective-permute-start(bf16[1,144,512]{2,1,0:T(8,128)(2,1)S(1)} %get-tuple-element.150), channel_id=1, source_target_pairs={{0,16},{4,20},{8,24},{12,28},{16,0},{20,4},{24,8},{28,12},{1,17},{... | collective-permute-start | bytes 442376 | tf_op jit(solution)/shard_map/ppermute | solution.py:391
  68.2 11.2 %collective-permute-start.14 = (bf16[2,144,512]{2,1,0:T(8,128)(2,1)S(1)}, bf16[2,144,512]{2,1,0:T(8,128)(2,1)S(1)}, u32[]{:S(2)}, u32[]{:S(2)}) collective-permute-start(bf16[2,144,512]{2,1,0:T(8,128)(2,1)S(1)} %get-tuple-element.153), channel_id=1, source_target_pairs={{0,8},{4,12},{8,0},{12,4},{16,24},{20,28},{24,16},{28,20},{1,9},{5... | collective-permute-start | bytes 884744 | tf_op jit(solution)/shard_map/ppermute | solution.py:391
  69.9 9.7 %collective-permute-start.1 = (bf16[256,512]{1,0:T(8,128)(2,1)S(1)}, bf16[256,512]{1,0:T(8,128)(2,1)S(1)}, u32[]{:S(2)}, u32[]{:S(2)}) collective-permute-start(bf16[256,512]{1,0:T(8,128)(2,1)S(1)} %get-tuple-element.111.refs_0_), channel_id=1, source_target_pairs={{0,2},{1,3},{2,0},{3,1},{4,6},{5,7},{6,4},{7,5},{8,10},{9,11},{10,... | collective-permute-start | bytes 786440 | tf_op jit(solution)/shard_map/ppermute | solution.py:391
  77.8 12.4 %collective-permute-start.21 = (bf16[4,112,512]{2,1,0:T(8,128)(2,1)S(1)}, bf16[4,112,512]{2,1,0:T(8,128)(2,1)S(1)}, u32[]{:S(2)}, u32[]{:S(2)}) collective-permute-start(bf16[4,112,512]{2,1,0:T(8,128)(2,1)S(1)} %get-tuple-element.174), channel_id=1, source_target_pairs={{0,4},{4,0},{8,12},{12,8},{16,20},{20,16},{24,28},{28,24},{1,5},{5... | collective-permute-start | bytes 1376264 | tf_op jit(solution)/shard_map/ppermute | solution.py:391
  79.6 7.6 %collective-permute-start.19 = (bf16[256,512]{1,0:T(8,128)(2,1)S(1)}, bf16[256,512]{1,0:T(8,128)(2,1)S(1)}, u32[]{:S(2)}, u32[]{:S(2)}) collective-permute-start(bf16[256,512]{1,0:T(8,128)(2,1)S(1)} %collective-permute-done.1.refs_2_), channel_id=1, source_target_pairs={{0,1},{1,0},{2,3},{3,2},{4,5},{5,4},{6,7},{7,6},{8,9},{9,8},{10,11... | collective-permute-start | bytes 786440 | tf_op jit(solution)/shard_map/ppermute | solution.py:391
  80.2 14.0 %collective-permute-start.20 = (bf16[2,128,512]{2,1,0:T(8,128)(2,1)S(1)}, bf16[2,128,512]{2,1,0:T(8,128)(2,1)S(1)}, u32[]{:S(2)}, u32[]{:S(2)}) collective-permute-start(bf16[2,128,512]{2,1,0:T(8,128)(2,1)S(1)} %get-tuple-element.164), channel_id=1, source_target_pairs={{0,8},{4,12},{8,0},{12,4},{16,24},{20,28},{24,16},{28,20},{1,9},{5... | collective-permute-start | bytes 786440 | tf_op jit(solution)/shard_map/ppermute | solution.py:391
  80.8 9.3 %collective-permute-start.22 = (bf16[1,144,512]{2,1,0:T(8,128)(2,1)S(1)}, bf16[1,144,512]{2,1,0:T(8,128)(2,1)S(1)}, u32[]{:S(2)}, u32[]{:S(2)}) collective-permute-start(bf16[1,144,512]{2,1,0:T(8,128)(2,1)S(1)} %get-tuple-element.162), channel_id=1, source_target_pairs={{0,16},{4,20},{8,24},{12,28},{16,0},{20,4},{24,8},{28,12},{1,17},{... | collective-permute-start | bytes 442376 | tf_op jit(solution)/shard_map/ppermute | solution.py:391
  86.3 16.5 %collective-permute-start.23 = (bf16[4,80,512]{2,1,0:T(8,128)(2,1)S(1)}, bf16[4,80,512]{2,1,0:T(8,128)(2,1)S(1)}, u32[]{:S(2)}, u32[]{:S(2)}) collective-permute-start(bf16[4,80,512]{2,1,0:T(8,128)(2,1)S(1)} %get-tuple-element.185), channel_id=1, source_target_pairs={{0,4},{4,0},{8,12},{12,8},{16,20},{20,16},{24,28},{28,24},{1,5},{5... | collective-permute-start | bytes 983048 | tf_op jit(solution)/shard_map/ppermute | solution.py:391
  88.8 18.1 %collective-permute-start.29 = (bf16[4,64,512]{2,1,0:T(8,128)(2,1)S(1)}, bf16[4,64,512]{2,1,0:T(8,128)(2,1)S(1)}, u32[]{:S(2)}, u32[]{:S(2)}) collective-permute-start(bf16[4,64,512]{2,1,0:T(8,128)(2,1)S(1)} %get-tuple-element.205), channel_id=1, source_target_pairs={{0,4},{4,0},{8,12},{12,8},{16,20},{20,16},{24,28},{28,24},{1,5},{5... | collective-permute-start | bytes 786440 | tf_op jit(solution)/shard_map/ppermute | solution.py:391
  90.3 12.5 %collective-permute-start.24 = (bf16[2,112,512]{2,1,0:T(8,128)(2,1)S(1)}, bf16[2,112,512]{2,1,0:T(8,128)(2,1)S(1)}, u32[]{:S(2)}, u32[]{:S(2)}) collective-permute-start(bf16[2,112,512]{2,1,0:T(8,128)(2,1)S(1)} %get-tuple-element.178), channel_id=1, source_target_pairs={{0,8},{4,12},{8,0},{12,4},{16,24},{20,28},{24,16},{28,20},{1,9},{5... | collective-permute-start | bytes 688136 | tf_op jit(solution)/shard_map/ppermute | solution.py:391
  94.2 8.6 %collective-permute-start.25 = (bf16[1,128,512]{2,1,0:T(8,128)(2,1)S(1)}, bf16[1,128,512]{2,1,0:T(8,128)(2,1)S(1)}, u32[]{:S(2)}, u32[]{:S(2)}) collective-permute-start(bf16[1,128,512]{2,1,0:T(8,128)(2,1)S(1)} %get-tuple-element.180), channel_id=1, source_target_pairs={{0,16},{4,20},{8,24},{12,28},{16,0},{20,4},{24,8},{28,12},{1,17},{... | collective-permute-start | bytes 393224 | tf_op jit(solution)/shard_map/ppermute | solution.py:391
  98.6 30.2 %collective-permute-start.26 = (bf16[2,512,256]{2,1,0:T(8,128)(2,1)S(1)}, bf16[2,512,256]{2,1,0:T(8,128)(2,1)S(1)}, u32[]{:S(2)}, u32[]{:S(2)}) collective-permute-start(bf16[2,512,256]{2,1,0:T(8,128)(2,1)S(1)} %get-tuple-element.199), channel_id=1, source_target_pairs={{4,0},{8,4},{12,8},{16,12},{20,16},{24,20},{28,24},{5,1},{9,5},{13... | collective-permute-start | bytes 1572872 | tf_op jit(solution)/shard_map/ppermute | solution.py:444
  102.9 18.8 %collective-permute-start.28 = (bf16[2,80,512]{2,1,0:T(8,128)(2,1)S(1)}, bf16[2,80,512]{2,1,0:T(8,128)(2,1)S(1)}, u32[]{:S(2)}, u32[]{:S(2)}) collective-permute-start(bf16[2,80,512]{2,1,0:T(8,128)(2,1)S(1)} %get-tuple-element.193), channel_id=1, source_target_pairs={{0,8},{4,12},{8,0},{12,4},{16,24},{20,28},{24,16},{28,20},{1,9},{5... | collective-permute-start | bytes 491528 | tf_op jit(solution)/shard_map/ppermute | solution.py:391
  107.0 16.2 %collective-permute-start.31 = (bf16[2,64,512]{2,1,0:T(8,128)(2,1)S(1)}, bf16[2,64,512]{2,1,0:T(8,128)(2,1)S(1)}, u32[]{:S(2)}, u32[]{:S(2)}) collective-permute-start(bf16[2,64,512]{2,1,0:T(8,128)(2,1)S(1)} %get-tuple-element.207), channel_id=1, source_target_pairs={{0,8},{4,12},{8,0},{12,4},{16,24},{20,28},{24,16},{28,20},{1,9},{5... | collective-permute-start | bytes 393224 | tf_op jit(solution)/shard_map/ppermute | solution.py:391
  112.4 9.5 %collective-permute-start.27 = (bf16[1,112,512]{2,1,0:T(8,128)(2,1)S(1)}, bf16[1,112,512]{2,1,0:T(8,128)(2,1)S(1)}, u32[]{:S(2)}, u32[]{:S(2)}) collective-permute-start(bf16[1,112,512]{2,1,0:T(8,128)(2,1)S(1)} %get-tuple-element.191), channel_id=1, source_target_pairs={{0,16},{4,20},{8,24},{12,28},{16,0},{20,4},{24,8},{28,12},{1,17},{... | collective-permute-start | bytes 344072 | tf_op jit(solution)/shard_map/ppermute | solution.py:391
  121.8 6.2 %collective-permute-start.30 = (bf16[1,80,512]{2,1,0:T(8,128)(2,1)S(1)}, bf16[1,80,512]{2,1,0:T(8,128)(2,1)S(1)}, u32[]{:S(2)}, u32[]{:S(2)}) collective-permute-start(bf16[1,80,512]{2,1,0:T(8,128)(2,1)S(1)} %get-tuple-element.209), channel_id=1, source_target_pairs={{0,16},{4,20},{8,24},{12,28},{16,0},{20,4},{24,8},{28,12},{1,17},{... | collective-permute-start | bytes 245768 | tf_op jit(solution)/shard_map/ppermute | solution.py:391
  123.2 5.5 %collective-permute-start.32 = (bf16[1,64,512]{2,1,0:T(8,128)(2,1)S(1)}, bf16[1,64,512]{2,1,0:T(8,128)(2,1)S(1)}, u32[]{:S(2)}, u32[]{:S(2)}) collective-permute-start(bf16[1,64,512]{2,1,0:T(8,128)(2,1)S(1)} %get-tuple-element.214), channel_id=1, source_target_pairs={{0,16},{4,20},{8,24},{12,28},{16,0},{20,4},{24,8},{28,12},{1,17},{... | collective-permute-start | bytes 196616 | tf_op jit(solution)/shard_map/ppermute | solution.py:391
  (7 other events, 57.3 us)
